TPU v7x, 32 devices: a whole 2x2x4 slice. The times are simulated.
32 devices in a mesh: dp: 8 (over z, x), row: 2 (over y), col: 2 (over core).
Axes of the slice: x: 2, y: 2, z: 4, core: 2. Of those that a mesh axis runs over, the one named last changes fastest.
Arguments:
- images: bfloat16 [10960, 1024], P(('dp', 'row'), 'col'), may hold values from -19 to 19
- cotangent: bfloat16 [10960, 1024], P(('dp', 'row'), 'col'), may hold values from -6 to 6
- triplet_master: float32 [2, 1024, 3, 1024], P(None, ('col', 'dp'), None, 'row'), may hold values from -0.1875 to 0.1875
- triplet_first: float32 [2, 1024, 3, 1024], P(None, ('col', 'dp'), None, 'row'), may hold values from -28 to 28
- triplet_second: float32 [2, 1024, 3, 1024], P(None, ('col', 'dp'), None, 'row'), may hold values from 1.7536 to 7.0144
- project_master: float32 [2, 1024, 1024], P(None, ('row', 'dp'), 'col'), may hold values from -0.375 to 0.375
- project_first: float32 [2, 1024, 1024], P(None, ('row', 'dp'), 'col'), may hold values from -28 to 28
- project_second: float32 [2, 1024, 1024], P(None, ('row', 'dp'), 'col'), may hold values from 1.7536 to 7.0144
- expand_master: float32 [2, 1024, 4096], P(None, ('col', 'dp'), 'row'), may hold values from -0.1875 to 0.1875
- expand_first: float32 [2, 1024, 4096], P(None, ('col', 'dp'), 'row'), may hold values from -28 to 28
- expand_second: float32 [2, 1024, 4096], P(None, ('col', 'dp'), 'row'), may hold values from 1.7536 to 7.0144
- shrink_master: float32 [2, 4096, 1024], P(None, ('row', 'dp'), 'col'), may hold values from -0.09375 to 0.09375
- shrink_first: float32 [2, 4096, 1024], P(None, ('row', 'dp'), 'col'), may hold values from -28 to 28
- shrink_second: float32 [2, 4096, 1024], P(None, ('row', 'dp'), 'col'), may hold values from 1.7536 to 7.0144
- vectors_master: float32 [2, 14336], P(None, ('dp', 'row', 'col')), may hold values from -0.6 to 1.5
- vectors_first: float32 [2, 14336], P(None, ('dp', 'row', 'col')), may hold values from -32 to 32
- vectors_second: float32 [2, 14336], P(None, ('dp', 'row', 'col')), may hold values from 2.74 to 10.96
Outputs:
- block_out: bfloat16 [10960, 1024], P(('dp', 'row'), 'col')
- input_grad: float32 [10960, 1024], P(('dp', 'row'), 'col')
- new_triplet_first: float32 [2, 1024, 3, 1024], P(None, ('col', 'dp'), None, 'row')
- new_triplet_second: float32 [2, 1024, 3, 1024], P(None, ('col', 'dp'), None, 'row')
- new_triplet_master: float32 [2, 1024, 3, 1024], P(None, ('col', 'dp'), None, 'row')
- new_project_first: float32 [2, 1024, 1024], P(None, ('row', 'dp'), 'col')
- new_project_second: float32 [2, 1024, 1024], P(None, ('row', 'dp'), 'col')
- new_project_master: float32 [2, 1024, 1024], P(None, ('row', 'dp'), 'col')
- new_expand_first: float32 [2, 1024, 4096], P(None, ('col', 'dp'), 'row')
- new_expand_second: float32 [2, 1024, 4096], P(None, ('col', 'dp'), 'row')
- new_expand_master: float32 [2, 1024, 4096], P(None, ('col', 'dp'), 'row')
- new_shrink_first: float32 [2, 4096, 1024], P(None, ('row', 'dp'), 'col')
- new_shrink_second: float32 [2, 4096, 1024], P(None, ('row', 'dp'), 'col')
- new_shrink_master: float32 [2, 4096, 1024], P(None, ('row', 'dp'), 'col')
- new_vectors_first: float32 [2, 14336], P(None, ('dp', 'row', 'col'))
- new_vectors_second: float32 [2, 14336], P(None, ('dp', 'row', 'col'))
- new_vectors_master: float32 [2, 14336], P(None, ('dp', 'row', 'col'))
All inputs are finite; a program needn't handle non-finite values.
Results may differ from a plain program's by a relative error of at most 0.012.
Values may be sent and summed in bfloat16 or wider, within the bound.
A program may use at most 256 MiB of HBM per device.

v0:
```python
import jax
import jax.numpy as jnp
from jax import lax
from jax.sharding import PartitionSpec as P

D = 1024
HEAD_DIM = 64
FF = 4096
LAYERS = 2
STEP = 10
IMAGES = 1
SEQ = 1370


norm_epsilon = 1e-06
beta_first = 0.9
beta_second = 0.999
adam_epsilon = 1e-08
learn_rate = 0.02
vector_rate = 0.1
decay_rate = 0.05


def contract(left, right, left_dims, right_dims):
    return lax.dot_general(
        left, right, ((left_dims, right_dims), ((), ())), preferred_element_type=jnp.float32
    )


def feature_sums(first, second):
    return lax.psum((first, second), "col")


def row_rows(values):
    return lax.all_gather(values, "row", axis=0, tiled=True)


def col_rows(values):
    return lax.all_gather(values, "col", axis=0, tiled=True)


def head_rows(values):
    return lax.all_gather(values, "col", axis=2, tiled=True)


def head_sum(values):
    return lax.psum_scatter(values, "col", scatter_dimension=2, tiled=True)


def row_sum(left, right, left_dims, right_dims):
    return lax.psum_scatter(
        contract(left, right, left_dims, right_dims), "row", scatter_dimension=0, tiled=True
    )


def col_sum(left, right, left_dims, right_dims):
    return lax.psum_scatter(
        contract(left, right, left_dims, right_dims), "col", scatter_dimension=0, tiled=True
    )


def gelu_value(values):
    return jax.nn.gelu(values, approximate=False)


def norm_forward(values, gain, shift):
    total, square = feature_sums(jnp.sum(values, 1), jnp.sum(values * values, 1))
    centre = total / D
    spread = square / D - centre * centre
    inverse = lax.rsqrt(spread + norm_epsilon)[:, None]
    unit = (values - centre[:, None]) * inverse
    return ((unit * gain + shift).astype(jnp.bfloat16), unit, inverse)


def norm_backward(grad, unit, inverse, gain):
    scaled = grad * gain
    first, second = feature_sums(jnp.sum(scaled, 1), jnp.sum(scaled * unit, 1))
    return inverse * (scaled - first[:, None] / D - unit * (second[:, None] / D))


def attend_forward(triple):
    seq_len = triple.shape[0] // IMAGES
    heads = triple.shape[2] // HEAD_DIM
    stacked = (
        triple.reshape(IMAGES, seq_len, 3, heads, HEAD_DIM)
        .transpose(0, 3, 2, 1, 4)
        .reshape(IMAGES * heads, 3, seq_len, HEAD_DIM)
    )
    factor = HEAD_DIM ** (-0.5)

    def one_head(block):
        scores = contract(block[0], block[1], (1,), (1,)) * factor
        peak = jnp.max(scores, 1, keepdims=True)
        weights = jnp.exp(scores - peak)
        total = jnp.sum(weights, 1, keepdims=True)
        probs = (weights / total).astype(jnp.bfloat16)
        return (
            jnp.dot(probs, block[2], preferred_element_type=jnp.float32),
            (peak + jnp.log(total))[:, 0],
        )

    results, logsum = lax.map(one_head, stacked)
    mixed = (
        results.reshape(IMAGES, heads, seq_len, HEAD_DIM)
        .transpose(0, 2, 1, 3)
        .reshape(IMAGES * seq_len, heads * HEAD_DIM)
    )
    return (mixed.astype(jnp.bfloat16), stacked, logsum)


def attend_backward(stacked, logsum, grad_mixed):
    count = stacked.shape[0]
    seq_len = stacked.shape[2]
    heads = count // IMAGES
    factor = HEAD_DIM ** (-0.5)
    grads = (
        grad_mixed.reshape(IMAGES, seq_len, heads, HEAD_DIM)
        .transpose(0, 2, 1, 3)
        .reshape(count, seq_len, HEAD_DIM)
    )

    def one_head(pack):
        block, norm_log, back = pack
        scores = contract(block[0], block[1], (1,), (1,)) * factor
        probs = jnp.exp(scores - norm_log[:, None])
        back_probs = contract(back, block[2], (1,), (1,))
        inner = jnp.sum(probs * back_probs, 1, keepdims=True)
        back_scores = (probs * (back_probs - inner)).astype(jnp.bfloat16)
        grad_query = jnp.dot(back_scores, block[1], preferred_element_type=jnp.float32) * factor
        grad_key = contract(back_scores, block[0], (0,), (0,)) * factor
        grad_value = contract(probs.astype(jnp.bfloat16), back, (0,), (0,))
        return jnp.stack([grad_query, grad_key, grad_value])

    result = lax.map(one_head, (stacked, logsum, grads))
    return (
        result.reshape(IMAGES, heads, 3, seq_len, HEAD_DIM)
        .transpose(0, 3, 2, 1, 4)
        .reshape(IMAGES * seq_len, 3, heads * HEAD_DIM)
    )


def adam_step(master, first, second, grad, rate, decay):
    first_new = beta_first * first + (1.0 - beta_first) * grad
    second_new = beta_second * second + (1.0 - beta_second) * grad * grad
    ratio = (
        first_new
        / (1.0 - beta_first**STEP)
        / (jnp.sqrt(second_new / (1.0 - beta_second**STEP)) + adam_epsilon)
    )
    return (first_new, second_new, master - rate * (ratio + decay * master))


def local(
    images,
    cotangent,
    triplet_master,
    triplet_first,
    triplet_second,
    project_master,
    project_first,
    project_second,
    expand_master,
    expand_first,
    expand_second,
    shrink_master,
    shrink_first,
    shrink_second,
    vectors_master,
    vectors_first,
    vectors_second,
):
    features = images.shape[1]
    col_count = lax.axis_size("col")
    row_at = lax.axis_index("row")
    col_at = lax.axis_index("col")
    triplet_w, project_w, expand_w, shrink_w = (
        lax.all_gather(triplet_master.astype(jnp.bfloat16), "dp", axis=1, tiled=True),
        lax.all_gather(project_master.astype(jnp.bfloat16), "dp", axis=1, tiled=True),
        lax.all_gather(expand_master.astype(jnp.bfloat16), "dp", axis=1, tiled=True),
        lax.all_gather(shrink_master.astype(jnp.bfloat16), "dp", axis=1, tiled=True),
    )
    vectors = lax.all_gather(vectors_master, ("dp", "row", "col"), axis=1, tiled=True)
    group_tokens = IMAGES * SEQ
    head_width = triplet_w.shape[3] // col_count
    hidden_width = expand_w.shape[2]
    head_start = (row_at * col_count + col_at) * head_width
    feature_start = col_at * features
    marks = [
        0,
        D,
        2 * D,
        3 * D,
        4 * D,
        5 * D,
        6 * D,
        7 * D,
        8 * D,
        8 * D + FF,
        9 * D + FF,
        10 * D + FF,
    ]
    starts = [
        feature_start,
        feature_start,
        head_start,
        head_start,
        feature_start,
        feature_start,
        feature_start,
        feature_start,
        row_at * hidden_width,
        feature_start,
        feature_start,
    ]
    widths = [
        features,
        features,
        head_width,
        head_width,
        features,
        features,
        features,
        features,
        hidden_width,
        features,
        features,
    ]

    def pieces(vector):
        return [
            lax.dynamic_slice_in_dim(
                vector[marks[place] : marks[place + 1]], starts[place], widths[place]
            )
            for place in range(11)
        ]

    def spread_out(parts):
        return jnp.concatenate(
            [
                lax.dynamic_update_slice_in_dim(
                    jnp.zeros((marks[place + 1] - marks[place],), jnp.float32),
                    parts[place],
                    starts[place],
                    0,
                )
                for place in range(11)
            ]
        )

    state = images.astype(jnp.float32)
    kept = []
    layer_pieces = []
    for layer in range(LAYERS):
        parts = pieces(vectors[layer])
        layer_pieces.append(parts)
        (
            norm_gain,
            norm_shift,
            query_bias,
            value_bias,
            mixer_bias,
            branch_scale,
            second_gain,
            second_shift,
            hidden_bias,
            output_bias,
            output_scale,
        ) = parts
        normed, unit_one, inverse_one = norm_forward(state, norm_gain, norm_shift)
        normed_all = row_rows(normed)
        partial_value = contract(normed_all, triplet_w[layer], (1,), (0,))
        summed = head_sum(partial_value.reshape(group_tokens, 3, col_count, head_width))[:, :, 0, :]
        biases = jnp.stack([query_bias, jnp.zeros_like(query_bias), value_bias])
        triple = (summed + biases).astype(jnp.bfloat16)
        mixed, stacked, logsum = attend_forward(triple)
        mixed_all = head_rows(mixed.reshape(group_tokens, 1, 1, head_width)).reshape(
            group_tokens, col_count * head_width
        )
        branch = row_sum(mixed_all, project_w[layer], (1,), (0,)) + mixer_bias
        middle = state + branch_scale * branch
        normed_two, unit_two, inverse_two = norm_forward(middle, second_gain, second_shift)
        normed_two_all = row_rows(normed_two)
        inner = col_sum(normed_two_all, expand_w[layer], (1,), (0,)) + hidden_bias
        active_all = col_rows(gelu_value(inner).astype(jnp.bfloat16))
        output = row_sum(active_all, shrink_w[layer], (1,), (0,)) + output_bias
        kept.append(
            (
                unit_one,
                inverse_one,
                normed_all,
                stacked,
                logsum,
                mixed_all,
                branch,
                unit_two,
                inverse_two,
                normed_two_all,
                inner,
                active_all,
                output,
            )
        )
        state = middle + output_scale * output
    block_out = state.astype(jnp.bfloat16)
    grad = cotangent.astype(jnp.float32)
    triplet_grads, project_grads, expand_grads, shrink_grads, vector_grads = ([], [], [], [], [])
    for layer in reversed(range(LAYERS)):
        (
            unit_one,
            inverse_one,
            normed_all,
            stacked,
            logsum,
            mixed_all,
            branch,
            unit_two,
            inverse_two,
            normed_two_all,
            inner,
            active_all,
            output,
        ) = kept[layer]
        (
            norm_gain,
            norm_shift,
            query_bias,
            value_bias,
            mixer_bias,
            branch_scale,
            second_gain,
            second_shift,
            hidden_bias,
            output_bias,
            output_scale,
        ) = layer_pieces[layer]
        output_scale_grad = jnp.sum(grad * output, 0)
        back_out = (output_scale * grad).astype(jnp.bfloat16)
        output_bias_grad = jnp.sum(back_out.astype(jnp.float32), 0)
        back_out_all = row_rows(back_out)
        shrink_grads.append(contract(active_all, back_out_all, (0,), (0,)))
        back_active = col_sum(back_out_all, shrink_w[layer], (1,), (1,))
        pullback = jax.vjp(gelu_value, inner)[1]
        back_inner = pullback(back_active)[0].astype(jnp.bfloat16)
        hidden_bias_grad = jnp.sum(back_inner.astype(jnp.float32), 0)
        back_inner_all = col_rows(back_inner)
        expand_grads.append(contract(normed_two_all, back_inner_all, (0,), (0,)))
        back_two = row_sum(back_inner_all, expand_w[layer], (1,), (1,))
        second_gain_grad = jnp.sum(back_two * unit_two, 0)
        second_shift_grad = jnp.sum(back_two, 0)
        grad_middle = grad + norm_backward(back_two, unit_two, inverse_two, second_gain)
        branch_scale_grad = jnp.sum(grad_middle * branch, 0)
        back_branch = (branch_scale * grad_middle).astype(jnp.bfloat16)
        mixer_bias_grad = jnp.sum(back_branch.astype(jnp.float32), 0)
        back_branch_all = row_rows(back_branch)
        project_grads.append(contract(mixed_all, back_branch_all, (0,), (0,)))
        back_partial = contract(back_branch_all, project_w[layer], (1,), (1,))
        back_mixed = head_sum(back_partial.reshape(group_tokens, 1, col_count, head_width))[
            :, 0, 0, :
        ].astype(jnp.bfloat16)
        back_triple = attend_backward(stacked, logsum, back_mixed).astype(jnp.bfloat16)
        triple_sums = jnp.sum(back_triple.astype(jnp.float32), 0)
        back_triple_all = head_rows(back_triple.reshape(group_tokens, 3, 1, head_width)).reshape(
            group_tokens, 3, col_count * head_width
        )
        triplet_grads.append(contract(normed_all, back_triple_all, (0,), (0,)))
        back_one = row_sum(back_triple_all, triplet_w[layer], (1, 2), (1, 2))
        norm_gain_grad = jnp.sum(back_one * unit_one, 0)
        norm_shift_grad = jnp.sum(back_one, 0)
        grad = grad_middle + norm_backward(back_one, unit_one, inverse_one, norm_gain)
        vector_grads.append(
            spread_out(
                [
                    norm_gain_grad,
                    norm_shift_grad,
                    triple_sums[0],
                    triple_sums[2],
                    mixer_bias_grad,
                    branch_scale_grad,
                    second_gain_grad,
                    second_shift_grad,
                    hidden_bias_grad,
                    output_bias_grad,
                    output_scale_grad,
                ]
            )
        )
    grads = (
        jnp.stack(triplet_grads[::-1]),
        jnp.stack(project_grads[::-1]),
        jnp.stack(expand_grads[::-1]),
        jnp.stack(shrink_grads[::-1]),
    )
    reduced = (
        lax.psum_scatter(grads[0], "dp", scatter_dimension=1, tiled=True),
        lax.psum_scatter(grads[1], "dp", scatter_dimension=1, tiled=True),
        lax.psum_scatter(grads[2], "dp", scatter_dimension=1, tiled=True),
        lax.psum_scatter(grads[3], "dp", scatter_dimension=1, tiled=True),
    )
    vector_reduced = lax.psum_scatter(
        jnp.stack(vector_grads[::-1]), ("dp", "row", "col"), scatter_dimension=1, tiled=True
    )
    triplet_out = adam_step(
        triplet_master, triplet_first, triplet_second, reduced[0], learn_rate, decay_rate
    )
    project_out = adam_step(
        project_master, project_first, project_second, reduced[1], learn_rate, decay_rate
    )
    expand_out = adam_step(
        expand_master, expand_first, expand_second, reduced[2], learn_rate, decay_rate
    )
    shrink_out = adam_step(
        shrink_master, shrink_first, shrink_second, reduced[3], learn_rate, decay_rate
    )
    vector_out = adam_step(
        vectors_master, vectors_first, vectors_second, vector_reduced, vector_rate, 0.0
    )
    return (
        block_out,
        grad,
        triplet_out[0],
        triplet_out[1],
        triplet_out[2],
        project_out[0],
        project_out[1],
        project_out[2],
        expand_out[0],
        expand_out[1],
        expand_out[2],
        shrink_out[0],
        shrink_out[1],
        shrink_out[2],
        vector_out[0],
        vector_out[1],
        vector_out[2],
    )


def solution(mesh):
    return jax.shard_map(
        local,
        mesh=mesh,
        in_specs=(
            P(("dp", "row"), "col"),
            P(("dp", "row"), "col"),
            P(None, ("col", "dp"), None, "row"),
            P(None, ("col", "dp"), None, "row"),
            P(None, ("col", "dp"), None, "row"),
            P(None, ("row", "dp"), "col"),
            P(None, ("row", "dp"), "col"),
            P(None, ("row", "dp"), "col"),
            P(None, ("col", "dp"), "row"),
            P(None, ("col", "dp"), "row"),
            P(None, ("col", "dp"), "row"),
            P(None, ("row", "dp"), "col"),
            P(None, ("row", "dp"), "col"),
            P(None, ("row", "dp"), "col"),
            P(None, ("dp", "row", "col")),
            P(None, ("dp", "row", "col")),
            P(None, ("dp", "row", "col")),
        ),
        out_specs=(
            P(("dp", "row"), "col"),
            P(("dp", "row"), "col"),
            P(None, ("col", "dp"), None, "row"),
            P(None, ("col", "dp"), None, "row"),
            P(None, ("col", "dp"), None, "row"),
            P(None, ("row", "dp"), "col"),
            P(None, ("row", "dp"), "col"),
            P(None, ("row", "dp"), "col"),
            P(None, ("col", "dp"), "row"),
            P(None, ("col", "dp"), "row"),
            P(None, ("col", "dp"), "row"),
            P(None, ("row", "dp"), "col"),
            P(None, ("row", "dp"), "col"),
            P(None, ("row", "dp"), "col"),
            P(None, ("dp", "row", "col")),
            P(None, ("dp", "row", "col")),
            P(None, ("dp", "row", "col")),
        ),
        check_vma=False,
    )
```

profile of v0, /device:TPU:0, one launch (start us, length us, event | category | flops | bytes accessed | tf_op | source)
XLA Modules:
  0.0 2294.3 jit_solution(2978077665630370329)
XLA Ops:
  8.7 43.8 %all-gather = f32[32,448,2]{1,2,0:T(2,128)S(1)} all-gather(f32[1,448,2]{1,2,0:T(2,128)} %bitcast.474), channel_id=1, replica_groups=mesh['dp'=8,'row'=2,'col'=2] {'dp','row','col'}, dimensions={0}, use_global_device_ids=true | all-gather | bytes 118272 | tf_op jit(solution)/shard_map/all_gather | solution.py:182
  59.2 20.7 all-gather.50.cloned.1.call-done
  82.6 60.6 %all-gather.34.cloned.1.call-done = bf16[2,512,3,512]{3,1,2,0:T(8,128)(2,1)} async-done(((bf16[2,64,3,512]{3,1,2,0:T(8,128)(2,1)}), bf16[2,512,3,512]{3,1,2,0:T(8,128)(2,1)}) %all-gather.34.cloned.1.call-update) | async-done | bytes 3145744 | tf_op jit(solution)/shard_map/all_gather | solution.py:177
  147.2 7.0 fusion.107
  155.8 36.3 %all-reduce.38.cloned.1.call-done = f32[1370,3,2,256]{3,0,2,1:T(8,128)} async-done(((f32[1370,3,2,256]{3,0,2,1:T(8,128)}), f32[1370,3,2,256]{3,0,2,1:T(8,128)}) %all-reduce.38.cloned.1.call-update) | async-done | bytes 8417296
  209.4 24.2 %while.44 = (s32[]{:T(128)}, bf16[4,1370,64]{1,2,0:T(8,128)(2,1)S(1)}, f32[4,1370]{1,0:T(4,128)S(1)}, bf16[4,3,1370,64]{3,2,1,0:T(8,128)(2,1)}, s32[]{:T(128)}, /*index=5*/s32[]{:T(128)}, s32[]{}, s32[]{}) while((s32[]{:T(128)}, bf16[4,1370,64]{1,2,0:T(8,128)(2,1)S(1)}, f32[4,1370]{1,0:T(4,128)S(1)}, bf16[4,3,1370,64]{3,2,1,0:T(8,128)(2,1)}, ...), condition=%wide.region_8.9_spmd, body=%wide.region_5.8_spmd.sunk | while | flops 493623328 | bytes 24256424 | solution.py:102
  235.7 10.0 all-gather.36.cloned.1.call-done
  248.2 41.4 %all-gather.38.cloned.1.call-done = bf16[2,512,512]{2,1,0:T(8,128)(2,1)} async-done(((bf16[2,64,512]{2,1,0:T(8,128)(2,1)}), bf16[2,512,512]{2,1,0:T(8,128)(2,1)}) %all-gather.38.cloned.1.call-update) | async-done | bytes 1048592 | tf_op jit(solution)/shard_map/all_gather | solution.py:178
  292.1 36.1 %fusion = f32[688,512]{1,0:T(8,128)} fusion(f32[1370,512]{1,0:T(8,128)S(1)} %fusion.121), kind=kCustom, calls=%all-reduce-scatter | all-reduce-scatter fusion | flops 704513 | bytes 4215296
  346.8 21.7 all-gather.52.cloned.1.call-done
  370.1 74.5 %all-gather.40.cloned.1.call-done = bf16[2,512,2048]{2,1,0:T(8,128)(2,1)} async-done(((bf16[2,64,2048]{2,1,0:T(8,128)(2,1)}), bf16[2,512,2048]{2,1,0:T(8,128)(2,1)}) %all-gather.40.cloned.1.call-update) | async-done | bytes 4194320 | tf_op jit(solution)/shard_map/all_gather | solution.py:179
  444.7 7.4 fusion.81
  452.1 17.6 fusion.1
  473.6 15.8 concatenate.9
  489.4 15.2 fusion.76
  505.7 13.2 all-gather.54.cloned.1.call-done
  525.0 71.2 %all-gather.42.cloned.1.call-done = bf16[2,2048,512]{2,1,0:T(8,128)(2,1)} async-done(((bf16[2,256,512]{2,1,0:T(8,128)(2,1)}), bf16[2,2048,512]{2,1,0:T(8,128)(2,1)}) %all-gather.42.cloned.1.call-update) | async-done | bytes 4194320 | tf_op jit(solution)/shard_map/all_gather | solution.py:180
  596.2 7.9 fusion.83
  604.1 36.2 %fusion.2 = f32[688,512]{1,0:T(8,128)S(1)} fusion(f32[1370,512]{1,0:T(8,128)} %fusion.83), kind=kCustom, calls=%all-reduce-scatter.2 | all-reduce-scatter fusion | flops 704513 | bytes 4215296
  657.4 23.1 %all-gather.56.cloned.1.call-done = bf16[2,685,512]{2,1,0:T(8,128)(2,1)} async-done(((bf16[1,685,512]{2,1,0:T(8,128)(2,1)}), bf16[2,685,512]{2,1,0:T(8,128)(2,1)}) %all-gather.56.cloned.1.call-update) | async-done | bytes 1402896 | tf_op jit(solution)/shard_map/all_gather | solution.py:35
  682.2 7.1 fusion.105
  691.5 36.9 %all-reduce.40.cloned.1.call-done = f32[1370,3,2,256]{3,0,2,1:T(8,128)} async-done(((f32[1370,3,2,256]{3,0,2,1:T(8,128)}), f32[1370,3,2,256]{3,0,2,1:T(8,128)}) %all-reduce.40.cloned.1.call-update) | async-done | bytes 8417296
  749.3 24.1 %while.45 = (s32[]{:T(128)}, bf16[4,1370,64]{1,2,0:T(8,128)(2,1)S(1)}, f32[4,1370]{1,0:T(4,128)S(1)}, bf16[4,3,1370,64]{3,2,1,0:T(8,128)(2,1)}, s32[]{:T(128)}, /*index=5*/s32[]{:T(128)}, s32[]{}, s32[]{}) while((s32[]{:T(128)}, bf16[4,1370,64]{1,2,0:T(8,128)(2,1)S(1)}, f32[4,1370]{1,0:T(4,128)S(1)}, bf16[4,3,1370,64]{3,2,1,0:T(8,128)(2,1)}, ...), condition=%wide.region_24.25_spmd, body=%wide.region_21.24_spmd.sunk | while | flops 493623328 | bytes 24256424 | solution.py:102
  778.1 8.0 all-gather.44.cloned.1.call-done
  792.5 38.0 %fusion.3 = f32[688,512]{1,0:T(8,128)S(1)} fusion(f32[1370,512]{1,0:T(8,128)} %fusion.119), kind=kCustom, calls=%all-reduce-scatter.3 | all-reduce-scatter fusion | flops 704513 | bytes 4215296
  833.1 9.4 fusion.86
  852.3 17.6 fusion.6
  879.7 8.0 fusion.85
  887.7 17.7 fusion.4
  908.5 15.7 concatenate.14
  924.2 15.7 concatenate.12
  939.9 17.6 convert_reduce_fusion
  957.6 15.9 all-gather.64.cloned.1.call-done
  979.6 7.9 fusion.84
  987.5 38.1 %fusion.7 = f32[688,512]{1,0:T(8,128)S(1)} fusion(f32[1370,512]{1,0:T(8,128)} %fusion.84), kind=kCustom, calls=%all-reduce-scatter.7 | all-reduce-scatter fusion | flops 704513 | bytes 4215296
  1045.7 25.5 %all-gather.66.cloned.1.call-done = bf16[2,685,512]{2,1,0:T(8,128)(2,1)} async-done(((bf16[1,685,512]{2,1,0:T(8,128)(2,1)}), bf16[2,685,512]{2,1,0:T(8,128)(2,1)}) %all-gather.66.cloned.1.call-update) | async-done | bytes 1402896 | tf_op jit(solution)/shard_map/all_gather | solution.py:35
  1075.3 10.5 reduce-scatter.36.cloned.1.call-done
  1089.2 98.4 %while.46 = (s32[]{:T(128)}, bf16[4,3,1370,64]{2,3,1,0:T(8,128)(2,1)}, bf16[4,3,1370,64]{3,2,1,0:T(8,128)(2,1)}, f32[4,1370]{1,0:T(4,128)}, bf16[4,1370,64]{1,2,...) while((s32[]{:T(128)}, bf16[4,3,1370,64]{2,3,1,0:T(8,128)(2,1)}, ...), condition=%wide.region_41.42_spmd, body=%wide.region_39.41_spmd.sunk | while | flops 1218158848 | bytes 75067408 | solution.py:134
  1195.1 14.8 all-gather.46.cloned.1.call-done
  1210.0 18.8 copy.94
  1241.6 38.9 %fusion.8 = f32[688,512]{1,0:T(8,128)} fusion(f32[1370,512]{1,0:T(8,128)} %convolution_bitcast_fusion.5), kind=kCustom, calls=%all-reduce-scatter.8 | all-reduce-scatter fusion | flops 704513 | bytes 4215296
  1300.7 27.5 %all-gather.68.cloned.1.call-done = bf16[2,685,512]{2,1,0:T(8,128)(2,1)} async-done(((bf16[1,685,512]{2,1,0:T(8,128)(2,1)}), bf16[2,685,512]{2,1,0:T(8,128)(2,1)}) %all-gather.68.cloned.1.call-update) | async-done | bytes 1402896 | tf_op jit(solution)/shard_map/all_gather | solution.py:35
  1329.8 8.0 fusion.82
  1337.8 17.6 fusion.9
  1359.3 15.7 concatenate.17
  1375.1 9.4 convert_reduce_fusion.1
  1384.9 15.5 all-gather.70.cloned.1.call-done
  1406.6 7.9 fusion.80
  1414.5 38.9 %fusion.10 = f32[688,512]{1,0:T(8,128)} fusion(f32[1370,512]{1,0:T(8,128)} %fusion.80), kind=kCustom, calls=%all-reduce-scatter.10 | all-reduce-scatter fusion | flops 704513 | bytes 4215296
  1473.8 27.5 %all-gather.72.cloned.1.call-done = bf16[2,685,512]{2,1,0:T(8,128)(2,1)} async-done(((bf16[1,685,512]{2,1,0:T(8,128)(2,1)}), bf16[2,685,512]{2,1,0:T(8,128)(2,1)}) %all-gather.72.cloned.1.call-update) | async-done | bytes 1402896 | tf_op jit(solution)/shard_map/all_gather | solution.py:35
  1505.4 7.4 fusion.77
  1519.2 100.6 %while.47 = (s32[]{:T(128)}, bf16[4,3,1370,64]{2,3,1,0:T(8,128)(2,1)}, bf16[4,3,1370,64]{3,2,1,0:T(8,128)(2,1)}, f32[4,1370]{1,0:T(4,128)}, bf16[4,1370,64]{1,2,...) while((s32[]{:T(128)}, bf16[4,3,1370,64]{2,3,1,0:T(8,128)(2,1)}, ...), condition=%wide.region_56.57_spmd, body=%wide.region_54.56_spmd.sunk | while | flops 1218158848 | bytes 75067408 | solution.py:134
  1522.1 6.9 multiply_reduce_fusion.21
  1529.1 7.2 multiply_convert_fusion.10
  1637.0 7.4 reshape.399
  1659.6 7.8 convolution_bitcast_fusion.2
  1667.5 7.6 fusion.87
  1678.8 8.7 convolution_bitcast_fusion.3
  1689.0 18.9 copy.100
  1720.5 67.9 %fusion.133 = (f32[688,512]{1,0:T(8,128)S(1)}, f32[688,512]{1,0:T(8,128)S(1)}) fusion(f32[1370,512]{1,0:T(8,128)} %fusion.87, f32[1370,512]{1,0:T(8,128)} %convolution_bitcast_fusion.4), kind=kCustom, calls=%all-reduce-scatter.12 | all-reduce-scatter fusion | flops 1409025 | bytes 8430080
  1834.9 7.9 pad_maximum_fusion
  1877.1 137.4 %reduce-scatter.48.cloned.1.call-done = f32[448,2]{1,0:T(8,128)} async-done(((f32[14336,2]{1,0:T(8,128)}), f32[448,2]{1,0:T(8,128)}) %reduce-scatter.48.cloned.1.call-update) | async-done | bytes 3600
  2016.9 146.7 %reduce-scatter.44.cloned.1.call-done = f32[2,64,2048]{2,1,0:T(8,128)} async-done(((f32[2,512,2048]{2,1,0:T(8,128)}), f32[2,64,2048]{2,1,0:T(8,128)}) %reduce-scatter.44.cloned.1.call-update) | async-done | bytes 1048592 | tf_op jit(solution)/shard_map/reduce_scatter | solution.py:396
  2168.0 116.6 %reduce-scatter.40.cloned.1.call-done = f32[2,64,3,512]{3,1,2,0:T(8,128)} async-done(((f32[2,512,3,512]{3,1,2,0:T(8,128)}), f32[2,64,3,512]{3,1,2,0:T(8,128)}) %reduce-scatter.40.cloned.1.call-update) | async-done | bytes 786448 | tf_op jit(solution)/shard_map/reduce_scatter | solution.py:394
  (696 shorter events, 637.9 us)
Async XLA Ops:
  7.2 51.1 %copy-start.30 = (f32[2,64,3,512]{3,1,2,0:T(8,128)S(1)}, f32[2,64,3,512]{3,1,2,0:T(8,128)}, u32[]{:S(2)}) copy-start(f32[2,64,3,512]{3,1,2,0:T(8,128)} %param.27) | copy-start | bytes 2359300
  7.2 72.7 %all-gather.50.cloned.1.call-start = ((), (), s32[]{:S(2)}) async-start(), calls=%async_computation.21 | async-start | bytes 2113536 | tf_op jit(solution)/shard_map/all_gather | solution.py:35
  52.7 182.9 %copy-start.45 = (f32[14336,2]{0,1:T(2,128)}, f32[14336,2]{0,1:T(2,128)S(1)}, u32[]{:S(2)}) copy-start(f32[14336,2]{0,1:T(2,128)S(1)} %reshape.387) | copy-start | bytes 344068
  58.2 84.9 %all-gather.34.cloned.1.call-start = ((), (), s32[]{:S(2)}) async-start(), calls=%async_computation.7 | async-start | bytes 3538944 | tf_op jit(solution)/shard_map/all_gather | solution.py:177
  59.1 133.0 %all-reduce.38.cloned.1.call-start = ((), (), s32[]{:S(2)}) async-start(), calls=%async_computation.34 | async-start | bytes 16908288
  154.3 91.4 %all-gather.36.cloned.1.call-start = ((), (), s32[]{:S(2)}) async-start(), calls=%async_computation.8 | async-start | bytes 2113536 | tf_op jit(solution)/shard_map/all_gather | solution.py:43
  233.6 56.1 %copy-start.48 = (f32[4,1370]{1,0:T(4,128)}, f32[4,1370]{1,0:T(4,128)S(1)}, u32[]{:S(2)}) copy-start(f32[4,1370]{1,0:T(4,128)S(1)} %get-tuple-element.555) | copy-start | bytes 65764
  234.8 54.9 %all-gather.38.cloned.1.call-start = ((), (), s32[]{:S(2)}) async-start(), calls=%async_computation.9 | async-start | bytes 1179648 | tf_op jit(solution)/shard_map/all_gather | solution.py:178
  235.5 133.0 %all-gather.52.cloned.1.call-start = ((), (), s32[]{:S(2)}) async-start(), calls=%async_computation.22 | async-start | bytes 2113536 | tf_op jit(solution)/shard_map/all_gather | solution.py:35
  235.6 102.5 %copy-start.68 = (f32[1,512]{1,0:T(1,128)}, f32[1,512]{1,0:T(1,128)S(1)}, u32[]{:S(2)}) copy-start(f32[1,512]{1,0:T(1,128)S(1)} %constant_dynamic-slice_fusion.21) | copy-start | bytes 6148
  235.7 106.9 %copy-start.76 = (f32[1,512]{1,0:T(1,128)}, f32[1,512]{1,0:T(1,128)S(1)}, u32[]{:S(2)}) copy-start(f32[1,512]{1,0:T(1,128)S(1)} %constant_dynamic-slice_fusion.14) | copy-start | bytes 6148
  329.0 3.9 collective-permute-start
  340.1 308.4 %copy-start.4 = (f32[685,512]{1,0:T(8,128)}, f32[685,512]{1,0:T(8,128)S(1)}, u32[]{:S(2)}) copy-start(f32[685,512]{1,0:T(8,128)S(1)} %get-tuple-element.296) | copy-start | bytes 4208644
  344.3 100.3 %all-gather.40.cloned.1.call-start = ((), (), s32[]{:S(2)}) async-start(), calls=%async_computation.10 | async-start | bytes 4718592 | tf_op jit(solution)/shard_map/all_gather | solution.py:179
  345.3 173.6 %all-gather.54.cloned.1.call-start = ((), (), s32[]{:S(2)}) async-start(), calls=%async_computation.23 | async-start | bytes 8454144 | tf_op jit(solution)/shard_map/all_gather | solution.py:39
  370.1 82.0 %copy-start.33 = (bf16[1370,512]{1,0:T(8,128)(2,1)}, bf16[1370,512]{1,0:T(8,128)(2,1)S(1)}, u32[]{:S(2)}) copy-start(bf16[1370,512]{1,0:T(8,128)(2,1)S(1)} %reshape.391) | copy-start | bytes 4208644
  470.5 3.1 collective-permute-start.1
  504.6 91.6 %all-gather.42.cloned.1.call-start = ((), (), s32[]{:S(2)}) async-start(), calls=%async_computation.11 | async-start | bytes 4718592 | tf_op jit(solution)/shard_map/all_gather | solution.py:180
  505.6 174.9 %all-gather.56.cloned.1.call-start = ((), (), s32[]{:S(2)}) async-start(), calls=%async_computation.24 | async-start | bytes 2113536 | tf_op jit(solution)/shard_map/all_gather | solution.py:35
  505.7 147.2 %copy-start.78 = (f32[1,512]{1,0:T(1,128)}, f32[1,512]{1,0:T(1,128)S(1)}, u32[]{:S(2)}) copy-start(f32[1,512]{1,0:T(1,128)S(1)} %constant_dynamic-slice_fusion.9) | copy-start | bytes 6148
  505.7 142.8 %copy-start.84 = (f32[1,512]{1,0:T(1,128)}, f32[1,512]{1,0:T(1,128)S(1)}, u32[]{:S(2)}) copy-start(f32[1,512]{1,0:T(1,128)S(1)} %constant_dynamic-slice_fusion.11) | copy-start | bytes 6148
  640.3 3.8 collective-permute-start.2
  650.3 196.5 %copy-start.6 = (f32[685,512]{1,0:T(8,128)}, f32[685,512]{1,0:T(8,128)S(1)}, u32[]{:S(2)}) copy-start(f32[685,512]{1,0:T(8,128)S(1)} %get-tuple-element.293) | copy-start | bytes 4208644
  654.6 73.9 %all-reduce.40.cloned.1.call-start = ((), (), s32[]{:S(2)}) async-start(), calls=%async_computation.35 | async-start | bytes 16908288
  689.3 86.1 %all-gather.62.cloned.1.call-start = ((), (), s32[]{:S(2)}) async-start(), calls=%async_computation.27 | async-start | bytes 2113536 | tf_op jit(solution)/shard_map/all_gather | solution.py:35
  691.4 94.7 %all-gather.44.cloned.1.call-start = ((), (), s32[]{:S(2)}) async-start(), calls=%async_computation.12 | async-start | bytes 2113536 | tf_op jit(solution)/shard_map/all_gather | solution.py:43
  775.2 102.9 %all-gather.58.cloned.1.call-start = ((), (), s32[]{:S(2)}) async-start(), calls=%async_computation.25 | async-start | bytes 2113536 | tf_op jit(solution)/shard_map/all_gather | solution.py:35
  775.3 71.4 %copy-start.83 = (f32[1,512]{1,0:T(1,128)}, f32[1,512]{1,0:T(1,128)S(1)}, u32[]{:S(2)}) copy-start(f32[1,512]{1,0:T(1,128)S(1)} %constant_dynamic-slice_fusion.5) | copy-start | bytes 6148
  830.5 12.0 collective-permute-start.3
  848.6 190.6 %copy-start.2 = (f32[685,512]{1,0:T(8,128)}, f32[685,512]{1,0:T(8,128)S(1)}, u32[]{:S(2)}) copy-start(f32[685,512]{1,0:T(8,128)S(1)} %get-tuple-element.292) | copy-start | bytes 4208644
  852.3 121.2 %all-gather.64.cloned.1.call-start = ((), (), s32[]{:S(2)}) async-start(), calls=%async_computation.28 | async-start | bytes 8454144 | tf_op jit(solution)/shard_map/all_gather | solution.py:39
  870.8 37.7 %collective-permute-start.6 = (f32[3,2048]{1,0:T(4,128)S(1)}, f32[3,2048]{1,0:T(4,128)S(1)}, u32[]{:S(2)}, u32[]{:S(2)}) collective-permute-start(f32[3,2048]{1,0:T(4,128)S(1)} %slice.286), channel_id=1, source_target_pairs={{0,1},{2,3},{4,5},{6,7},{8,9},{10,11},{12,13},{14,15},{16,17},{18,... | collective-permute-start | bytes 73736
  906.2 18.1 collective-permute-start.4
  957.6 113.6 %all-gather.66.cloned.1.call-start = ((), (), s32[]{:S(2)}) async-start(), calls=%async_computation.29 | async-start | bytes 2113536 | tf_op jit(solution)/shard_map/all_gather | solution.py:35
  1025.7 3.7 collective-permute-start.7
  1043.6 42.3 %reduce-scatter.36.cloned.1.call-start = ((), (), s32[]{:S(2)}) async-start(), calls=%async_computation.13 | async-start | bytes 4227072 | tf_op jit(solution)/shard_map/reduce_scatter | solution.py:47
  1075.3 134.7 %all-gather.46.cloned.1.call-start = ((), (), s32[]{:S(2)}) async-start(), calls=%async_computation.14 | async-start | bytes 6340608 | tf_op jit(solution)/shard_map/all_gather | solution.py:43
  1194.9 133.3 %all-gather.68.cloned.1.call-start = ((), (), s32[]{:S(2)}) async-start(), calls=%async_computation.30 | async-start | bytes 2113536 | tf_op jit(solution)/shard_map/all_gather | solution.py:35
  1241.6 48.4 %copy-start.62 = (f32[685]{0:T(1024)S(1)}, f32[685]{0:T(1024)}, u32[]{:S(2)}) copy-start(f32[685]{0:T(1024)} %copy-done.61) | copy-start | bytes 8224
  1241.6 48.4 %copy-start.79 = (f32[1,512]{1,0:T(1,128)S(1)}, f32[1,512]{1,0:T(1,128)}, u32[]{:S(2)}) copy-start(f32[1,512]{1,0:T(1,128)} %copy-done.78) | copy-start | bytes 6148
  1281.3 3.5 collective-permute-start.8
  1300.6 99.8 %all-gather.70.cloned.1.call-start = ((), (), s32[]{:S(2)}) async-start(), calls=%async_computation.31 | async-start | bytes 8454144 | tf_op jit(solution)/shard_map/all_gather | solution.py:39
  1356.2 3.1 collective-permute-start.9
  1384.5 116.7 %all-gather.72.cloned.1.call-start = ((), (), s32[]{:S(2)}) async-start(), calls=%async_computation.32 | async-start | bytes 2113536 | tf_op jit(solution)/shard_map/all_gather | solution.py:35
  1414.5 48.5 %copy-start.5 = (f32[685,512]{1,0:T(8,128)S(1)}, f32[685,512]{1,0:T(8,128)}, u32[]{:S(2)}) copy-start(f32[685,512]{1,0:T(8,128)} %copy-done.4) | copy-start | bytes 4208644
  1414.5 48.5 %copy-start.56 = (f32[685]{0:T(1024)S(1)}, f32[685]{0:T(1024)}, u32[]{:S(2)}) copy-start(f32[685]{0:T(1024)} %copy-done.55) | copy-start | bytes 8224
  1414.5 48.5 %copy-start.58 = (f32[685]{0:T(1024)S(1)}, f32[685]{0:T(1024)}, u32[]{:S(2)}) copy-start(f32[685]{0:T(1024)} %copy-done.57) | copy-start | bytes 8224
  1414.5 48.6 %copy-start.77 = (f32[1,512]{1,0:T(1,128)S(1)}, f32[1,512]{1,0:T(1,128)}, u32[]{:S(2)}) copy-start(f32[1,512]{1,0:T(1,128)} %copy-done.76) | copy-start | bytes 6148
  1454.3 3.5 collective-permute-start.10
  1473.7 42.2 %reduce-scatter.38.cloned.1.call-start = ((), (), s32[]{:S(2)}) async-start(), calls=%async_computation.15 | async-start | bytes 4227072 | tf_op jit(solution)/shard_map/reduce_scatter | solution.py:47
  1505.4 131.6 %all-gather.60.cloned.1.call-start = ((), (), s32[]{:S(2)}) async-start(), calls=%async_computation.26 | async-start | bytes 8454144 | tf_op jit(solution)/shard_map/all_gather | solution.py:39
  1512.8 176.0 %all-gather.48.cloned.1.call-start = ((), (), s32[]{:S(2)}) async-start(), calls=%async_computation.16 | async-start | bytes 6340608 | tf_op jit(solution)/shard_map/all_gather | solution.py:43
  1627.3 233.0 %reduce-scatter.42.cloned.1.call-start = ((), (), s32[]{:S(2)}) async-start(), calls=%async_computation.18 | async-start | bytes 2359296 | tf_op jit(solution)/shard_map/reduce_scatter | solution.py:395
  1636.7 229.7 %reduce-scatter.46.cloned.1.call-start = ((), (), s32[]{:S(2)}) async-start(), calls=%async_computation.20 | async-start | bytes 9437184 | tf_op jit(solution)/shard_map/reduce_scatter | solution.py:397
  1658.0 356.5 %reduce-scatter.48.cloned.1.call-start = ((), (), s32[]{:S(2)}) async-start(), calls=%async_computation.33 | async-start | bytes 7569408
  1720.5 83.6 %copy-start.11 = (bf16[685,512]{1,0:T(8,128)(2,1)S(1)}, bf16[685,512]{1,0:T(8,128)(2,1)}, u32[]{:S(2)}) copy-start(bf16[685,512]{1,0:T(8,128)(2,1)} %param.25) | copy-start | bytes 2104324
  1788.4 11.8 collective-permute-start.11
  1798.2 12.0 collective-permute-start.5
  1834.8 328.8 %reduce-scatter.44.cloned.1.call-start = ((), (), s32[]{:S(2)}) async-start(), calls=%async_computation.19 | async-start | bytes 9437184 | tf_op jit(solution)/shard_map/reduce_scatter | solution.py:396
  1842.8 441.8 %reduce-scatter.40.cloned.1.call-start = ((), (), s32[]{:S(2)}) async-start(), calls=%async_computation.17 | async-start | bytes 7077888 | tf_op jit(solution)/shard_map/reduce_scatter | solution.py:394
  1874.0 141.6 %copy-start.87 = (f32[2,448]{1,0:T(2,128)S(1)}, f32[2,448]{1,0:T(2,128)}, u32[]{:S(2)}) copy-start(f32[2,448]{1,0:T(2,128)} %param.39) | copy-start | bytes 10756
  1877.1 407.5 %copy-start.31 = (f32[2,64,3,512]{3,1,2,0:T(8,128)S(1)}, f32[2,64,3,512]{3,1,2,0:T(8,128)}, u32[]{:S(2)}) copy-start(f32[2,64,3,512]{3,1,2,0:T(8,128)} %param.27) | copy-start | bytes 2359300
  1877.1 407.5 %copy-start.43 = (f32[2,64,3,512]{3,1,2,0:T(8,128)S(1)}, f32[2,64,3,512]{3,1,2,0:T(8,128)}, u32[]{:S(2)}) copy-start(f32[2,64,3,512]{3,1,2,0:T(8,128)} %param.29) | copy-start | bytes 2359300
  1877.1 407.5 %copy-start.44 = (f32[2,64,3,512]{3,1,2,0:T(8,128)S(1)}, f32[2,64,3,512]{3,1,2,0:T(8,128)}, u32[]{:S(2)}) copy-start(f32[2,64,3,512]{3,1,2,0:T(8,128)} %param.28) | copy-start | bytes 2359300
  (105 other events, 1145.8 us)
Sparse Core Ops, SparseCore 0:
  58.4 21.4 all-gather.49
  82.6 60.4 all-gather.33
  154.4 37.6 all-reduce.37
  234.9 10.7 all-gather.35
  248.3 41.3 all-gather.37
  344.5 23.9 all-gather.51
  371.3 73.3 all-gather.39
  504.8 14.0 all-gather.53
  521.6 74.5 all-gather.41
  654.7 25.7 all-gather.55
  689.4 38.9 all-reduce.39
  730.4 26.5 all-gather.61
  775.3 10.7 all-gather.43
  852.4 25.6 all-gather.57
  957.7 15.7 all-gather.63
  1043.7 27.4 all-gather.65
  1075.4 10.3 reduce-scatter.35
  1195.0 14.9 all-gather.45
  1300.8 27.3 all-gather.67
  1384.6 15.8 all-gather.69
  1473.8 27.3 all-gather.71
  1505.5 10.3 reduce-scatter.37
  1517.5 17.0 all-gather.59
  1627.5 14.9 all-gather.47
  1646.0 68.8 reduce-scatter.41
  1718.4 147.9 reduce-scatter.45
  1868.7 145.8 reduce-scatter.47
  2018.6 144.9 reduce-scatter.43
  2167.2 117.3 reduce-scatter.39
where the time goes:
time: 2310 us; the launch traced here: 2290 us
  waiting for transfers between devices  973 us (42%)
  blocking collectives  430 us (19%)
  local copies, waits for them, and re-layouts  320 us (14%)
  matrix products  313 us (14%)
  other arithmetic  208 us (9%)
  starting transfers between devices  33.7 us (1%)
    unnamed x11, blocking collectives  365 us
    dot_general x64, matrix products, contract(): lax.dot_general(left, right, ((left_dims, right_dims), ((), ())), preferr...  279 us
    unnamed x44, waiting for transfers between devices  217 us
    unnamed x307, local copies, waits for them, and re-layouts  189 us
    all_gather x8, waiting for transfers between devices, row_rows(): return lax.all_gather(values, 'row', axis=0, tiled=True)  151 us
    reduce_scatter x1, waiting for transfers between devices, local(): lax.psum_scatter(grads[2], 'dp', scatter_dimension=1, tiled=True)  147 us
    reduce_scatter x1, waiting for transfers between devices, local(): lax.psum_scatter(grads[0], 'dp', scatter_dimension=1, tiled=True)  117 us
    all_gather x1, waiting for transfers between devices, local(): lax.all_gather(expand_master.astype(jnp.bfloat16), 'dp', axis=1, tiled=True)  74.5 us
  transfers between devices with their start and end apart: 41, of which 31 were waited for; matrix products, arithmetic and copies ran while one was open for 22% of the time, Pallas kernels for 0%

commit v1 on v0

v1 whole, which is shorter than its diff:
```python
import jax
import jax.numpy as jnp
from jax import lax
from jax.sharding import PartitionSpec as P

D = 1024
HEAD_DIM = 64
FF = 4096
LAYERS = 2
STEP = 10
TILE = 16

norm_epsilon = 1e-06
beta_first = 0.9
beta_second = 0.999
adam_epsilon = 1e-08
learn_rate = 0.02
vector_rate = 0.1
decay_rate = 0.05
bf16 = jnp.bfloat16
f32 = jnp.float32


def contract(left, right, left_dims, right_dims):
    return lax.dot_general(
        left, right, ((left_dims, right_dims), ((), ())), preferred_element_type=f32
    )


def swap(values, axis):
    return lax.ppermute(values, axis, [(0, 1), (1, 0)])


def pair_swap(values):
    count = lax.axis_size("dp")
    return lax.ppermute(values, "dp", [(at, at ^ 1) for at in range(count)])


def shifted(values, step):
    count = lax.axis_size("dp")
    return lax.ppermute(values, "dp", [(at, (at + step) % count) for at in range(count)])


def ordered(mine, other, place, axis):
    return jnp.where(
        place == 0,
        jnp.concatenate([mine, other], axis),
        jnp.concatenate([other, mine], axis),
    )


def dp_gather(block):
    count = lax.axis_size("dp")
    at = lax.axis_index("dp")
    place = at % 2
    line = jnp.stack([block] + [shifted(block, step) for step in range(2, count, 2)])
    both = ordered(line[:, None], pair_swap(line)[:, None], place, 1)
    pairs = count // 2
    back = (at // 2 - jnp.arange(pairs)) % pairs
    return jnp.take(both, back, axis=0).reshape((count,) + block.shape)


def dp_scatter(blocks):
    count = lax.axis_size("dp")
    at = lax.axis_index("dp")
    place = at % 2
    split = blocks.reshape((count // 2, 2) + blocks.shape[1:])
    mine = lax.dynamic_index_in_dim(split, place, 1, False)
    other = lax.dynamic_index_in_dim(split, 1 - place, 1, False)
    summed = (mine.astype(f32) + pair_swap(other).astype(f32)).astype(blocks.dtype)
    total = lax.dynamic_index_in_dim(summed, at // 2, 0, False).astype(f32)
    for step in range(1, count // 2):
        part = lax.dynamic_index_in_dim(summed, (at // 2 + step) % (count // 2), 0, False)
        total = total + shifted(part, 2 * step).astype(f32)
    return total


def gelu_value(values):
    return jax.nn.gelu(values, approximate=False)


def norm_forward(values, gain, shift):
    centre = jnp.sum(values, 1, keepdims=True) / D
    spread = jnp.sum(values * values, 1, keepdims=True) / D - centre * centre
    inverse = lax.rsqrt(spread + norm_epsilon)
    unit = (values - centre) * inverse
    return ((unit * gain + shift).astype(bf16), unit, inverse)


def norm_backward(grad, unit, inverse, gain):
    scaled = grad * gain
    first = jnp.sum(scaled, 1, keepdims=True)
    second = jnp.sum(scaled * unit, 1, keepdims=True)
    return inverse * (scaled - first / D - unit * (second / D))


def attend_forward(stacked, bias):
    factor = HEAD_DIM ** (-0.5)

    def one_head(block):
        scores = contract(block[0], block[1], (1,), (1,)) * factor + bias
        peak = jnp.max(scores, 1, keepdims=True)
        weights = jnp.exp(scores - peak)
        total = jnp.sum(weights, 1, keepdims=True)
        probs = (weights / total).astype(bf16)
        return (
            jnp.dot(probs, block[2], preferred_element_type=f32),
            (peak + jnp.log(total))[:, 0],
        )

    return lax.map(one_head, stacked)


def attend_backward(stacked, logsum, grads, bias):
    factor = HEAD_DIM ** (-0.5)

    def one_head(pack):
        block, norm_log, back = pack
        scores = contract(block[0], block[1], (1,), (1,)) * factor + bias
        probs = jnp.exp(scores - norm_log[:, None])
        back_probs = contract(back, block[2], (1,), (1,))
        inner = jnp.sum(probs * back_probs, 1, keepdims=True)
        back_scores = (probs * (back_probs - inner)).astype(bf16)
        grad_query = jnp.dot(back_scores, block[1], preferred_element_type=f32) * factor
        grad_key = contract(back_scores, block[0], (0,), (0,)) * factor
        grad_value = contract(probs.astype(bf16), back, (0,), (0,))
        return jnp.stack([grad_query, grad_key, grad_value])

    return lax.map(one_head, (stacked, logsum, grads))


def adam_step(master, first, second, grad, rate, decay):
    first_new = beta_first * first + (1.0 - beta_first) * grad
    second_new = beta_second * second + (1.0 - beta_second) * grad * grad
    ratio = (
        first_new
        / (1.0 - beta_first**STEP)
        / (jnp.sqrt(second_new / (1.0 - beta_second**STEP)) + adam_epsilon)
    )
    return (first_new, second_new, master - rate * (ratio + decay * master))


MARKS = [0, D, 2 * D, 3 * D, 4 * D, 5 * D, 6 * D, 7 * D, 8 * D, 8 * D + FF, 9 * D + FF, 10 * D + FF]


def local(
    images,
    cotangent,
    triplet_master,
    triplet_first,
    triplet_second,
    project_master,
    project_first,
    project_second,
    expand_master,
    expand_first,
    expand_second,
    shrink_master,
    shrink_first,
    shrink_second,
    vectors_master,
    vectors_first,
    vectors_second,
):
    count = lax.axis_size("dp")
    row_at = lax.axis_index("row")
    col_at = lax.axis_index("col")
    tokens, features = images.shape
    rows = -(-tokens // (2 * TILE)) * TILE
    group = 2 * rows
    half = D // 2
    heads = half // 2 // HEAD_DIM
    width = heads * HEAD_DIM

    def to_tokens(values):
        padded = jnp.pad(values, ((0, 2 * rows - tokens), (0, 0))).reshape(2, rows, features)
        mine = lax.dynamic_index_in_dim(padded, col_at, 0, False)
        other = swap(lax.dynamic_index_in_dim(padded, 1 - col_at, 0, False), "col")
        return ordered(mine, other, col_at, 1)

    def to_features(values):
        split = values.reshape(rows, 2, features).transpose(1, 0, 2)
        mine = lax.dynamic_index_in_dim(split, col_at, 0, False)
        other = swap(lax.dynamic_index_in_dim(split, 1 - col_at, 0, False), "col")
        return ordered(mine, other, col_at, 0)[:tokens]

    def row_rows(values):
        return jnp.concatenate([values, swap(values, "row")], 0)

    def row_sum(partial):
        return partial[:rows] + swap(partial[rows:].astype(bf16), "row").astype(f32)

    shard_shapes = [
        values.shape[1:] for values in (triplet_master, project_master, expand_master, shrink_master)
    ]
    lane = half

    def flat(parts):
        return jnp.concatenate([part.reshape(-1, lane) for part in parts], 0)

    def unflat(values, lead=()):
        parts = []
        at = 0
        for shape in shard_shapes:
            size = 1
            for side in shape:
                size *= side
            size //= lane
            parts.append(values[..., at : at + size, :].reshape(lead + shape))
            at += size
        return parts

    weights = []
    for layer in range(LAYERS):
        block = flat(
            [
                values[layer].astype(bf16)
                for values in (triplet_master, project_master, expand_master, shrink_master)
            ]
        )
        column = dp_gather(block)
        both = ordered(column[None], swap(column, "col")[None], col_at, 0)
        qkv, mix, up, down = unflat(both, (2, count))
        weights.append(
            (
                qkv.reshape(D, 3, half),
                mix.transpose(1, 2, 0, 3).reshape(half, D),
                up.reshape(D, FF // 2),
                down.transpose(1, 2, 0, 3).reshape(FF // 2, D),
            )
        )

    spot = vectors_master
    spot = ordered(spot[:, None], swap(spot, "col")[:, None], col_at, 1)
    spot = ordered(spot[:, None], swap(spot, "row")[:, None], row_at, 1)
    vectors = dp_gather(spot).transpose(1, 0, 2, 3, 4).reshape(LAYERS, -1)

    place = jnp.arange(2 * group) % rows
    late = jnp.arange(2 * group) // group
    valid = place + late * rows < tokens
    bias = jnp.where(valid, 0.0, -1e30).astype(f32)[None]

    def to_heads(values, parts):
        split = values.reshape(group, parts, 2, width).transpose(2, 0, 1, 3)
        mine = lax.dynamic_index_in_dim(split, col_at, 0, False)
        other = swap(lax.dynamic_index_in_dim(split, 1 - col_at, 0, False), "col")
        return (
            ordered(mine, other, col_at, 0)
            .reshape(2 * group, parts, heads, HEAD_DIM)
            .transpose(2, 1, 0, 3)
        )

    def from_heads(values):
        parts = values.shape[1]
        split = values.transpose(2, 1, 0, 3).reshape(2, group, parts, width)
        mine = lax.dynamic_index_in_dim(split, col_at, 0, False)
        other = swap(lax.dynamic_index_in_dim(split, 1 - col_at, 0, False), "col")
        return ordered(mine[:, :, None], other[:, :, None], col_at, 2).reshape(group, parts, half)

    head_start = row_at * half + col_at * width

    def pieces(vector):
        return [vector[MARKS[at] : MARKS[at + 1]] for at in range(11)]

    state = to_tokens(images).astype(f32)
    kept = []
    layer_pieces = []
    for layer in range(LAYERS):
        parts = pieces(vectors[layer])
        layer_pieces.append(parts)
        triplet_w, project_w, expand_w, shrink_w = weights[layer]
        normed, unit_one, inverse_one = norm_forward(state, parts[0], parts[1])
        normed_all = row_rows(normed)
        half_start = row_at * half
        biases = jnp.stack(
            [
                lax.dynamic_slice_in_dim(parts[2], half_start, half),
                jnp.zeros((half,), f32),
                lax.dynamic_slice_in_dim(parts[3], half_start, half),
            ]
        )
        triple = (contract(normed_all, triplet_w, (1,), (0,)) + biases).astype(bf16)
        stacked = to_heads(triple, 3)
        results, logsum = attend_forward(stacked, bias)
        mixed = from_heads(results.astype(bf16)[:, None])[:, 0]
        branch = row_sum(contract(mixed, project_w, (1,), (0,))) + parts[4]
        middle = state + parts[5] * branch
        normed_two, unit_two, inverse_two = norm_forward(middle, parts[6], parts[7])
        normed_two_all = row_rows(normed_two)
        hidden_bias = lax.dynamic_slice_in_dim(parts[8], row_at * (FF // 2), FF // 2)
        inner = contract(normed_two_all, expand_w, (1,), (0,)) + hidden_bias
        active = gelu_value(inner).astype(bf16)
        output = row_sum(contract(active, shrink_w, (1,), (0,))) + parts[9]
        kept.append(
            (
                unit_one,
                inverse_one,
                normed_all,
                stacked,
                logsum,
                mixed,
                branch,
                unit_two,
                inverse_two,
                normed_two_all,
                inner,
                active,
                output,
            )
        )
        state = middle + parts[10] * output
    block_out = to_features(state.astype(bf16))
    grad = to_tokens(cotangent).astype(f32)
    reduced = [None] * LAYERS
    vector_grads = [None] * LAYERS
    for layer in reversed(range(LAYERS)):
        (
            unit_one,
            inverse_one,
            normed_all,
            stacked,
            logsum,
            mixed,
            branch,
            unit_two,
            inverse_two,
            normed_two_all,
            inner,
            active,
            output,
        ) = kept[layer]
        parts = layer_pieces[layer]
        triplet_w, project_w, expand_w, shrink_w = weights[layer]
        output_scale_grad = jnp.sum(grad * output, 0)
        back_out = (parts[10] * grad).astype(bf16)
        output_bias_grad = jnp.sum(back_out.astype(f32), 0)
        back_out_all = row_rows(back_out)
        shrink_grad = contract(active, back_out_all, (0,), (0,)).astype(bf16)
        back_active = contract(back_out_all, shrink_w, (1,), (1,))
        back_inner = jax.vjp(gelu_value, inner)[1](back_active)[0].astype(bf16)
        hidden_bias_grad = jnp.sum(back_inner.astype(f32), 0)
        expand_grad = contract(normed_two_all, back_inner, (0,), (0,)).astype(bf16)
        back_two = row_sum(contract(back_inner, expand_w, (1,), (1,)))
        second_gain_grad = jnp.sum(back_two * unit_two, 0)
        second_shift_grad = jnp.sum(back_two, 0)
        grad_middle = grad + norm_backward(back_two, unit_two, inverse_two, parts[6])
        branch_scale_grad = jnp.sum(grad_middle * branch, 0)
        back_branch = (parts[5] * grad_middle).astype(bf16)
        mixer_bias_grad = jnp.sum(back_branch.astype(f32), 0)
        back_branch_all = row_rows(back_branch)
        project_grad = contract(mixed, back_branch_all, (0,), (0,)).astype(bf16)
        back_mixed = contract(back_branch_all, project_w, (1,), (1,)).astype(bf16)
        back_heads = to_heads(back_mixed[:, None], 1)[:, 0]
        back_stacked = attend_backward(stacked, logsum, back_heads, bias).astype(bf16)
        triple_sums = jnp.sum(back_stacked.astype(f32), 2)
        back_triple = from_heads(back_stacked)
        triplet_grad = contract(normed_all, back_triple, (0,), (0,)).astype(bf16)
        back_one = row_sum(contract(back_triple, triplet_w, (1, 2), (1, 2)))
        norm_gain_grad = jnp.sum(back_one * unit_one, 0)
        norm_shift_grad = jnp.sum(back_one, 0)
        grad = grad_middle + norm_backward(back_one, unit_one, inverse_one, parts[0])

        def spread(values, size, start):
            return lax.dynamic_update_slice_in_dim(jnp.zeros((size,), f32), values, start, 0)

        vector_grads[layer] = jnp.concatenate(
            [
                norm_gain_grad,
                norm_shift_grad,
                spread(triple_sums[:, 0].reshape(width), D, head_start),
                spread(triple_sums[:, 2].reshape(width), D, head_start),
                mixer_bias_grad,
                branch_scale_grad,
                second_gain_grad,
                second_shift_grad,
                spread(hidden_bias_grad, FF, row_at * (FF // 2)),
                output_bias_grad,
                output_scale_grad,
            ]
        )
        wide = [
            triplet_grad.reshape(2, count, -1, lane),
            project_grad.reshape(count, -1, 2, lane).transpose(2, 0, 1, 3),
            expand_grad.reshape(2, count, -1, lane),
            shrink_grad.reshape(count, -1, 2, lane).transpose(2, 0, 1, 3),
        ]
        blocks = jnp.concatenate(wide, 2)
        mine = lax.dynamic_index_in_dim(blocks, col_at, 0, False)
        other = swap(lax.dynamic_index_in_dim(blocks, 1 - col_at, 0, False), "col")
        reduced[layer] = unflat(
            dp_scatter((mine.astype(f32) + other.astype(f32)).astype(bf16))
        )
    grad_out = to_features(grad)

    spots = jnp.stack(vector_grads).reshape(LAYERS, count, 2, 2, -1)
    for axis, at, dim in (("col", col_at, 3), ("row", row_at, 2)):
        mine = lax.dynamic_index_in_dim(spots, at, dim, False)
        spots = mine + swap(lax.dynamic_index_in_dim(spots, 1 - at, dim, False), axis)
    vector_reduced = dp_scatter(spots.transpose(1, 0, 2))

    outs = []
    states = (
        (triplet_master, triplet_first, triplet_second),
        (project_master, project_first, project_second),
        (expand_master, expand_first, expand_second),
        (shrink_master, shrink_first, shrink_second),
    )
    for kind, (master, first, second) in enumerate(states):
        total = jnp.stack([reduced[layer][kind] for layer in range(LAYERS)])
        outs += adam_step(master, first, second, total, learn_rate, decay_rate)
    outs += adam_step(
        vectors_master, vectors_first, vectors_second, vector_reduced, vector_rate, 0.0
    )
    return (block_out, grad_out, *outs)


def solution(mesh):
    tokens = P(("dp", "row"), "col")
    triplet = P(None, ("col", "dp"), None, "row")
    narrow = P(None, ("row", "dp"), "col")
    wide = P(None, ("col", "dp"), "row")
    vector = P(None, ("dp", "row", "col"))
    states = (triplet,) * 3 + (narrow,) * 3 + (wide,) * 3 + (narrow,) * 3 + (vector,) * 3
    return jax.shard_map(
        local,
        mesh=mesh,
        in_specs=(tokens, tokens) + states,
        out_specs=(tokens, tokens) + states,
        check_vma=False,
    )
```

time: 2310 us -> 1730 us (0.75)
  waiting for transfers between devices: 973 us -> 542 us
  blocking collectives: 430 us -> 0 us
  local copies, waits for them, and re-layouts: 320 us -> 472 us
  starting transfers between devices: 33.7 us -> 103 us
  matrix products: 313 us -> 374 us
    ppermute x0 -> x60, waiting for transfers between devices: none -> 542 us  [the longest x18 209 us: shifted(): lax.ppermute(values, 'dp', [(at, (at + step) % count) for at in range(cou...]
    all_gather x20 -> x0, waiting for transfers between devices: 476 us -> none  [the longest x8 151 us: row_rows(): return lax.all_gather(values, 'row', axis=0, tiled=True)]
    unnamed x11 -> x0, blocking collectives: 365 us -> none
    reduce_scatter x6 -> x0, waiting for transfers between devices: 280 us -> none  [the longest x1 147 us: local(): lax.psum_scatter(grads[2], 'dp', scatter_dimension=1, tiled=True)]
    unnamed x44 -> x0, waiting for transfers between devices: 217 us -> none
    unnamed x307 -> x394, local copies, waits for them, and re-layouts: 189 us -> 74.5 us
    ppermute x0 -> x60, starting transfers between devices: none -> 103 us  [the longest x18 74.4 us: shifted(): lax.ppermute(values, 'dp', [(at, (at + step) % count) for at in range(cou...]
    reshape x2 -> x24, local copies, waits for them, and re-layouts: 12.5 us -> 115 us  [the longest x4 26.2 us: local(): shrink_grad.reshape(count, -1, 2, lane).transpose(2, 0, 1, 3)]
  transfers between devices with their start and end apart: 41 -> 60, of which waited for: 31 -> 29; matrix products, arithmetic and copies ran while one was open for 22% -> 33% of each run, Pallas kernels for 0% -> 0%
where the time goes in v1:
time: 1730 us; the launch traced here: 1700 us
  waiting for transfers between devices  542 us (31%)
  local copies, waits for them, and re-layouts  472 us (27%)
  matrix products  374 us (22%)
  other arithmetic  208 us (12%)
  starting transfers between devices  103 us (6%)
    dot_general x64, matrix products, contract(): lax.dot_general(left, right, ((left_dims, right_dims), ((), ())), preferr...  311 us
    ppermute x18, waiting for transfers between devices, shifted(): lax.ppermute(values, 'dp', [(at, (at + step) % count) for at in range(cou...  209 us
    ppermute x6, waiting for transfers between devices, pair_swap(): return lax.ppermute(values, 'dp', [(at, at ^ 1) for at in range(count)])  174 us
    ppermute x36, waiting for transfers between devices, swap(): return lax.ppermute(values, axis, [(0, 1), (1, 0)])  160 us
    unnamed x394, local copies, waits for them, and re-layouts  74.5 us
    ppermute x18, starting transfers between devices, shifted(): lax.ppermute(values, 'dp', [(at, (at + step) % count) for at in range(cou...  74.4 us
    convert_element_type x8, other arithmetic, one_head(): back_scores = (probs * (back_probs - inner)).astype(bf16)  51.9 us
    slice x10, local copies, waits for them, and re-layouts, unflat(): parts.append(values[..., at:at + size, :].reshape(lead + shape))  49 us
  transfers between devices with their start and end apart: 60, of which 29 were waited for; matrix products, arithmetic and copies ran while one was open for 33% of the time, Pallas kernels for 0%

profile of v1, /device:TPU:0, one launch (start us, length us, event | category | flops | bytes accessed | tf_op | source)
XLA Modules:
  0.0 1704.5 jit_solution(16101094597464114912)
XLA Ops:
  14.5 14.2 collective-permute-done.8
  31.1 31.3 %collective-permute-done.9 = bf16[768,512]{1,0:T(8,128)(2,1)S(1)} collective-permute-done((bf16[768,512]{1,0:T(8,128)(2,1)}, bf16[768,512]{1,0:T(8,128)(2,1)S(1)}, u32[]{:S(2)}, u32[]{:S(2)}) %collective-permute-start.9) | collective-permute-done | bytes 786464 | tf_op jit(solution)/shard_map/ppermute | solution.py:41
  68.4 10.8 collective-permute-done.19
  79.3 49.7 %collective-permute-done.20 = bf16[768,512]{1,0:T(8,128)(2,1)S(1)} collective-permute-done((bf16[768,512]{1,0:T(8,128)(2,1)S(1)}, bf16[768,512]{1,0:T(8,128)(2,1)S(1)}, u32[]{:S(2)}, u32[]{:S(2)}) %collective-permute-start.20) | collective-permute-done | bytes 786464 | tf_op jit(solution)/shard_map/ppermute | solution.py:41
  138.0 6.7 maximum_select_fusion.2
  151.3 52.9 %collective-permute-done.22 = bf16[4,768,512]{2,1,0:T(8,128)(2,1)} collective-permute-done((bf16[4,768,512]{2,1,0:T(8,128)(2,1)}, bf16[4,768,512]{2,1,0:T(8,128)(2,1)}, u32[]{:S(2)}, u32[]{:S(2)}) %collective-permute-start.22) | collective-permute-done | bytes 3145760 | tf_op jit(solution)/shard_map/ppermute | solution.py:36
  204.2 6.6 maximum_select_fusion.3
  217.2 10.4 broadcast_select_fusion
  227.6 9.3 copy.169
  236.9 9.4 copy.184
  256.1 50.2 %collective-permute-start.3 = (f32[2,2,2,448]{3,0,2,1:T(2,128)S(1)}, f32[2,2,2,448]{3,0,2,1:T(2,128)S(1)}, u32[]{:S(2)}, u32[]{:S(2)}) collective-permute-start(f32[2,2,2,448]{3,0,2,1:T(2,128)S(1)} %maximum_select_fusion.16), channel_id=1, source_target_pairs={{0,8},{4,12},{8,16},{12,20},{16,24},{20,28},{24,0},{28,4},{1,9},{5... | collective-permute-start | bytes 43016 | tf_op jit(solution)/shard_map/ppermute | solution.py:41
  321.5 9.4 copy.170
  330.9 9.2 copy.185
  340.1 22.2 %maximum_select_fusion = (bf16[2,8,768,512]{2,1,3,0:T(8,128)(2,1)S(1)}, bf16[2,8,768,512]{2,1,3,0:T(8,128)(2,1)}) fusion(bf16[1,8,768,512]{2,1,3,0:T(8,128)(2,1)} %bitcast.29, bf16[1,8,768,512]{2,1,3,0:T(8,128)(2,1)} %copy.170, pred[]{:T(512)S(6)} %eq.47, bf16[1,8,768,512]{2,1,3,0:T(8,128)(2,1)} %copy.185, bf16[1,8,768,512]{2,1,3,0:T(8,128)(2,1)} %bitcast.54), kind=kLoop, calls=%fused_computation.129 | loop fusion | flops 37748736 | bytes 50331648 | tf_op jit(solution)/shard_map/jit(_where)/select_n | solution.py:45
  369.0 7.7 copy.172
  376.8 9.1 reshape_reshape.12
  420.4 46.8 %while.48 = (s32[]{:T(128)}, bf16[4,1408,64]{1,2,0:T(8,128)(2,1)S(1)}, f32[4,1408]{1,0:T(4,128)S(1)}, bf16[4,3,1408,64]{3,2,1,0:T(8,128)(2,1)}, s32[]{:T(128)}, /*index=5*/s32[]{:T(128)}, s32[]{}, s32[]{}) while((s32[]{:T(128)}, bf16[4,1408,64]{1,2,0:T(8,128)(2,1)S(1)}, f32[4,1408]{1,0:T(4,128)S(1)}, ...), condition=%wide.region_5.7_spmd.clone, body=%wide.region_2.6_spmd.clone.sunk | while | flops 523394432 | bytes 57036948 | solution.py:111
  482.7 18.0 %collective-permute-done.15 = bf16[352,1024]{1,0:T(8,128)(2,1)S(1)} collective-permute-done((bf16[352,1024]{1,0:T(8,128)(2,1)S(1)}, bf16[352,1024]{1,0:T(8,128)(2,1)S(1)}, u32[]{:S(2)}, u32[]{:S(2)}) %collective-permute-start.15) | collective-permute-done | bytes 720928 | tf_op jit(solution)/shard_map/ppermute | solution.py:31
  508.2 7.5 copy.182
  515.7 7.6 reshape_reshape.13
  527.2 17.9 %multiply_convert_fusion.3 = (bf16[704,2048]{1,0:T(8,128)(2,1)S(1)}, f32[704,2048]{1,0:T(8,128)}, f32[704,2048]{1,0:T(8,128)}) fusion(f32[2048]{0:T(1024)S(1)} %dynamic_slice.188, bf16[1024,2048]{1,0:T(8,128)(2,1)S(1)} %copy-done.48, bf16[352,1024]{1,0:T(8,128)(2,1)} %collective-permute-done.16, bf16[352,1024]{1,0:T(8,128)(2,1)S(1)} %add_convert_fusion.7), kind=kOutput, calls=%fused_computation.168 | convolution fusion | flops 3050831872 | bytes 20062208 | tf_op jit(solution)/shard_map/dot_general | solution.py:25
  550.0 16.0 collective-permute-done.17
  572.9 7.7 copy.187
  580.6 9.1 reshape_reshape.14
  601.8 8.1 constant_dynamic-slice_fusion.22
  629.2 46.7 %while.49 = (s32[]{:T(128)}, bf16[4,1408,64]{1,2,0:T(8,128)(2,1)S(1)}, f32[4,1408]{1,0:T(4,128)S(1)}, bf16[4,3,1408,64]{3,2,1,0:T(8,128)(2,1)}, s32[]{:T(128)}, /*index=5*/s32[]{:T(128)}, s32[]{}, s32[]{}) while((s32[]{:T(128)}, bf16[4,1408,64]{1,2,0:T(8,128)(2,1)S(1)}, f32[4,1408]{1,0:T(4,128)S(1)}, ...), condition=%wide.region_13.15_spmd.clone, body=%wide.region_10.14_spmd.clone.sunk | while | flops 523394432 | bytes 57036948 | solution.py:111
  698.7 17.3 %collective-permute-done.26 = bf16[352,1024]{1,0:T(8,128)(2,1)S(1)} collective-permute-done((bf16[352,1024]{1,0:T(8,128)(2,1)S(1)}, bf16[352,1024]{1,0:T(8,128)(2,1)S(1)}, u32[]{:S(2)}, u32[]{:S(2)}) %collective-permute-start.26) | collective-permute-done | bytes 720928 | tf_op jit(solution)/shard_map/ppermute | solution.py:31
  726.5 7.5 copy.197
  734.0 7.6 reshape_reshape.15
  745.5 17.4 %multiply_convert_fusion.2 = (bf16[704,2048]{1,0:T(8,128)(2,1)S(1)}, f32[704,2048]{1,0:T(8,128)S(1)}, f32[704,2048]{1,0:T(8,128)}) fusion(f32[2048]{0:T(1024)S(1)} %dynamic_slice.193, bf16[1024,2048]{1,0:T(8,128)(2,1)S(1)} %copy-done.51, bf16[352,1024]{1,0:T(8,128)(2,1)} %collective-permute-done.27, bf16[352,1024]{1,0:T(8,128)(2,1)S(1)} %add_convert_fusion.5), kind=kOutput, calls=%fused_computation.155 | convolution fusion | flops 3050831872 | bytes 20062208 | tf_op jit(solution)/shard_map/dot_general | solution.py:25
  762.9 8.8 convert_reduce_fusion
  780.4 13.7 collective-permute-done.32
  794.1 13.0 collective-permute-done.28
  814.1 15.2 collective-permute-done.33
  836.0 121.4 %while.50 = (s32[]{:T(128)}, bf16[4,3,1408,64]{2,3,1,0:T(8,128)(2,1)}, bf16[4,3,1408,64]{3,2,1,0:T(8,128)(2,1)}, f32[4,1408]{1,0:T(4,128)S(1)}, bf16[4,1408,64]{...) while((s32[]{:T(128)}, bf16[4,3,1408,64]{2,3,1,0:T(8,128)(2,1)}, ...), condition=%wide.region_20.22_spmd.clone, body=%wide.region_18.21_spmd.clone.sunk | while | flops 1288625536 | bytes 124578064 | solution.py:129
  841.9 8.9 multiply_reduce_fusion.20
  872.2 8.9 multiply_reduce_fusion.20
  902.5 8.9 multiply_reduce_fusion.20
  932.8 8.9 multiply_reduce_fusion.20
  966.6 7.0 constant_dynamic-slice_fusion.14
  991.3 17.6 %collective-permute-done.36 = bf16[352,1024]{1,0:T(8,128)(2,1)S(1)} collective-permute-done((bf16[352,1024]{1,0:T(8,128)(2,1)S(1)}, bf16[352,1024]{1,0:T(8,128)(2,1)S(1)}, u32[]{:S(2)}, u32[]{:S(2)}) %collective-permute-start.36) | collective-permute-done | bytes 720928 | tf_op jit(solution)/shard_map/ppermute | solution.py:31
  1013.0 16.8 collective-permute-done.37
  1029.8 11.3 convert_reduce_fusion.1
  1052.9 7.6 reshape.1068
  1060.5 7.6 convolution_convert_fusion
  1068.2 8.0 reshape.1069
  1103.3 7.5 reshape.1066
  1138.0 123.9 %while.51 = (s32[]{:T(128)}, bf16[4,3,1408,64]{2,3,1,0:T(8,128)(2,1)}, bf16[4,3,1408,64]{3,2,1,0:T(8,128)(2,1)}, f32[4,1408]{1,0:T(4,128)}, bf16[4,1408,64]{1,2,...) while((s32[]{:T(128)}, bf16[4,3,1408,64]{2,3,1,0:T(8,128)(2,1)}, ...), condition=%wide.region_27.29_spmd.clone, body=%wide.region_25.28_spmd.clone.sunk | while | flops 1288625536 | bytes 124578064 | solution.py:129
  1144.3 8.8 multiply_reduce_fusion.21
  1175.3 8.8 multiply_reduce_fusion.21
  1206.2 8.8 multiply_reduce_fusion.21
  1237.2 8.8 multiply_reduce_fusion.21
  1271.1 7.1 constant_dynamic-slice_fusion.10
  1284.7 7.5 convolution_convert_fusion.3
  1292.2 7.7 reshape.1063
  1299.9 6.9 convolution_convert_fusion.2
  1306.8 8.0 reshape.1064
  1340.3 7.5 reshape.1061
  1383.5 16.7 collective-permute-done.42
  1443.7 113.3 %collective-permute-done.56 = f32[4,2,448]{2,1,0:T(2,128)S(1)} collective-permute-done((f32[4,2,448]{2,1,0:T(2,128)S(1)}, f32[4,2,448]{2,1,0:T(2,128)S(1)}, u32[]{:S(2)}, u32[]{:S(2)}) %collective-permute-start.56) | collective-permute-done | bytes 14368 | tf_op jit(solution)/shard_map/ppermute | solution.py:36
  1579.0 10.0 collective-permute-done.51
  1589.1 33.7 %collective-permute-done.52 = bf16[768,512]{1,0:T(8,128)(2,1)S(1)} collective-permute-done((bf16[768,512]{1,0:T(8,128)(2,1)S(1)}, bf16[768,512]{1,0:T(8,128)(2,1)S(1)}, u32[]{:S(2)}, u32[]{:S(2)}) %collective-permute-start.52) | collective-permute-done | bytes 786464 | tf_op jit(solution)/shard_map/ppermute | solution.py:41
  1630.0 9.7 collective-permute-done.46
  1639.7 47.4 %collective-permute-done.47 = bf16[768,512]{1,0:T(8,128)(2,1)} collective-permute-done((bf16[768,512]{1,0:T(8,128)(2,1)}, bf16[768,512]{1,0:T(8,128)(2,1)}, u32[]{:S(2)}, u32[]{:S(2)}) %collective-permute-start.47) | collective-permute-done | bytes 786464 | tf_op jit(solution)/shard_map/ppermute | solution.py:41
  (965 shorter events, 767.7 us)
Async XLA Ops:
  4.9 23.8 %collective-permute-start.8 = (bf16[768,512]{1,0:T(8,128)(2,1)}, bf16[768,512]{1,0:T(8,128)(2,1)S(1)}, u32[]{:S(2)}, u32[]{:S(2)}) collective-permute-start(bf16[768,512]{1,0:T(8,128)(2,1)} %get-tuple-element.427), channel_id=1, source_target_pairs={{0,8},{4,12},{8,16},{12,20},{16,24},{20,28},{24,0},{28,4},{1,9},{5... | collective-permute-start | bytes 2359304 | tf_op jit(solution)/shard_map/ppermute | solution.py:41
  7.9 54.5 %collective-permute-start.9 = (bf16[768,512]{1,0:T(8,128)(2,1)}, bf16[768,512]{1,0:T(8,128)(2,1)S(1)}, u32[]{:S(2)}, u32[]{:S(2)}) collective-permute-start(bf16[768,512]{1,0:T(8,128)(2,1)} %get-tuple-element.427), channel_id=1, source_target_pairs={{0,16},{4,20},{8,24},{12,28},{16,0},{20,4},{24,8},{28,12},{1,17},{... | collective-permute-start | bytes 2359304 | tf_op jit(solution)/shard_map/ppermute | solution.py:41
  10.5 51.9 %collective-permute-start.10 = (bf16[768,512]{1,0:T(8,128)(2,1)}, bf16[768,512]{1,0:T(8,128)(2,1)S(1)}, u32[]{:S(2)}, u32[]{:S(2)}) collective-permute-start(bf16[768,512]{1,0:T(8,128)(2,1)} %get-tuple-element.427), channel_id=1, source_target_pairs={{0,24},{4,28},{8,0},{12,4},{16,8},{20,12},{24,16},{28,20},{1,25},{... | collective-permute-start | bytes 2359304 | tf_op jit(solution)/shard_map/ppermute | solution.py:41
  13.4 65.8 %collective-permute-start.19 = (bf16[768,512]{1,0:T(8,128)(2,1)S(1)}, bf16[768,512]{1,0:T(8,128)(2,1)S(1)}, u32[]{:S(2)}, u32[]{:S(2)}) collective-permute-start(bf16[768,512]{1,0:T(8,128)(2,1)S(1)} %get-tuple-element.423), channel_id=1, source_target_pairs={{0,8},{4,12},{8,16},{12,20},{16,24},{20,28},{24,0},{28,4},{1,9},{5... | collective-permute-start | bytes 2359304 | tf_op jit(solution)/shard_map/ppermute | solution.py:41
  14.1 114.8 %collective-permute-start.20 = (bf16[768,512]{1,0:T(8,128)(2,1)S(1)}, bf16[768,512]{1,0:T(8,128)(2,1)S(1)}, u32[]{:S(2)}, u32[]{:S(2)}) collective-permute-start(bf16[768,512]{1,0:T(8,128)(2,1)S(1)} %get-tuple-element.423), channel_id=1, source_target_pairs={{0,16},{4,20},{8,24},{12,28},{16,0},{20,4},{24,8},{28,12},{1,17},{... | collective-permute-start | bytes 2359304 | tf_op jit(solution)/shard_map/ppermute | solution.py:41
  28.7 100.3 %collective-permute-start.21 = (bf16[768,512]{1,0:T(8,128)(2,1)S(1)}, bf16[768,512]{1,0:T(8,128)(2,1)S(1)}, u32[]{:S(2)}, u32[]{:S(2)}) collective-permute-start(bf16[768,512]{1,0:T(8,128)(2,1)S(1)} %get-tuple-element.423), channel_id=1, source_target_pairs={{0,24},{4,28},{8,0},{12,4},{16,8},{20,12},{24,16},{28,20},{1,25},{... | collective-permute-start | bytes 2359304 | tf_op jit(solution)/shard_map/ppermute | solution.py:41
  66.7 71.3 %collective-permute-start.11 = (bf16[4,768,512]{2,1,0:T(8,128)(2,1)}, bf16[4,768,512]{2,1,0:T(8,128)(2,1)}, u32[]{:S(2)}, u32[]{:S(2)}) collective-permute-start(bf16[4,768,512]{2,1,0:T(8,128)(2,1)} %get-tuple-element.401), channel_id=1, source_target_pairs={{0,4},{4,0},{8,12},{12,8},{16,20},{20,16},{24,28},{28,24},{1,5},{5... | collective-permute-start | bytes 9437192 | tf_op jit(solution)/shard_map/ppermute | solution.py:36
  131.9 72.3 %collective-permute-start.22 = (bf16[4,768,512]{2,1,0:T(8,128)(2,1)}, bf16[4,768,512]{2,1,0:T(8,128)(2,1)}, u32[]{:S(2)}, u32[]{:S(2)}) collective-permute-start(bf16[4,768,512]{2,1,0:T(8,128)(2,1)} %get-tuple-element.399), channel_id=1, source_target_pairs={{0,4},{4,0},{8,12},{12,8},{16,20},{20,16},{24,28},{28,24},{1,5},{5... | collective-permute-start | bytes 9437192 | tf_op jit(solution)/shard_map/ppermute | solution.py:36
  236.9 103.3 %collective-permute-start.12 = (bf16[8,768,512]{1,0,2:T(8,128)(2,1)}, bf16[8,768,512]{1,0,2:T(8,128)(2,1)}, u32[]{:S(2)}, u32[]{:S(2)}) collective-permute-start(bf16[8,768,512]{1,0,2:T(8,128)(2,1)} %copy.169), channel_id=1, source_target_pairs={{0,1},{1,0},{2,3},{3,2},{4,5},{5,4},{6,7},{7,6},{8,9},{9,8},{10,11... | collective-permute-start | bytes 18874376 | tf_op jit(solution)/shard_map/ppermute | solution.py:31
  246.3 93.8 %collective-permute-start.23 = (bf16[8,768,512]{1,0,2:T(8,128)(2,1)}, bf16[8,768,512]{1,0,2:T(8,128)(2,1)}, u32[]{:S(2)}, u32[]{:S(2)}) collective-permute-start(bf16[8,768,512]{1,0,2:T(8,128)(2,1)} %copy.184), channel_id=1, source_target_pairs={{0,1},{1,0},{2,3},{3,2},{4,5},{5,4},{6,7},{7,6},{8,9},{9,8},{10,11... | collective-permute-start | bytes 18874376 | tf_op jit(solution)/shard_map/ppermute | solution.py:31
  246.8 5.6 collective-permute-start.1
  246.9 253.8 %copy-start.23 = (bf16[352,512]{1,0:T(8,128)(2,1)}, bf16[352,512]{1,0:T(8,128)(2,1)S(1)}, u32[]{:S(2)}) copy-start(bf16[352,512]{1,0:T(8,128)(2,1)S(1)} %get-tuple-element.437) | copy-start | bytes 1081348
  252.4 3.7 collective-permute-start.2
  256.1 52.6 %collective-permute-start.3 = (f32[2,2,2,448]{3,0,2,1:T(2,128)S(1)}, f32[2,2,2,448]{3,0,2,1:T(2,128)S(1)}, u32[]{:S(2)}, u32[]{:S(2)}) collective-permute-start(f32[2,2,2,448]{3,0,2,1:T(2,128)S(1)} %maximum_select_fusion.16), channel_id=1, source_target_pairs={{0,8},{4,12},{8,16},{12,20},{16,24},{20,28},{24,0},{28,4},{1,9},{5... | collective-permute-start | bytes 43016 | tf_op jit(solution)/shard_map/ppermute | solution.py:41
  306.3 4.6 collective-permute-start.4
  306.3 4.6 collective-permute-start.5
  308.8 10.3 collective-permute-start
  311.0 4.3 collective-permute-start.6
  319.1 181.6 %copy-start.28 = (bf16[352,512]{1,0:T(8,128)(2,1)}, bf16[352,512]{1,0:T(8,128)(2,1)S(1)}, u32[]{:S(2)}) copy-start(bf16[352,512]{1,0:T(8,128)(2,1)S(1)} %collective-permute-done) | copy-start | bytes 1081348
  319.9 66.0 %copy-start.98 = (bf16[352,1024]{1,0:T(8,128)(2,1)}, bf16[352,1024]{1,0:T(8,128)(2,1)S(1)}, u32[]{:S(2)}) copy-start(bf16[352,1024]{1,0:T(8,128)(2,1)S(1)} %fusion.126) | copy-start | bytes 2162692
  319.9 66.0 %collective-permute-start.7 = (bf16[352,1024]{1,0:T(8,128)(2,1)S(1)}, bf16[352,1024]{1,0:T(8,128)(2,1)S(1)}, u32[]{:S(2)}, u32[]{:S(2)}) collective-permute-start(bf16[352,1024]{1,0:T(8,128)(2,1)S(1)} %fusion.126), channel_id=1, source_target_pairs={{0,2},{2,0},{1,3},{3,1},{4,6},{6,4},{5,7},{7,5},{8,10},{10,8},{9,1... | collective-permute-start | bytes 2162696 | tf_op jit(solution)/shard_map/ppermute | solution.py:31
  404.4 5.3 collective-permute-start.13
  471.9 6.9 collective-permute-start.14
  482.1 18.6 %collective-permute-start.15 = (bf16[352,1024]{1,0:T(8,128)(2,1)S(1)}, bf16[352,1024]{1,0:T(8,128)(2,1)S(1)}, u32[]{:S(2)}, u32[]{:S(2)}) collective-permute-start(bf16[352,1024]{1,0:T(8,128)(2,1)S(1)} %slice.539), channel_id=1, source_target_pairs={{0,2},{2,0},{1,3},{3,1},{4,6},{6,4},{5,7},{7,5},{8,10},{10,8},{9,1... | collective-permute-start | bytes 2162696 | tf_op jit(solution)/shard_map/ppermute | solution.py:31
  501.7 25.4 %collective-permute-start.16 = (bf16[352,1024]{1,0:T(8,128)(2,1)S(1)}, bf16[352,1024]{1,0:T(8,128)(2,1)}, u32[]{:S(2)}, u32[]{:S(2)}) collective-permute-start(bf16[352,1024]{1,0:T(8,128)(2,1)S(1)} %add_convert_fusion.7), channel_id=1, source_target_pairs={{0,2},{2,0},{1,3},{3,1},{4,6},{6,4},{5,7},{7,5},{8,10},{10,8},{9,1... | collective-permute-start | bytes 2162696 | tf_op jit(solution)/shard_map/ppermute | solution.py:31
  548.4 17.6 %collective-permute-start.17 = (bf16[352,1024]{1,0:T(8,128)(2,1)S(1)}, bf16[352,1024]{1,0:T(8,128)(2,1)S(1)}, u32[]{:S(2)}, u32[]{:S(2)}) collective-permute-start(bf16[352,1024]{1,0:T(8,128)(2,1)S(1)} %slice.538), channel_id=1, source_target_pairs={{0,2},{2,0},{1,3},{3,1},{4,6},{6,4},{5,7},{7,5},{8,10},{10,8},{9,1... | collective-permute-start | bytes 2162696 | tf_op jit(solution)/shard_map/ppermute | solution.py:31
  566.5 149.4 %copy-start.9 = (f32[352,1024]{1,0:T(8,128)}, f32[352,1024]{1,0:T(8,128)S(1)}, u32[]{:S(2)}) copy-start(f32[352,1024]{1,0:T(8,128)S(1)} %get-tuple-element.374) | copy-start | bytes 4325380
  566.9 22.8 %collective-permute-start.18 = (bf16[352,1024]{1,0:T(8,128)(2,1)S(1)}, bf16[352,1024]{1,0:T(8,128)(2,1)}, u32[]{:S(2)}, u32[]{:S(2)}) collective-permute-start(bf16[352,1024]{1,0:T(8,128)(2,1)S(1)} %add_convert_fusion.6), channel_id=1, source_target_pairs={{0,2},{2,0},{1,3},{3,1},{4,6},{6,4},{5,7},{7,5},{8,10},{10,8},{9,1... | collective-permute-start | bytes 2162696 | tf_op jit(solution)/shard_map/ppermute | solution.py:31
  611.1 5.4 collective-permute-start.24
  684.6 9.9 collective-permute-start.25
  697.8 18.1 %collective-permute-start.26 = (bf16[352,1024]{1,0:T(8,128)(2,1)S(1)}, bf16[352,1024]{1,0:T(8,128)(2,1)S(1)}, u32[]{:S(2)}, u32[]{:S(2)}) collective-permute-start(bf16[352,1024]{1,0:T(8,128)(2,1)S(1)} %slice.537), channel_id=1, source_target_pairs={{0,2},{2,0},{1,3},{3,1},{4,6},{6,4},{5,7},{7,5},{8,10},{10,8},{9,1... | collective-permute-start | bytes 2162696 | tf_op jit(solution)/shard_map/ppermute | solution.py:31
  698.6 18.9 %collective-permute-start.30 = (bf16[352,512]{1,0:T(8,128)(2,1)S(1)}, bf16[352,512]{1,0:T(8,128)(2,1)S(1)}, u32[]{:S(2)}, u32[]{:S(2)}) collective-permute-start(bf16[352,512]{1,0:T(8,128)(2,1)S(1)} %get-tuple-element.432), channel_id=1, source_target_pairs={{0,1},{1,0},{2,3},{3,2},{4,5},{5,4},{6,7},{7,6},{8,9},{9,8},{10,11... | collective-permute-start | bytes 1081352 | tf_op jit(solution)/shard_map/ppermute | solution.py:31
  716.9 28.6 %collective-permute-start.27 = (bf16[352,1024]{1,0:T(8,128)(2,1)S(1)}, bf16[352,1024]{1,0:T(8,128)(2,1)}, u32[]{:S(2)}, u32[]{:S(2)}) collective-permute-start(bf16[352,1024]{1,0:T(8,128)(2,1)S(1)} %add_convert_fusion.5), channel_id=1, source_target_pairs={{0,2},{2,0},{1,3},{3,1},{4,6},{6,4},{5,7},{7,5},{8,10},{10,8},{9,1... | collective-permute-start | bytes 2162696 | tf_op jit(solution)/shard_map/ppermute | solution.py:31
  719.1 43.8 %collective-permute-start.31 = (bf16[352,1024]{1,0:T(8,128)(2,1)S(1)}, bf16[352,1024]{1,0:T(8,128)(2,1)}, u32[]{:S(2)}, u32[]{:S(2)}) collective-permute-start(bf16[352,1024]{1,0:T(8,128)(2,1)S(1)} %get-tuple-element.346), channel_id=1, source_target_pairs={{0,2},{2,0},{1,3},{3,1},{4,6},{6,4},{5,7},{7,5},{8,10},{10,8},{9,1... | collective-permute-start | bytes 2162696 | tf_op jit(solution)/shard_map/ppermute | solution.py:31
  775.0 19.1 %collective-permute-start.32 = (bf16[352,1024]{1,0:T(8,128)(2,1)S(1)}, bf16[352,1024]{1,0:T(8,128)(2,1)S(1)}, u32[]{:S(2)}, u32[]{:S(2)}) collective-permute-start(bf16[352,1024]{1,0:T(8,128)(2,1)S(1)} %slice.535), channel_id=1, source_target_pairs={{0,2},{2,0},{1,3},{3,1},{4,6},{6,4},{5,7},{7,5},{8,10},{10,8},{9,1... | collective-permute-start | bytes 2162696 | tf_op jit(solution)/shard_map/ppermute | solution.py:31
  778.9 28.3 %collective-permute-start.28 = (bf16[352,1024]{1,0:T(8,128)(2,1)S(1)}, bf16[352,1024]{1,0:T(8,128)(2,1)S(1)}, u32[]{:S(2)}, u32[]{:S(2)}) collective-permute-start(bf16[352,1024]{1,0:T(8,128)(2,1)S(1)} %slice.536), channel_id=1, source_target_pairs={{0,2},{2,0},{1,3},{3,1},{4,6},{6,4},{5,7},{7,5},{8,10},{10,8},{9,1... | collective-permute-start | bytes 2162696 | tf_op jit(solution)/shard_map/ppermute | solution.py:31
  813.6 15.7 collective-permute-start.33
  832.0 1.7 collective-permute-start.34
  980.1 3.0 collective-permute-start.35
  990.7 18.3 %collective-permute-start.36 = (bf16[352,1024]{1,0:T(8,128)(2,1)S(1)}, bf16[352,1024]{1,0:T(8,128)(2,1)S(1)}, u32[]{:S(2)}, u32[]{:S(2)}) collective-permute-start(bf16[352,1024]{1,0:T(8,128)(2,1)S(1)} %slice.534), channel_id=1, source_target_pairs={{0,2},{2,0},{1,3},{3,1},{4,6},{6,4},{5,7},{7,5},{8,10},{10,8},{9,1... | collective-permute-start | bytes 2162696 | tf_op jit(solution)/shard_map/ppermute | solution.py:31
  1012.5 17.4 %collective-permute-start.37 = (bf16[352,1024]{1,0:T(8,128)(2,1)S(1)}, bf16[352,1024]{1,0:T(8,128)(2,1)S(1)}, u32[]{:S(2)}, u32[]{:S(2)}) collective-permute-start(bf16[352,1024]{1,0:T(8,128)(2,1)S(1)} %get-tuple-element.354), channel_id=1, source_target_pairs={{0,2},{2,0},{1,3},{3,1},{4,6},{6,4},{5,7},{7,5},{8,10},{10,8},{9,1... | collective-permute-start | bytes 2162696 | tf_op jit(solution)/shard_map/ppermute | solution.py:31
  1046.1 35.3 %collective-permute-start.38 = (bf16[352,1024]{1,0:T(8,128)(2,1)S(1)}, bf16[352,1024]{1,0:T(8,128)(2,1)S(1)}, u32[]{:S(2)}, u32[]{:S(2)}) collective-permute-start(bf16[352,1024]{1,0:T(8,128)(2,1)S(1)} %slice.533), channel_id=1, source_target_pairs={{0,2},{2,0},{1,3},{3,1},{4,6},{6,4},{5,7},{7,5},{8,10},{10,8},{9,1... | collective-permute-start | bytes 2162696 | tf_op jit(solution)/shard_map/ppermute | solution.py:31
  1087.6 23.2 %collective-permute-start.39 = (bf16[352,1024]{1,0:T(8,128)(2,1)}, bf16[352,1024]{1,0:T(8,128)(2,1)}, u32[]{:S(2)}, u32[]{:S(2)}) collective-permute-start(bf16[352,1024]{1,0:T(8,128)(2,1)} %get-tuple-element.358), channel_id=1, source_target_pairs={{0,2},{2,0},{1,3},{3,1},{4,6},{6,4},{5,7},{7,5},{8,10},{10,8},{9,1... | collective-permute-start | bytes 2162696 | tf_op jit(solution)/shard_map/ppermute | solution.py:31
  1121.0 13.7 collective-permute-start.40
  1133.5 275.7 %collective-permute-start.49 = (bf16[8,768,512]{2,1,0:T(8,128)(2,1)}, bf16[8,768,512]{2,1,0:T(8,128)(2,1)}, u32[]{:S(2)}, u32[]{:S(2)}) collective-permute-start(bf16[8,768,512]{2,1,0:T(8,128)(2,1)} %dynamic-slice_bitcast_fusion.28), channel_id=1, source_target_pairs={{0,1},{1,0},{2,3},{3,2},{4,5},{5,4},{6,7},{7,6},{8,9},{9,8},{10,11... | collective-permute-start | bytes 18874376 | tf_op jit(solution)/shard_map/ppermute | solution.py:31
  1284.7 44.3 %collective-permute-start.41 = (bf16[704,3,256]{2,0,1:T(8,128)(2,1)}, bf16[704,3,256]{2,0,1:T(8,128)(2,1)}, u32[]{:S(2)}, u32[]{:S(2)}) collective-permute-start(bf16[704,3,256]{2,0,1:T(8,128)(2,1)} %bitcast.90), channel_id=1, source_target_pairs={{0,1},{1,0},{2,3},{3,2},{4,5},{5,4},{6,7},{7,6},{8,9},{9,8},{10,11... | collective-permute-start | bytes 3244040 | tf_op jit(solution)/shard_map/ppermute | solution.py:31
  1360.2 63.0 %collective-permute-start.44 = (bf16[8,768,512]{2,1,0:T(8,128)(2,1)}, bf16[8,768,512]{2,1,0:T(8,128)(2,1)}, u32[]{:S(2)}, u32[]{:S(2)}) collective-permute-start(bf16[8,768,512]{2,1,0:T(8,128)(2,1)} %dynamic-slice_bitcast_fusion.29), channel_id=1, source_target_pairs={{0,1},{1,0},{2,3},{3,2},{4,5},{5,4},{6,7},{7,6},{8,9},{9,8},{10,11... | collective-permute-start | bytes 18874376 | tf_op jit(solution)/shard_map/ppermute | solution.py:31
  1363.7 7.3 collective-permute-start.29
  1381.4 18.8 %collective-permute-start.42 = (bf16[352,1024]{1,0:T(8,128)(2,1)}, bf16[352,1024]{1,0:T(8,128)(2,1)}, u32[]{:S(2)}, u32[]{:S(2)}) collective-permute-start(bf16[352,1024]{1,0:T(8,128)(2,1)} %slice.532), channel_id=1, source_target_pairs={{0,2},{2,0},{1,3},{3,1},{4,6},{6,4},{5,7},{7,5},{8,10},{10,8},{9,1... | collective-permute-start | bytes 2162696 | tf_op jit(solution)/shard_map/ppermute | solution.py:31
  1419.5 141.6 %collective-permute-start.50 = (bf16[4,768,512]{2,1,0:T(8,128)(2,1)}, bf16[4,768,512]{2,1,0:T(8,128)(2,1)}, u32[]{:S(2)}, u32[]{:S(2)}) collective-permute-start(bf16[4,768,512]{2,1,0:T(8,128)(2,1)} %dynamic-slice_bitcast_fusion.30), channel_id=1, source_target_pairs={{0,4},{4,0},{8,12},{12,8},{16,20},{20,16},{24,28},{28,24},{1,5},{5... | collective-permute-start | bytes 9437192 | tf_op jit(solution)/shard_map/ppermute | solution.py:36
  1434.5 138.2 %collective-permute-start.45 = (bf16[4,768,512]{2,1,0:T(8,128)(2,1)}, bf16[4,768,512]{2,1,0:T(8,128)(2,1)}, u32[]{:S(2)}, u32[]{:S(2)}) collective-permute-start(bf16[4,768,512]{2,1,0:T(8,128)(2,1)} %dynamic-slice_bitcast_fusion.31), channel_id=1, source_target_pairs={{0,4},{4,0},{8,12},{12,8},{16,20},{20,16},{24,28},{28,24},{1,5},{5... | collective-permute-start | bytes 9437192 | tf_op jit(solution)/shard_map/ppermute | solution.py:36
  1435.2 1.3 collective-permute-start.54
  1436.7 4.0 collective-permute-start.55
  1440.7 116.3 %collective-permute-start.56 = (f32[4,2,448]{2,1,0:T(2,128)S(1)}, f32[4,2,448]{2,1,0:T(2,128)S(1)}, u32[]{:S(2)}, u32[]{:S(2)}) collective-permute-start(f32[4,2,448]{2,1,0:T(2,128)S(1)} %dynamic-slice_bitcast_fusion.42), channel_id=1, source_target_pairs={{0,4},{4,0},{8,12},{12,8},{16,20},{20,16},{24,28},{28,24},{1,5},{5... | collective-permute-start | bytes 43016 | tf_op jit(solution)/shard_map/ppermute | solution.py:36
  1443.6 127.9 %collective-permute-start.43 = (f32[352,512]{1,0:T(8,128)S(1)}, f32[352,512]{1,0:T(8,128)S(1)}, u32[]{:S(2)}, u32[]{:S(2)}) collective-permute-start(f32[352,512]{1,0:T(8,128)S(1)} %bitcast.565), channel_id=1, source_target_pairs={{0,1},{1,0},{2,3},{3,2},{4,5},{5,4},{6,7},{7,6},{8,9},{9,8},{10,11... | collective-permute-start | bytes 2162696 | tf_op jit(solution)/shard_map/ppermute | solution.py:31
  1557.1 9.5 collective-permute-start.57
  1557.9 9.6 collective-permute-start.58
  1561.1 6.4 collective-permute-start.59
  1566.6 22.4 %collective-permute-start.51 = (bf16[768,512]{1,0:T(8,128)(2,1)S(1)}, bf16[768,512]{1,0:T(8,128)(2,1)S(1)}, u32[]{:S(2)}, u32[]{:S(2)}) collective-permute-start(bf16[768,512]{1,0:T(8,128)(2,1)S(1)} %get-tuple-element.392), channel_id=1, source_target_pairs={{0,8},{4,12},{8,16},{12,20},{16,24},{20,28},{24,0},{28,4},{1,9},{5... | collective-permute-start | bytes 2359304 | tf_op jit(solution)/shard_map/ppermute | solution.py:41
  1567.5 55.3 %collective-permute-start.52 = (bf16[768,512]{1,0:T(8,128)(2,1)S(1)}, bf16[768,512]{1,0:T(8,128)(2,1)S(1)}, u32[]{:S(2)}, u32[]{:S(2)}) collective-permute-start(bf16[768,512]{1,0:T(8,128)(2,1)S(1)} %get-tuple-element.394), channel_id=1, source_target_pairs={{0,16},{4,20},{8,24},{12,28},{16,0},{20,4},{24,8},{28,12},{1,17},{... | collective-permute-start | bytes 2359304 | tf_op jit(solution)/shard_map/ppermute | solution.py:41
  1567.5 55.3 %collective-permute-start.53 = (bf16[768,512]{1,0:T(8,128)(2,1)S(1)}, bf16[768,512]{1,0:T(8,128)(2,1)S(1)}, u32[]{:S(2)}, u32[]{:S(2)}) collective-permute-start(bf16[768,512]{1,0:T(8,128)(2,1)S(1)} %get-tuple-element.393), channel_id=1, source_target_pairs={{0,24},{4,28},{8,0},{12,4},{16,8},{20,12},{24,16},{28,20},{1,25},{... | collective-permute-start | bytes 2359304 | tf_op jit(solution)/shard_map/ppermute | solution.py:41
  1577.0 62.7 %collective-permute-start.46 = (bf16[768,512]{1,0:T(8,128)(2,1)}, bf16[768,512]{1,0:T(8,128)(2,1)}, u32[]{:S(2)}, u32[]{:S(2)}) collective-permute-start(bf16[768,512]{1,0:T(8,128)(2,1)} %get-tuple-element.395), channel_id=1, source_target_pairs={{0,8},{4,12},{8,16},{12,20},{16,24},{20,28},{24,0},{28,4},{1,9},{5... | collective-permute-start | bytes 2359304 | tf_op jit(solution)/shard_map/ppermute | solution.py:41
  1577.6 109.5 %collective-permute-start.47 = (bf16[768,512]{1,0:T(8,128)(2,1)}, bf16[768,512]{1,0:T(8,128)(2,1)}, u32[]{:S(2)}, u32[]{:S(2)}) collective-permute-start(bf16[768,512]{1,0:T(8,128)(2,1)} %get-tuple-element.397), channel_id=1, source_target_pairs={{0,16},{4,20},{8,24},{12,28},{16,0},{20,4},{24,8},{28,12},{1,17},{... | collective-permute-start | bytes 2359304 | tf_op jit(solution)/shard_map/ppermute | solution.py:41
  1589.0 98.1 %collective-permute-start.48 = (bf16[768,512]{1,0:T(8,128)(2,1)}, bf16[768,512]{1,0:T(8,128)(2,1)}, u32[]{:S(2)}, u32[]{:S(2)}) collective-permute-start(bf16[768,512]{1,0:T(8,128)(2,1)} %get-tuple-element.396), channel_id=1, source_target_pairs={{0,24},{4,28},{8,0},{12,4},{16,8},{20,12},{24,16},{28,20},{1,25},{... | collective-permute-start | bytes 2359304 | tf_op jit(solution)/shard_map/ppermute | solution.py:41
  (222 other events, 2089.7 us)

commit v2 on v1

--- a/solution.py
+++ b/solution.py
@@ -1,6 +1,10 @@
+import functools
+
 import jax
 import jax.numpy as jnp
 from jax import lax
+from jax.experimental import pallas as pl
+from jax.experimental.pallas import tpu as pltpu
 from jax.sharding import PartitionSpec as P
 
 D = 1024
@@ -141,6 +145,653 @@
 
 
 MARKS = [0, D, 2 * D, 3 * D, 4 * D, 5 * D, 6 * D, 7 * D, 8 * D, 8 * D + FF, 9 * D + FF, 10 * D + FF]
+
+
+MESH = pl.DeviceIdType.MESH
+KINDS = 4
+GROUPS = LAYERS * KINDS
+SPLIT = 2
+ANY = pl.BlockSpec(memory_space=pl.ANY)
+WHOLE = pl.BlockSpec(memory_space=pltpu.VMEM)
+
+
+def nt(left, right):
+    return contract(left, right, (1,), (1,))
+
+
+def nn(left, right):
+    return contract(left, right, (1,), (0,))
+
+
+def tn(left, right):
+    return contract(left, right, (0,), (0,))
+
+
+class Place:
+    def __init__(self, count):
+        self.count = count
+        self.line = count // 2
+        self.dp = lax.axis_index("dp")
+        self.row = lax.axis_index("row")
+        self.col = lax.axis_index("col")
+        self.pair = lax.rem(self.dp, 2)
+        self.outer = lax.div(self.dp, 2)
+        self.x_dp = self.dp + 1 - 2 * self.pair
+        self.x_peer = (self.x_dp, self.row, self.col)
+        self.y_peer = (self.dp, 1 - self.row, self.col)
+        self.c_peer = (self.dp, self.row, 1 - self.col)
+
+    def ahead(self, step):
+        return lax.rem(self.dp + 2 * step, self.count)
+
+    def behind(self, step):
+        return lax.rem(self.dp + self.count - 2 * step, self.count)
+
+    def z_peer(self, step):
+        return (self.ahead(step), self.row, self.col)
+
+    def greet(self):
+        barrier = pltpu.get_barrier_semaphore()
+        peers = [self.z_peer(step) for step in range(1, self.line)]
+        peers += [self.x_peer, self.y_peer, self.c_peer]
+        for peer in peers:
+            pl.semaphore_signal(barrier, inc=1, device_id=peer, device_id_type=MESH)
+        pl.semaphore_wait(barrier, len(peers))
+
+
+def remote(source, target, send, recv, peer):
+    return pltpu.make_async_remote_copy(
+        source, target, send, recv, device_id=peer, device_id_type=MESH
+    )
+
+
+def aligned(value, by=128):
+    return pl.multiple_of(value, by)
+
+
+def weight_view(kind, ref, layer, place, dp, col):
+    if kind in (0, 2):
+        size = ref.shape[1] // (2 * place.count)
+        return ref.at[layer, pl.ds(aligned((col * place.count + dp) * size, 16), size), :]
+    size = ref.shape[1] // place.count
+    return ref.at[
+        layer,
+        pl.ds(aligned(dp * size, 16), size),
+        pl.ds(aligned(col * (D // 2)), D // 2),
+    ]
+
+
+def column_view(kind, ref, layer, col):
+    if kind in (0, 2):
+        return ref.at[layer, pl.ds(aligned(col * (D // 2), 16), D // 2), :]
+    return ref.at[layer, :, pl.ds(aligned(col * (D // 2)), D // 2)]
+
+
+class Gather:
+    def __init__(self, place, shards, wholes, send, recv, own):
+        self.place, self.shards, self.wholes = place, shards, wholes
+        self.send, self.recv, self.own = send, recv, own
+
+    def line_copy(self, group, step):
+        layer, kind = divmod(group, KINDS)
+        place = self.place
+        return remote(
+            self.shards[kind].at[layer],
+            weight_view(kind, self.wholes[kind], layer, place, place.dp, place.col),
+            self.send.at[group, step - 1],
+            self.recv.at[group, step - 1],
+            place.z_peer(step),
+        )
+
+    def pair_copy(self, group, step):
+        layer, kind = divmod(group, KINDS)
+        place = self.place
+        view = weight_view(kind, self.wholes[kind], layer, place, place.behind(step), place.col)
+        at = place.line - 1 + step
+        return remote(
+            self.shards[kind].at[layer] if step == 0 else view,
+            view,
+            self.send.at[group, at],
+            self.recv.at[group, at],
+            place.x_peer,
+        )
+
+    def core_copy(self, group):
+        layer, kind = divmod(group, KINDS)
+        place = self.place
+        view = column_view(kind, self.wholes[kind], layer, place.col)
+        at = 2 * place.line - 1
+        return remote(
+            view, view, self.send.at[group, at], self.recv.at[group, at], place.c_peer
+        )
+
+    def own_copy(self, group):
+        layer, kind = divmod(group, KINDS)
+        place = self.place
+        return pltpu.make_async_copy(
+            self.shards[kind].at[layer],
+            weight_view(kind, self.wholes[kind], layer, place, place.dp, place.col),
+            self.own.at[group],
+        )
+
+    def start(self, group):
+        for step in range(1, self.place.line):
+            self.line_copy(group, step).start()
+        self.pair_copy(group, 0).start()
+        self.own_copy(group).start()
+
+    def to_pair(self, group):
+        for step in range(1, self.place.line):
+            self.line_copy(group, step).wait_recv()
+            self.pair_copy(group, step).start()
+
+    def to_core(self, group):
+        self.own_copy(group).wait()
+        for step in range(self.place.line):
+            self.pair_copy(group, step).wait_recv()
+        self.core_copy(group).start()
+
+    def arrive(self, group):
+        self.core_copy(group).wait_recv()
+
+    def finish(self):
+        for group in range(GROUPS):
+            for step in range(1, self.place.line):
+                self.line_copy(group, step).wait_send()
+            for step in range(self.place.line):
+                self.pair_copy(group, step).wait_send()
+            self.core_copy(group).wait_send()
+
+
+def gather_vectors(place, spot, spare, raw, vecs, send, recv):
+    for at, peer in enumerate((place.c_peer, place.y_peer, place.x_peer)):
+        copy = remote(spot, spare.at[at], send.at[at], recv.at[at], peer)
+        copy.start()
+        copy.wait()
+        spot[...] = spot[...] + spare[at]
+    copies = []
+    for step in range(1, place.line):
+        copy = remote(
+            spot, raw.at[place.outer], send.at[2 + step], recv.at[2 + step], place.z_peer(step)
+        )
+        copy.start()
+        copies.append(copy)
+    raw[place.outer] = spot[...]
+    for copy in copies:
+        copy.wait()
+    used = vecs.shape[1] // 128 // place.line
+    for outer in range(place.line):
+        for layer in range(LAYERS):
+            for at in range(used):
+                start = (outer * used + at) * 128
+                vecs[layer : layer + 1, start : start + 128] = raw[outer, layer, at : at + 1, :]
+
+
+def norm_rows(source, gain, shift, unit, inverse, target, rows):
+    size = 32
+
+    def step(at, carry):
+        place = pl.ds(aligned(at * size, size), size)
+        values = source[place, :].astype(f32)
+        centre = jnp.sum(values, 1, keepdims=True) * (1.0 / D)
+        spread = jnp.sum(values * values, 1, keepdims=True) * (1.0 / D) - centre * centre
+        scale = lax.rsqrt(spread + norm_epsilon)
+        norm = (values - centre) * scale
+        unit[place, :] = norm
+        inverse[place, :] = jnp.broadcast_to(scale, (size, 128))
+        target[place, :] = (norm * gain + shift).astype(bf16)
+        return carry
+
+    lax.fori_loop(0, rows // size, step, 0)
+
+
+def gelu_both(values):
+    normal = 0.5 + 0.5 * lax.erf(values * (0.5**0.5))
+    density = jnp.exp(-0.5 * values * values) * 0.3989422804014327
+    return values * normal, normal + values * density
+
+
+def forward_kernel(count, tokens, *refs):
+    (
+        state_in,
+        spot_in,
+        bias_in,
+        shard_a,
+        shard_b,
+        shard_c,
+        shard_d,
+        w_a,
+        w_b,
+        w_c,
+        w_d,
+        vecs_out,
+        unit_one_out,
+        inv_one_out,
+        normed_out,
+        heads_out,
+        lse_out,
+        mixed_out,
+        branch_out,
+        unit_two_out,
+        inv_two_out,
+        normed_two_out,
+        active_out,
+        slope_out,
+        output_out,
+        block_out,
+        state,
+        spot,
+        spare,
+        raw,
+        vecs,
+        wq,
+        wm,
+        wu,
+        wd,
+        unit,
+        inverse,
+        unit_two,
+        inverse_two,
+        normed,
+        normed_two,
+        heads_all,
+        head_tx,
+        head_mix,
+        lse,
+        mixed_all,
+        branch,
+        output,
+        active,
+        slope,
+        tx,
+        rx,
+        part,
+        g_send,
+        g_recv,
+        g_own,
+        v_send,
+        v_recv,
+        y_send,
+        y_recv,
+        c_send,
+        c_recv,
+        stage_sem,
+        save_sem,
+    ) = refs
+    rows = state_in.shape[0]
+    group = 2 * rows
+    half = D // 2
+    width = half // 2
+    place = Place(count)
+    row, col = place.row, place.col
+    wholes = (w_a, w_b, w_c, w_d)
+    gather = Gather(place, (shard_a, shard_b, shard_c, shard_d), wholes, g_send, g_recv, g_own)
+    place.greet()
+    gather.start(0)
+    gather.start(1)
+
+    pending = {}
+
+    def save(name, at, source, target):
+        settle(name)
+        copy = pltpu.make_async_copy(source, target, save_sem.at[at])
+        copy.start()
+        pending[name] = copy
+
+    def settle(*names):
+        for name in names:
+            if name in pending:
+                pending.pop(name).wait()
+
+    staged = {}
+
+    def stage(kind, layer):
+        gather.arrive(layer * KINDS + kind)
+        buffer = (wq, wm, wu, wd)[kind]
+        copy = pltpu.make_async_copy(wholes[kind].at[layer], buffer, stage_sem.at[kind])
+        copy.start()
+        staged[kind] = copy
+
+    def ready(kind):
+        staged.pop(kind).wait()
+
+    y_at = [0]
+
+    def y_copy(source, target):
+        at = y_at[0]
+        y_at[0] += 1
+        return remote(source, target, y_send.at[at], y_recv.at[at], place.y_peer)
+
+    chunk = rows // SPLIT
+
+    def exchange_rows(buffer):
+        copies = []
+        for at in range(SPLIT):
+            copies.append(
+                y_copy(
+                    buffer.at[pl.ds(at * chunk, chunk), :],
+                    buffer.at[pl.ds(rows + at * chunk, chunk), :],
+                )
+            )
+            copies[-1].start()
+        return copies
+
+    spot[...] = spot_in[...]
+    state[...] = state_in[...].astype(f32)
+    gather_vectors(place, spot, spare, raw, vecs, v_send, v_recv)
+    save("vecs", 11, vecs, vecs_out)
+    gather.to_pair(0)
+    gather.start(2)
+
+    plan = {
+        (0, "norm"): ((gather.to_core, 0), (stage, 0, 0), (gather.to_pair, 1), (gather.start, 3)),
+        (0, "triple"): ((gather.to_core, 1),),
+        (0, "attend"): ((gather.to_pair, 2), (stage, 1, 0), (gather.start, 4)),
+        (0, "project"): ((gather.to_core, 2),),
+        (0, "branch"): ((gather.to_pair, 3), (gather.start, 5), (stage, 2, 0)),
+        (0, "expand"): ((gather.to_core, 3), (gather.start, 6)),
+        (0, "shrink"): ((gather.to_pair, 4),),
+        (0, "output"): ((gather.to_core, 4), (stage, 0, 1), (gather.to_pair, 5), (gather.start, 7)),
+        (1, "norm"): ((gather.to_core, 5),),
+        (1, "triple"): ((stage, 1, 1), (gather.to_pair, 6)),
+        (1, "attend"): ((gather.to_core, 6),),
+        (1, "project"): ((gather.to_pair, 7),),
+        (1, "branch"): ((stage, 2, 1),),
+        (1, "expand"): ((gather.to_core, 7),),
+    }
+
+    lane = lax.broadcasted_iota(jnp.int32, (1, 128), 1) < HEAD_DIM
+    valid = lax.broadcasted_iota(jnp.int32, (rows, 1), 0) < tokens - col * rows
+
+    def vector(layer, at):
+        return vecs[layer : layer + 1, at * D : (at + 1) * D]
+
+    for layer in range(LAYERS):
+
+        def pump(name, layer=layer):
+            for action, *args in plan.get((layer, name), ()):
+                action(*args)
+
+        settle("unit", "inverse", "normed")
+        norm_rows(state, vector(layer, 0), vector(layer, 1), unit, inverse, normed, rows)
+        copies = exchange_rows(normed)
+        save("unit", 0, unit, unit_one_out.at[layer])
+        save("inverse", 1, inverse, inv_one_out.at[layer])
+        pump("norm")
+        ready(0)
+        heads, mixed = heads_all.at[layer], mixed_all.at[layer]
+
+        def triple(start):
+            def step(at, carry):
+                part_at = lax.rem(at, 3)
+                mine = lax.div(at, 3)
+                owner = jnp.where(mine == 1, col, 1 - col)
+                column = aligned(part_at * half + owner * width)
+                value = nn(normed[start : start + rows, :], wq[:, pl.ds(column, width)])
+                bias_at = aligned(
+                    jnp.where(part_at == 2, 3 * D, 2 * D) + row * half + owner * width
+                )
+                bias = vecs[layer : layer + 1, pl.ds(bias_at, width)]
+                bias = bias * jnp.where(part_at == 1, 0.0, 1.0)
+                value = jnp.where(valid, value + bias, 0.0).astype(bf16)
+                lanes = pl.ds(aligned(part_at * width), width)
+
+                @pl.when(mine == 0)
+                def _():
+                    head_tx[start : start + rows, lanes] = value
+
+                @pl.when(mine == 1)
+                def _():
+                    heads[pl.ds(aligned(col * group + start, 16), rows), lanes] = value
+
+                return carry
+
+            lax.fori_loop(0, 6, step, 0)
+
+        core_copies = []
+
+        def send_heads(start):
+            at = layer * 3 + (start > 0)
+            core_copies.append(
+                remote(
+                    head_tx.at[pl.ds(start, rows), :],
+                    heads.at[pl.ds(aligned(col * group + start, 16), rows), :],
+                    c_send.at[at],
+                    c_recv.at[at],
+                    place.c_peer,
+                )
+            )
+            core_copies[-1].start()
+
+        triple(0)
+        send_heads(0)
+        for copy in copies:
+            copy.wait()
+        save("normed", 2, normed, normed_out.at[layer])
+        triple(rows)
+        send_heads(rows)
+        pump("triple")
+        for copy in core_copies:
+            copy.wait()
+        save("heads", 3, heads, heads_out.at[layer])
+        settle("lse")
+
+        def attend(owner):
+            tile = rows // 2
+
+            def step(at, carry):
+                place_rows = pl.ds(aligned(owner * group + at * tile, 16), tile)
+                for pair in range(width // 128):
+                    lanes = slice(pair * 128, pair * 128 + 128)
+                    query = heads[place_rows, lanes] * jnp.asarray(HEAD_DIM**-0.5, bf16)
+                    zero = jnp.zeros_like(query)
+                    both = jnp.concatenate(
+                        [jnp.where(lane, query, zero), jnp.where(lane, zero, query)], 0
+                    )
+                    key = heads[:, width + pair * 128 : width + pair * 128 + 128]
+                    value = heads[:, 2 * width + pair * 128 : 2 * width + pair * 128 + 128]
+                    scores = nt(both, key) + bias_in[...]
+                    peak = jnp.max(scores, 1, keepdims=True)
+                    weights = jnp.exp(scores - peak)
+                    total = jnp.sum(weights, 1, keepdims=True)
+                    result = nn(weights.astype(bf16), value) / total
+                    logsum = peak + jnp.log(total)
+                    head_mix[place_rows, lanes] = jnp.where(
+                        lane, result[:tile], result[tile:]
+                    ).astype(bf16)
+                    lse[place_rows, lanes] = jnp.where(lane, logsum[:tile], logsum[tile:])
+                return carry
+
+            lax.fori_loop(0, group // tile, step, 0)
+
+        attend(1 - col)
+        lanes = pl.ds(aligned(col * width), width)
+        back = remote(
+            head_mix.at[pl.ds(aligned((1 - col) * group, 16), group), :],
+            mixed.at[:, lanes],
+            c_send.at[layer * 3 + 2],
+            c_recv.at[layer * 3 + 2],
+            place.c_peer,
+        )
+        back.start()
+        pump("attend")
+        attend(col)
+        mixed[:, lanes] = head_mix[pl.ds(aligned(col * group, 16), group), :]
+        back.wait()
+        save("lse", 4, lse, lse_out.at[layer])
+        save("mixed", 5, mixed, mixed_out.at[layer])
+        ready(1)
+        pump("project")
+        settle("normed_two")
+
+        def project(start, size, target, target_at):
+            def step(at, carry):
+                lanes = pl.ds(aligned(at * half), half)
+                value = nn(mixed[start : start + size, :], wm[:, lanes])
+                target[pl.ds(target_at, size), lanes] = value.astype(target.dtype)
+                return carry
+
+            lax.fori_loop(0, 2, step, 0)
+
+        copies = []
+        for at in range(SPLIT):
+            project(rows + at * chunk, chunk, tx, at * chunk)
+            view = pl.ds(at * chunk, chunk)
+            copies.append(y_copy(tx.at[view, :], rx.at[view, :]))
+            copies[-1].start()
+        project(0, rows, part, 0)
+        pump("branch")
+        for copy in copies:
+            copy.wait()
+        settle("branch", "unit_two", "inverse_two")
+        branch[...] = part[...] + rx[...].astype(f32) + vector(layer, 4)
+        state[...] = state[...] + vector(layer, 5) * branch[...]
+        save("branch", 6, branch, branch_out.at[layer])
+        norm_rows(
+            state, vector(layer, 6), vector(layer, 7), unit_two, inverse_two, normed_two, rows
+        )
+        copies = exchange_rows(normed_two)
+        save("unit_two", 7, unit_two, unit_two_out.at[layer])
+        save("inverse_two", 8, inverse_two, inv_two_out.at[layer])
+        pump("expand")
+        ready(2)
+        settle("active", "slope")
+
+        def expand(start, size):
+            def step(at, carry):
+                lanes = pl.ds(aligned(at * half), half)
+                bias_at = aligned(8 * D + row * (FF // 2) + at * half)
+                value = nn(normed_two[start : start + size, :], wu[:, lanes])
+                value = value + vecs[layer : layer + 1, pl.ds(bias_at, half)]
+                act, grad = gelu_both(value)
+                active[start : start + size, lanes] = act.astype(bf16)
+                slope[start : start + size, lanes] = grad.astype(bf16)
+                return carry
+
+            lax.fori_loop(0, FF // 2 // half, step, 0)
+
+        def shrink(start, size, target, target_at):
+            def step(at, carry):
+                lanes = pl.ds(aligned(at * half), half)
+                value = nn(active[start : start + size, :], wd[:, lanes])
+                target[pl.ds(target_at, size), lanes] = value.astype(target.dtype)
+                return carry
+
+            lax.fori_loop(0, 2, step, 0)
+
+        expand(0, rows)
+        stage(3, layer)
+        settle("normed")
+        ready(3)
+        shrink(0, rows, part, 0)
+        pump("shrink")
+        back_copies = []
+        for at in range(SPLIT):
+            copies[at].wait()
+            start = rows + at * chunk
+            expand(start, chunk)
+            shrink(start, chunk, tx, at * chunk)
+            view = pl.ds(at * chunk, chunk)
+            back_copies.append(y_copy(tx.at[view, :], rx.at[view, :]))
+            back_copies[-1].start()
+        save("normed_two", 9, normed_two, normed_two_out.at[layer])
+        save("active", 10, active, active_out.at[layer])
+        save("slope", 12, slope, slope_out.at[layer])
+        pump("output")
+        for copy in back_copies:
+            copy.wait()
+        settle("output")
+        output[...] = part[...] + rx[...].astype(f32) + vector(layer, 12)
+        state[...] = state[...] + vector(layer, 13) * output[...]
+        save("output", 13, output, output_out.at[layer])
+    block_out[...] = state[...].astype(bf16)
+    gather.finish()
+    settle(*list(pending))
+
+
+def forward_call(mesh_count, tokens, state, spot, bias, shards):
+    rows = state.shape[0]
+    group = 2 * rows
+    half = D // 2
+    width = half // 2
+    line = mesh_count // 2
+
+    def shape(*dims, kind=f32):
+        return jax.ShapeDtypeStruct(dims, kind)
+
+    outs = [
+        shape(LAYERS, D, 3 * half, kind=bf16),
+        shape(LAYERS, half, D, kind=bf16),
+        shape(LAYERS, D, FF // 2, kind=bf16),
+        shape(LAYERS, FF // 2, D, kind=bf16),
+        shape(LAYERS, 10 * D + FF),
+        shape(LAYERS, rows, D),
+        shape(LAYERS, rows, 128),
+        shape(LAYERS, group, D, kind=bf16),
+        shape(LAYERS, 2 * group, 3 * width, kind=bf16),
+        shape(LAYERS, 2 * group, width),
+        shape(LAYERS, group, half, kind=bf16),
+        shape(LAYERS, rows, D),
+        shape(LAYERS, rows, D),
+        shape(LAYERS, rows, 128),
+        shape(LAYERS, group, D, kind=bf16),
+        shape(LAYERS, group, FF // 2, kind=bf16),
+        shape(LAYERS, group, FF // 2, kind=bf16),
+        shape(LAYERS, rows, D),
+        shape(rows, D, kind=bf16),
+    ]
+    dma = pltpu.SemaphoreType.DMA
+    scratch = [
+        pltpu.VMEM((rows, D), f32),
+        pltpu.VMEM(spot.shape, f32),
+        pltpu.VMEM((3,) + spot.shape, f32),
+        pltpu.VMEM((line,) + spot.shape, f32),
+        pltpu.VMEM((LAYERS, 10 * D + FF), f32),
+        pltpu.VMEM((D, 3 * half), bf16),
+        pltpu.VMEM((half, D), bf16),
+        pltpu.VMEM((D, FF // 2), bf16),
+        pltpu.VMEM((FF // 2, D), bf16),
+        pltpu.VMEM((rows, D), f32),
+        pltpu.VMEM((rows, 128), f32),
+        pltpu.VMEM((rows, D), f32),
+        pltpu.VMEM((rows, 128), f32),
+        pltpu.VMEM((group, D), bf16),
+        pltpu.VMEM((group, D), bf16),
+        pltpu.VMEM((LAYERS, 2 * group, 3 * width), bf16),
+        pltpu.VMEM((group, 3 * width), bf16),
+        pltpu.VMEM((2 * group, width), bf16),
+        pltpu.VMEM((2 * group, width), f32),
+        pltpu.VMEM((LAYERS, group, half), bf16),
+        pltpu.VMEM((rows, D), f32),
+        pltpu.VMEM((rows, D), f32),
+        pltpu.VMEM((group, FF // 2), bf16),
+        pltpu.VMEM((group, FF // 2), bf16),
+        pltpu.VMEM((rows, D), bf16),
+        pltpu.VMEM((rows, D), bf16),
+        pltpu.VMEM((rows, D), f32),
+        dma((GROUPS, 2 * line)),
+        dma((GROUPS, 2 * line)),
+        dma((GROUPS,)),
+        dma((line + 2,)),
+        dma((line + 2,)),
+        dma((LAYERS * 4 * SPLIT,)),
+        dma((LAYERS * 4 * SPLIT,)),
+        dma((LAYERS * 3,)),
+        dma((LAYERS * 3,)),
+        dma((KINDS,)),
+        dma((14,)),
+    ]
+    return pl.pallas_call(
+        functools.partial(forward_kernel, mesh_count, tokens),
+        out_shape=outs,
+        in_specs=[WHOLE] * 3 + [ANY] * 4,
+        out_specs=[ANY] * 18 + [WHOLE],
+        scratch_shapes=scratch,
+        compiler_params=pltpu.CompilerParams(
+            collective_id=0, has_side_effects=True, vmem_limit_bytes=60 << 20
+        ),
+        name="forward",
+    )(state, spot, bias, *shards)
 
 
 def local(
@@ -210,31 +861,19 @@
             at += size
         return parts
 
-    weights = []
-    for layer in range(LAYERS):
-        block = flat(
-            [
-                values[layer].astype(bf16)
-                for values in (triplet_master, project_master, expand_master, shrink_master)
-            ]
-        )
-        column = dp_gather(block)
-        both = ordered(column[None], swap(column, "col")[None], col_at, 0)
-        qkv, mix, up, down = unflat(both, (2, count))
-        weights.append(
-            (
-                qkv.reshape(D, 3, half),
-                mix.transpose(1, 2, 0, 3).reshape(half, D),
-                up.reshape(D, FF // 2),
-                down.transpose(1, 2, 0, 3).reshape(FF // 2, D),
-            )
-        )
-
-    spot = vectors_master
-    spot = ordered(spot[:, None], swap(spot, "col")[:, None], col_at, 1)
-    spot = ordered(spot[:, None], swap(spot, "row")[:, None], row_at, 1)
-    vectors = dp_gather(spot).transpose(1, 0, 2, 3, 4).reshape(LAYERS, -1)
-
+
+    shards = [
+        triplet_master.astype(bf16).reshape(LAYERS, -1, 3 * half),
+        project_master.astype(bf16),
+        expand_master.astype(bf16),
+        shrink_master.astype(bf16),
+    ]
+    piece = vectors_master.shape[1]
+    line_at = (lax.axis_index("dp") % 2 * 2 + row_at) * 2 + col_at
+    spot = lax.dynamic_update_slice_in_dim(
+        jnp.zeros((LAYERS, 8 * piece), f32), vectors_master, line_at * piece, 1
+    ).reshape(LAYERS, -1, 128)
+    spot = jnp.pad(spot, ((0, 0), (0, -spot.shape[1] % 8), (0, 0)))
     place = jnp.arange(2 * group) % rows
     late = jnp.arange(2 * group) // group
     valid = place + late * rows < tokens
@@ -262,54 +901,20 @@
     def pieces(vector):
         return [vector[MARKS[at] : MARKS[at + 1]] for at in range(11)]
 
-    state = to_tokens(images).astype(f32)
+    kept_all = forward_call(count, tokens, to_tokens(images), spot, bias, shards)
+    (w_a, w_b, w_c, w_d, vectors, *saved, block_rows) = kept_all
+    layer_pieces = [pieces(vectors[layer]) for layer in range(LAYERS)]
     kept = []
-    layer_pieces = []
+    weights = []
     for layer in range(LAYERS):
-        parts = pieces(vectors[layer])
-        layer_pieces.append(parts)
-        triplet_w, project_w, expand_w, shrink_w = weights[layer]
-        normed, unit_one, inverse_one = norm_forward(state, parts[0], parts[1])
-        normed_all = row_rows(normed)
-        half_start = row_at * half
-        biases = jnp.stack(
-            [
-                lax.dynamic_slice_in_dim(parts[2], half_start, half),
-                jnp.zeros((half,), f32),
-                lax.dynamic_slice_in_dim(parts[3], half_start, half),
-            ]
-        )
-        triple = (contract(normed_all, triplet_w, (1,), (0,)) + biases).astype(bf16)
-        stacked = to_heads(triple, 3)
-        results, logsum = attend_forward(stacked, bias)
-        mixed = from_heads(results.astype(bf16)[:, None])[:, 0]
-        branch = row_sum(contract(mixed, project_w, (1,), (0,))) + parts[4]
-        middle = state + parts[5] * branch
-        normed_two, unit_two, inverse_two = norm_forward(middle, parts[6], parts[7])
-        normed_two_all = row_rows(normed_two)
-        hidden_bias = lax.dynamic_slice_in_dim(parts[8], row_at * (FF // 2), FF // 2)
-        inner = contract(normed_two_all, expand_w, (1,), (0,)) + hidden_bias
-        active = gelu_value(inner).astype(bf16)
-        output = row_sum(contract(active, shrink_w, (1,), (0,))) + parts[9]
-        kept.append(
-            (
-                unit_one,
-                inverse_one,
-                normed_all,
-                stacked,
-                logsum,
-                mixed,
-                branch,
-                unit_two,
-                inverse_two,
-                normed_two_all,
-                inner,
-                active,
-                output,
-            )
-        )
-        state = middle + parts[10] * output
-    block_out = to_features(state.astype(bf16))
+        (unit_one, inverse_one, normed_all, heads_all, lse, mixed, branch, unit_two, inverse_two,
+         normed_two_all, active, slope, output) = [value[layer] for value in saved]
+        weights.append((w_a[layer].reshape(D, 3, half), w_b[layer], w_c[layer], w_d[layer]))
+        stacked = heads_all.reshape(2 * group, 3, heads, HEAD_DIM).transpose(2, 1, 0, 3)
+        logsum = lse.reshape(2 * group, heads, HEAD_DIM)[:, :, 0].T
+        kept.append((unit_one, inverse_one[:, :1], normed_all, stacked, logsum, mixed, branch, unit_two,
+            inverse_two[:, :1], normed_two_all, slope, active, output))
+    block_out = to_features(block_rows)
     grad = to_tokens(cotangent).astype(f32)
     reduced = [None] * LAYERS
     vector_grads = [None] * LAYERS
@@ -325,7 +930,7 @@
             unit_two,
             inverse_two,
             normed_two_all,
-            inner,
+            slope,
             active,
             output,
         ) = kept[layer]
@@ -337,7 +942,7 @@
         back_out_all = row_rows(back_out)
         shrink_grad = contract(active, back_out_all, (0,), (0,)).astype(bf16)
         back_active = contract(back_out_all, shrink_w, (1,), (1,))
-        back_inner = jax.vjp(gelu_value, inner)[1](back_active)[0].astype(bf16)
+        back_inner = (slope.astype(f32) * back_active).astype(bf16)
         hidden_bias_grad = jnp.sum(back_inner.astype(f32), 0)
         expand_grad = contract(normed_two_all, back_inner, (0,), (0,)).astype(bf16)
         back_two = row_sum(contract(back_inner, expand_w, (1,), (1,)))

time: 1730 us -> 1230 us (0.71)
  the two profiles are of different devices: /device:TPU:0 before, /device:TPU:9 now
where the time goes in v2:
time: 1230 us; the launch traced here: 1220 us
  waiting for transfers between devices  300 us (24%)
  local copies, waits for them, and re-layouts  255 us (21%)
  matrix products  247 us (20%)
  Pallas kernels  239 us (19%)
  other arithmetic  147 us (12%)
  starting transfers between devices  30.8 us (3%)
    pallas_call x1, Pallas kernels, forward_call(): pl.pallas_call(functools.partial(forward_kernel, mesh_count, tokens), out...  239 us
    dot_general x48, matrix products, contract(): lax.dot_general(left, right, ((left_dims, right_dims), ((), ())), preferr...  223 us
    ppermute x9, waiting for transfers between devices, shifted(): lax.ppermute(values, 'dp', [(at, (at + step) % count) for at in range(cou...  118 us
    ppermute x3, waiting for transfers between devices, pair_swap(): return lax.ppermute(values, 'dp', [(at, at ^ 1) for at in range(count)])  114 us
    ppermute x20, waiting for transfers between devices, swap(): return lax.ppermute(values, axis, [(0, 1), (1, 0)])  69.1 us
    convert_element_type x8, other arithmetic, one_head(): back_scores = (probs * (back_probs - inner)).astype(bf16)  52.4 us
    unnamed x236, local copies, waits for them, and re-layouts  33 us
    reshape x4, local copies, waits for them, and re-layouts, local(): shrink_grad.reshape(count, -1, 2, lane).transpose(2, 0, 1, 3)  26.2 us
  transfers between devices with their start and end apart: 32, of which 15 were waited for; matrix products, arithmetic and copies ran while one was open for 32% of the time, Pallas kernels for 20%

profile of v2, /device:TPU:9, one launch (start us, length us, event | category | flops | bytes accessed | tf_op | source)
XLA Modules:
  0.0 1221.9 jit_solution(485198119732118972)
XLA Ops:
  13.9 238.5 %forward.1 = (bf16[2,1024,1536]{2,1,0:T(8,128)(2,1)}, bf16[2,512,1024]{2,1,0:T(8,128)(2,1)}, bf16[2,1024,2048]{2,1,0:T(8,128)(2,1)}, bf16[2,2048,1024]{2,1,0:T(8...) custom-call(bf16[352,1024]{1,0:T(8,128)(2,1)} %maximum_select_fusion, ...), custom_call_target="tpu_custom_call" | custom-call | tf_op jit(solution)/shard_map/forward/pallas_call | solution.py:784
  255.6 14.8 %collective-permute-done.3 = bf16[352,1024]{1,0:T(8,128)(2,1)S(1)} collective-permute-done((bf16[352,1024]{1,0:T(8,128)(2,1)S(1)}, bf16[352,1024]{1,0:T(8,128)(2,1)S(1)}, u32[]{:S(2)}, u32[]{:S(2)}) %collective-permute-start.3) | collective-permute-done | bytes 720928 | tf_op jit(solution)/shard_map/ppermute | solution.py:35
  270.4 7.9 convert_reduce_fusion
  282.9 13.7 %collective-permute-done.4 = bf16[352,1024]{1,0:T(8,128)(2,1)S(1)} collective-permute-done((bf16[352,1024]{1,0:T(8,128)(2,1)S(1)}, bf16[352,1024]{1,0:T(8,128)(2,1)S(1)}, u32[]{:S(2)}, u32[]{:S(2)}) %collective-permute-start.4) | collective-permute-done | bytes 720928 | tf_op jit(solution)/shard_map/ppermute | solution.py:35
  300.3 4.6 fusion.163
  307.8 6.5 collective-permute-done.5
  323.8 4.7 collective-permute-start.6
  341.3 116.7 %while.22 = (s32[]{:T(128)}, bf16[4,3,1408,64]{2,3,1,0:T(8,128)(2,1)}, bf16[4,3,1408,64]{2,3,0,1:T(8,128)(2,1)S(1)}, f32[4,1408]{1,0:T(4,128)S(1)}, bf16[4,1408,...) while((s32[]{:T(128)}, bf16[4,3,1408,64]{2,3,1,0:T(8,128)(2,1)}, ...), condition=%wide.region_4.5_spmd.clone, body=%wide.region_2.4_spmd.clone.sunk | while | flops 1288625536 | bytes 141158768 | solution.py:133
  341.5 4.5 fusion.207
  346.1 8.8 multiply_reduce_fusion.8
  354.9 6.6 multiply_convert_fusion.10
  370.6 4.5 fusion.207
  375.2 8.8 multiply_reduce_fusion.8
  384.0 6.6 multiply_convert_fusion.10
  404.4 8.8 multiply_reduce_fusion.8
  413.1 6.6 multiply_convert_fusion.10
  428.9 4.5 fusion.207
  433.5 8.8 multiply_reduce_fusion.8
  442.3 6.6 multiply_convert_fusion.10
  461.2 6.0 reshape.453
  467.2 7.1 constant_dynamic-slice_fusion.15
  474.2 6.4 copy.143
  480.6 4.9 fusion.162
  488.5 5.7 copy.142
  505.8 15.5 %collective-permute-done.8 = bf16[352,1024]{1,0:T(8,128)(2,1)} collective-permute-done((bf16[352,1024]{1,0:T(8,128)(2,1)}, bf16[352,1024]{1,0:T(8,128)(2,1)}, u32[]{:S(2)}, u32[]{:S(2)}) %collective-permute-start.8) | collective-permute-done | bytes 720928 | tf_op jit(solution)/shard_map/ppermute | solution.py:35
  536.2 7.7 convolution_convert_fusion
  543.8 7.8 reshape.464
  551.7 5.2 copy.217
  556.8 7.2 convert_reduce_fusion.1
  571.0 5.1 convolution_convert_fusion.1
  576.1 7.7 reshape.463
  603.3 4.7 convolution_convert_fusion.4
  608.0 4.6 copy.163
  612.7 8.8 reshape.461
  633.3 6.0 pad_maximum_fusion.1
  651.5 116.2 %while.23 = (s32[]{:T(128)}, bf16[4,3,1408,64]{2,3,1,0:T(8,128)(2,1)}, bf16[4,3,1408,64]{2,3,0,1:T(8,128)(2,1)S(1)}, f32[4,1408]{1,0:T(4,128)S(1)}, bf16[4,1408,...) while((s32[]{:T(128)}, bf16[4,3,1408,64]{2,3,1,0:T(8,128)(2,1)}, ...), condition=%wide.region_11.12_spmd.clone, body=%wide.region_9.11_spmd.clone.sunk | while | flops 1288625536 | bytes 140978480 | solution.py:133
  656.1 8.8 multiply_reduce_fusion.9
  664.9 6.6 multiply_convert_fusion.11
  685.1 8.8 multiply_reduce_fusion.9
  693.9 6.6 multiply_convert_fusion.11
  714.2 8.8 multiply_reduce_fusion.9
  723.0 6.6 multiply_convert_fusion.11
  743.3 8.8 multiply_reduce_fusion.9
  752.0 6.6 multiply_convert_fusion.11
  770.9 6.2 reshape.454
  777.1 7.0 constant_dynamic-slice_fusion.11
  784.1 6.5 copy.156
  791.1 6.9 convolution_convert_fusion.3
  797.9 7.6 reshape.458
  805.5 7.5 convolution_convert_fusion.2
  813.0 8.0 reshape.459
  821.0 5.2 copy.218
  842.7 4.7 copy.160
  847.4 7.5 reshape.456
  854.9 6.0 pad_maximum_fusion
  893.8 14.9 %collective-permute-done.14 = bf16[352,1024]{1,0:T(8,128)(2,1)} collective-permute-done((bf16[352,1024]{1,0:T(8,128)(2,1)}, bf16[352,1024]{1,0:T(8,128)(2,1)}, u32[]{:S(2)}, u32[]{:S(2)}) %collective-permute-start.14) | collective-permute-done | bytes 720928 | tf_op jit(solution)/shard_map/ppermute | solution.py:35
  911.0 6.6 fusion.52
  923.1 6.6 fusion.53
  944.9 113.5 %collective-permute-done.28 = f32[4,2,448]{2,1,0:T(2,128)S(1)} collective-permute-done((f32[4,2,448]{2,1,0:T(2,128)S(1)}, f32[4,2,448]{2,1,0:T(2,128)S(1)}, u32[]{:S(2)}, u32[]{:S(2)}) %collective-permute-start.28) | collective-permute-done | bytes 14368 | tf_op jit(solution)/shard_map/ppermute | solution.py:40
  1079.0 4.9 collective-permute-done.23
  1085.4 46.8 %collective-permute-done.24 = bf16[768,512]{1,0:T(8,128)(2,1)S(1)} collective-permute-done((bf16[768,512]{1,0:T(8,128)(2,1)S(1)}, bf16[768,512]{1,0:T(8,128)(2,1)S(1)}, u32[]{:S(2)}, u32[]{:S(2)}) %collective-permute-start.24) | collective-permute-done | bytes 786464 | tf_op jit(solution)/shard_map/ppermute | solution.py:45
  1132.2 39.2 %collective-permute-done.25 = bf16[768,512]{1,0:T(8,128)(2,1)S(1)} collective-permute-done((bf16[768,512]{1,0:T(8,128)(2,1)S(1)}, bf16[768,512]{1,0:T(8,128)(2,1)S(1)}, u32[]{:S(2)}, u32[]{:S(2)}) %collective-permute-start.25) | collective-permute-done | bytes 786464 | tf_op jit(solution)/shard_map/ppermute | solution.py:45
  1182.9 16.9 %collective-permute-done.19 = bf16[768,512]{1,0:T(8,128)(2,1)} collective-permute-done((bf16[768,512]{1,0:T(8,128)(2,1)}, bf16[768,512]{1,0:T(8,128)(2,1)}, u32[]{:S(2)}, u32[]{:S(2)}) %collective-permute-start.19) | collective-permute-done | bytes 786464 | tf_op jit(solution)/shard_map/ppermute | solution.py:45
  1199.8 5.5 collective-permute-done.20
  (630 shorter events, 353.5 us)
Async XLA Ops:
  2.8 8.9 collective-permute-start
  4.3 249.5 %collective-permute-start.2 = (bf16[352,512]{1,0:T(8,128)(2,1)}, bf16[352,512]{1,0:T(8,128)(2,1)S(1)}, u32[]{:S(2)}, u32[]{:S(2)}) collective-permute-start(bf16[352,512]{1,0:T(8,128)(2,1)} %get-tuple-element.309), channel_id=1, source_target_pairs={{0,1},{1,0},{2,3},{3,2},{4,5},{5,4},{6,7},{7,6},{8,9},{9,8},{10,11... | collective-permute-start | bytes 1081352 | tf_op jit(solution)/shard_map/ppermute | solution.py:35
  253.9 43.8 %copy-start.38 = (bf16[352,512]{1,0:T(8,128)(2,1)}, bf16[352,512]{1,0:T(8,128)(2,1)S(1)}, u32[]{:S(2)}) copy-start(bf16[352,512]{1,0:T(8,128)(2,1)S(1)} %collective-permute-done.2) | copy-start | bytes 1081348
  253.9 24.5 %slice-start.7 = ((s8[8388608]{0:T(1024)(128)(4,1)}), s8[4194304]{0:T(1024)(128)(4,1)S(1)}, s32[]{:S(2)}) async-start(s8[8388608]{0:T(1024)(128)(4,1)} %bitcast.527), calls=%async_computation.7 | async-start | bytes 8388608
  254.8 23.6 %copy-start.64 = (bf16[352,1024]{1,0:T(8,128)(2,1)}, bf16[352,1024]{1,0:T(8,128)(2,1)S(1)}, u32[]{:S(2)}) copy-start(bf16[352,1024]{1,0:T(8,128)(2,1)S(1)} %get-tuple-element.257) | copy-start | bytes 2162692
  254.8 15.7 %collective-permute-start.3 = (bf16[352,1024]{1,0:T(8,128)(2,1)S(1)}, bf16[352,1024]{1,0:T(8,128)(2,1)S(1)}, u32[]{:S(2)}, u32[]{:S(2)}) collective-permute-start(bf16[352,1024]{1,0:T(8,128)(2,1)S(1)} %get-tuple-element.257), channel_id=1, source_target_pairs={{0,2},{2,0},{1,3},{3,1},{4,6},{6,4},{5,7},{7,5},{8,10},{10,8},{9,1... | collective-permute-start | bytes 2162696 | tf_op jit(solution)/shard_map/ppermute | solution.py:35
  278.4 18.1 %copy-start.21 = (f32[2,352,1024]{2,1,0:T(8,128)S(1)}, f32[2,352,1024]{2,1,0:T(8,128)}, u32[]{:S(2)}) copy-start(f32[2,352,1024]{2,1,0:T(8,128)} %get-tuple-element.106) | copy-start | bytes 8650756
  281.7 14.8 %collective-permute-start.4 = (bf16[352,1024]{1,0:T(8,128)(2,1)S(1)}, bf16[352,1024]{1,0:T(8,128)(2,1)S(1)}, u32[]{:S(2)}, u32[]{:S(2)}) collective-permute-start(bf16[352,1024]{1,0:T(8,128)(2,1)S(1)} %slice.507), channel_id=1, source_target_pairs={{0,2},{2,0},{1,3},{3,1},{4,6},{6,4},{5,7},{7,5},{8,10},{10,8},{9,1... | collective-permute-start | bytes 2162696 | tf_op jit(solution)/shard_map/ppermute | solution.py:35
  300.3 14.1 %collective-permute-start.5 = (bf16[352,1024]{1,0:T(8,128)(2,1)}, bf16[352,1024]{1,0:T(8,128)(2,1)S(1)}, u32[]{:S(2)}, u32[]{:S(2)}) collective-permute-start(bf16[352,1024]{1,0:T(8,128)(2,1)} %get-tuple-element.259), channel_id=1, source_target_pairs={{0,2},{2,0},{1,3},{3,1},{4,6},{6,4},{5,7},{7,5},{8,10},{10,8},{9,1... | collective-permute-start | bytes 2162696 | tf_op jit(solution)/shard_map/ppermute | solution.py:35
  323.8 12.2 %collective-permute-start.6 = (bf16[704,1,256]{2,0,1:T(8,128)(2,1)}, bf16[704,1,256]{2,0,1:T(8,128)(2,1)}, u32[]{:S(2)}, u32[]{:S(2)}) collective-permute-start(bf16[704,1,256]{2,0,1:T(8,128)(2,1)} %bitcast.416), channel_id=1, source_target_pairs={{0,1},{1,0},{2,3},{3,2},{4,5},{5,4},{6,7},{7,6},{8,9},{9,8},{10,11... | collective-permute-start | bytes 1081352 | tf_op jit(solution)/shard_map/ppermute | solution.py:35
  346.0 8.9 slice-start
  346.1 8.8 slice-start.1
  375.2 8.9 slice-start
  375.2 8.8 slice-start.1
  404.3 8.9 slice-start
  433.4 8.9 slice-start
  480.6 13.6 %collective-permute-start.7 = (bf16[704,3,256]{2,0,1:T(8,128)(2,1)}, bf16[704,3,256]{2,0,1:T(8,128)(2,1)}, u32[]{:S(2)}, u32[]{:S(2)}) collective-permute-start(bf16[704,3,256]{2,0,1:T(8,128)(2,1)} %bitcast.29), channel_id=1, source_target_pairs={{0,1},{1,0},{2,3},{3,2},{4,5},{5,4},{6,7},{7,6},{8,9},{9,8},{10,11... | collective-permute-start | bytes 3244040 | tf_op jit(solution)/shard_map/ppermute | solution.py:35
  498.8 22.5 %copy-start.18 = (f32[2,352,1024]{2,1,0:T(8,128)S(1)}, f32[2,352,1024]{2,1,0:T(8,128)}, u32[]{:S(2)}) copy-start(f32[2,352,1024]{2,1,0:T(8,128)} %get-tuple-element.113) | copy-start | bytes 8650756
  503.8 17.5 %collective-permute-start.8 = (bf16[352,1024]{1,0:T(8,128)(2,1)}, bf16[352,1024]{1,0:T(8,128)(2,1)}, u32[]{:S(2)}, u32[]{:S(2)}) collective-permute-start(bf16[352,1024]{1,0:T(8,128)(2,1)} %slice.506), channel_id=1, source_target_pairs={{0,2},{2,0},{1,3},{3,1},{4,6},{6,4},{5,7},{7,5},{8,10},{10,8},{9,1... | collective-permute-start | bytes 2162696 | tf_op jit(solution)/shard_map/ppermute | solution.py:35
  503.8 20.3 %copy-start.14 = (f32[352,1024]{1,0:T(8,128)S(1)}, f32[352,1024]{1,0:T(8,128)}, u32[]{:S(2)}) copy-start(f32[352,1024]{1,0:T(8,128)} %get-tuple-element.260) | copy-start | bytes 4325380
  503.8 20.3 %copy-start.32 = (f32[704,1024]{1,0:T(8,128)S(1)}, f32[704,1024]{1,0:T(8,128)}, u32[]{:S(2)}) copy-start(f32[704,1024]{1,0:T(8,128)} %copy-done.31) | copy-start | bytes 8650756
  528.5 28.3 %copy-start.60 = (bf16[352,1024]{1,0:T(8,128)(2,1)}, bf16[352,1024]{1,0:T(8,128)(2,1)S(1)}, u32[]{:S(2)}) copy-start(bf16[352,1024]{1,0:T(8,128)(2,1)S(1)} %get-tuple-element.263) | copy-start | bytes 2162692
  528.5 28.3 %collective-permute-start.9 = (bf16[352,1024]{1,0:T(8,128)(2,1)S(1)}, bf16[352,1024]{1,0:T(8,128)(2,1)}, u32[]{:S(2)}, u32[]{:S(2)}) collective-permute-start(bf16[352,1024]{1,0:T(8,128)(2,1)S(1)} %get-tuple-element.263), channel_id=1, source_target_pairs={{0,2},{2,0},{1,3},{3,1},{4,6},{6,4},{5,7},{7,5},{8,10},{10,8},{9,1... | collective-permute-start | bytes 2162696 | tf_op jit(solution)/shard_map/ppermute | solution.py:35
  551.7 12.4 %slice-start.9 = ((s8[8388608]{0:T(1024)(128)(4,1)}), s8[4194304]{0:T(1024)(128)(4,1)S(1)}, s32[]{:S(2)}) async-start(s8[8388608]{0:T(1024)(128)(4,1)} %bitcast.529), calls=%async_computation.9 | async-start | bytes 8388608
  569.8 16.5 %collective-permute-start.10 = (bf16[352,1024]{1,0:T(8,128)(2,1)}, bf16[352,1024]{1,0:T(8,128)(2,1)S(1)}, u32[]{:S(2)}, u32[]{:S(2)}) collective-permute-start(bf16[352,1024]{1,0:T(8,128)(2,1)} %slice.505), channel_id=1, source_target_pairs={{0,2},{2,0},{1,3},{3,1},{4,6},{6,4},{5,7},{7,5},{8,10},{10,8},{9,1... | collective-permute-start | bytes 2162696 | tf_op jit(solution)/shard_map/ppermute | solution.py:35
  576.1 10.2 copy-start.74
  596.2 25.3 %collective-permute-start.11 = (bf16[352,1024]{1,0:T(8,128)(2,1)}, bf16[352,1024]{1,0:T(8,128)(2,1)}, u32[]{:S(2)}, u32[]{:S(2)}) collective-permute-start(bf16[352,1024]{1,0:T(8,128)(2,1)} %get-tuple-element.266), channel_id=1, source_target_pairs={{0,2},{2,0},{1,3},{3,1},{4,6},{6,4},{5,7},{7,5},{8,10},{10,8},{9,1... | collective-permute-start | bytes 2162696 | tf_op jit(solution)/shard_map/ppermute | solution.py:35
  630.5 16.0 %collective-permute-start.12 = (bf16[704,1,256]{2,0,1:T(8,128)(2,1)}, bf16[704,1,256]{2,0,1:T(8,128)(2,1)}, u32[]{:S(2)}, u32[]{:S(2)}) collective-permute-start(bf16[704,1,256]{2,0,1:T(8,128)(2,1)} %bitcast.415), channel_id=1, source_target_pairs={{0,1},{1,0},{2,3},{3,2},{4,5},{5,4},{6,7},{7,6},{8,9},{9,8},{10,11... | collective-permute-start | bytes 1081352 | tf_op jit(solution)/shard_map/ppermute | solution.py:35
  645.7 265.3 %collective-permute-start.21 = (bf16[8,768,512]{2,1,0:T(8,128)(2,1)}, bf16[8,768,512]{2,1,0:T(8,128)(2,1)}, u32[]{:S(2)}, u32[]{:S(2)}) collective-permute-start(bf16[8,768,512]{2,1,0:T(8,128)(2,1)} %dynamic-slice_bitcast_fusion.16), channel_id=1, source_target_pairs={{0,1},{1,0},{2,3},{3,2},{4,5},{5,4},{6,7},{7,6},{8,9},{9,8},{10,11... | collective-permute-start | bytes 18874376 | tf_op jit(solution)/shard_map/ppermute | solution.py:35
  656.0 8.9 slice-start.2
  656.1 8.8 slice-start.3
  685.0 8.9 slice-start.2
  685.1 8.8 slice-start.3
  714.1 8.9 slice-start.2
  714.2 8.8 slice-start.3
  743.2 8.9 slice-start.2
  790.6 44.6 %collective-permute-start.13 = (bf16[704,3,256]{2,0,1:T(8,128)(2,1)}, bf16[704,3,256]{2,0,1:T(8,128)(2,1)}, u32[]{:S(2)}, u32[]{:S(2)}) collective-permute-start(bf16[704,3,256]{2,0,1:T(8,128)(2,1)} %bitcast.56), channel_id=1, source_target_pairs={{0,1},{1,0},{2,3},{3,2},{4,5},{5,4},{6,7},{7,6},{8,9},{9,8},{10,11... | collective-permute-start | bytes 3244040 | tf_op jit(solution)/shard_map/ppermute | solution.py:35
  867.3 55.8 %collective-permute-start.16 = (bf16[8,768,512]{2,1,0:T(8,128)(2,1)}, bf16[8,768,512]{2,1,0:T(8,128)(2,1)}, u32[]{:S(2)}, u32[]{:S(2)}) collective-permute-start(bf16[8,768,512]{2,1,0:T(8,128)(2,1)} %dynamic-slice_bitcast_fusion.17), channel_id=1, source_target_pairs={{0,1},{1,0},{2,3},{3,2},{4,5},{5,4},{6,7},{7,6},{8,9},{9,8},{10,11... | collective-permute-start | bytes 18874376 | tf_op jit(solution)/shard_map/ppermute | solution.py:35
  873.3 5.0 collective-permute-start.1
  889.9 18.8 %copy-start.19 = (f32[2,352,1024]{2,1,0:T(8,128)S(1)}, f32[2,352,1024]{2,1,0:T(8,128)}, u32[]{:S(2)}) copy-start(f32[2,352,1024]{2,1,0:T(8,128)} %get-tuple-element.113) | copy-start | bytes 8650756
  889.9 18.8 %copy-start.73 = (f32[1,1024]{1,0:T(1,128)S(1)}, f32[1,1024]{1,0:T(1,128)}, u32[]{:S(2)}) copy-start(f32[1,1024]{1,0:T(1,128)} %get-tuple-element.321) | copy-start | bytes 12292
  890.8 17.9 %collective-permute-start.14 = (bf16[352,1024]{1,0:T(8,128)(2,1)}, bf16[352,1024]{1,0:T(8,128)(2,1)}, u32[]{:S(2)}, u32[]{:S(2)}) collective-permute-start(bf16[352,1024]{1,0:T(8,128)(2,1)} %slice.504), channel_id=1, source_target_pairs={{0,2},{2,0},{1,3},{3,1},{4,6},{6,4},{5,7},{7,5},{8,10},{10,8},{9,1... | collective-permute-start | bytes 2162696 | tf_op jit(solution)/shard_map/ppermute | solution.py:35
  893.1 17.8 %copy-start.88 = (f32[1024]{0:T(1024)S(1)}, f32[1024]{0:T(1024)}, u32[]{:S(2)}) copy-start(f32[1024]{0:T(1024)} %get-tuple-element.265) | copy-start | bytes 12292
  893.1 17.8 %copy-start.85 = (f32[1024]{0:T(1024)S(1)}, f32[1024]{0:T(1024)}, u32[]{:S(2)}) copy-start(f32[1024]{0:T(1024)} %get-tuple-element.228) | copy-start | bytes 12292
  893.2 17.8 %copy-start.84 = (f32[1024]{0:T(1024)S(1)}, f32[1024]{0:T(1024)}, u32[]{:S(2)}) copy-start(f32[1024]{0:T(1024)} %get-tuple-element.213) | copy-start | bytes 12292
  893.2 17.8 %copy-start.83 = (f32[1024]{0:T(1024)S(1)}, f32[1024]{0:T(1024)}, u32[]{:S(2)}) copy-start(f32[1024]{0:T(1024)} %get-tuple-element.223) | copy-start | bytes 12292
  893.2 17.8 %copy-start.81 = (f32[1024]{0:T(1024)S(1)}, f32[1024]{0:T(1024)}, u32[]{:S(2)}) copy-start(f32[1024]{0:T(1024)} %get-tuple-element.262) | copy-start | bytes 12292
  921.2 139.6 %collective-permute-start.22 = (bf16[4,768,512]{2,1,0:T(8,128)(2,1)}, bf16[4,768,512]{2,1,0:T(8,128)(2,1)}, u32[]{:S(2)}, u32[]{:S(2)}) collective-permute-start(bf16[4,768,512]{2,1,0:T(8,128)(2,1)} %dynamic-slice_bitcast_fusion.18), channel_id=1, source_target_pairs={{0,4},{4,0},{8,12},{12,8},{16,20},{20,16},{24,28},{28,24},{1,5},{5... | collective-permute-start | bytes 9437192 | tf_op jit(solution)/shard_map/ppermute | solution.py:40
  934.4 136.8 %collective-permute-start.17 = (bf16[4,768,512]{2,1,0:T(8,128)(2,1)}, bf16[4,768,512]{2,1,0:T(8,128)(2,1)}, u32[]{:S(2)}, u32[]{:S(2)}) collective-permute-start(bf16[4,768,512]{2,1,0:T(8,128)(2,1)} %dynamic-slice_bitcast_fusion.19), channel_id=1, source_target_pairs={{0,4},{4,0},{8,12},{12,8},{16,20},{20,16},{24,28},{28,24},{1,5},{5... | collective-permute-start | bytes 9437192 | tf_op jit(solution)/shard_map/ppermute | solution.py:40
  934.6 2.3 collective-permute-start.26
  937.0 3.7 collective-permute-start.27
  940.8 117.7 %collective-permute-start.28 = (f32[4,2,448]{2,1,0:T(2,128)S(1)}, f32[4,2,448]{2,1,0:T(2,128)S(1)}, u32[]{:S(2)}, u32[]{:S(2)}) collective-permute-start(f32[4,2,448]{2,1,0:T(2,128)S(1)} %dynamic-slice_bitcast_fusion.30), channel_id=1, source_target_pairs={{0,4},{4,0},{8,12},{12,8},{16,20},{20,16},{24,28},{28,24},{1,5},{5... | collective-permute-start | bytes 43016 | tf_op jit(solution)/shard_map/ppermute | solution.py:40
  943.9 126.1 %collective-permute-start.15 = (f32[352,512]{1,0:T(8,128)S(1)}, f32[352,512]{1,0:T(8,128)S(1)}, u32[]{:S(2)}, u32[]{:S(2)}) collective-permute-start(f32[352,512]{1,0:T(8,128)S(1)} %bitcast.508), channel_id=1, source_target_pairs={{0,1},{1,0},{2,3},{3,2},{4,5},{5,4},{6,7},{7,6},{8,9},{9,8},{10,11... | collective-permute-start | bytes 2162696 | tf_op jit(solution)/shard_map/ppermute | solution.py:35
  1058.5 8.2 collective-permute-start.29
  1059.1 7.8 collective-permute-start.30
  1060.8 10.4 slice-start.4
  1060.8 10.4 slice-start.5
  1060.8 8.2 collective-permute-start.31
  1066.7 17.2 %collective-permute-start.23 = (bf16[768,512]{1,0:T(8,128)(2,1)S(1)}, bf16[768,512]{1,0:T(8,128)(2,1)S(1)}, u32[]{:S(2)}, u32[]{:S(2)}) collective-permute-start(bf16[768,512]{1,0:T(8,128)(2,1)S(1)} %get-tuple-element.287), channel_id=1, source_target_pairs={{0,8},{4,12},{8,16},{12,20},{16,24},{20,28},{24,0},{28,4},{1,9},{5... | collective-permute-start | bytes 2359304 | tf_op jit(solution)/shard_map/ppermute | solution.py:45
  1066.9 65.3 %collective-permute-start.24 = (bf16[768,512]{1,0:T(8,128)(2,1)S(1)}, bf16[768,512]{1,0:T(8,128)(2,1)S(1)}, u32[]{:S(2)}, u32[]{:S(2)}) collective-permute-start(bf16[768,512]{1,0:T(8,128)(2,1)S(1)} %get-tuple-element.289), channel_id=1, source_target_pairs={{0,16},{4,20},{8,24},{12,28},{16,0},{20,4},{24,8},{28,12},{1,17},{... | collective-permute-start | bytes 2359304 | tf_op jit(solution)/shard_map/ppermute | solution.py:45
  1069.1 102.3 %collective-permute-start.25 = (bf16[768,512]{1,0:T(8,128)(2,1)S(1)}, bf16[768,512]{1,0:T(8,128)(2,1)S(1)}, u32[]{:S(2)}, u32[]{:S(2)}) collective-permute-start(bf16[768,512]{1,0:T(8,128)(2,1)S(1)} %get-tuple-element.288), channel_id=1, source_target_pairs={{0,24},{4,28},{8,0},{12,4},{16,8},{20,12},{24,16},{28,20},{1,25},{... | collective-permute-start | bytes 2359304 | tf_op jit(solution)/shard_map/ppermute | solution.py:45
  1075.6 107.3 %collective-permute-start.18 = (bf16[768,512]{1,0:T(8,128)(2,1)}, bf16[768,512]{1,0:T(8,128)(2,1)}, u32[]{:S(2)}, u32[]{:S(2)}) collective-permute-start(bf16[768,512]{1,0:T(8,128)(2,1)} %get-tuple-element.290), channel_id=1, source_target_pairs={{0,8},{4,12},{8,16},{12,20},{16,24},{20,28},{24,0},{28,4},{1,9},{5... | collective-permute-start | bytes 2359304 | tf_op jit(solution)/shard_map/ppermute | solution.py:45
  1077.0 122.8 %collective-permute-start.19 = (bf16[768,512]{1,0:T(8,128)(2,1)}, bf16[768,512]{1,0:T(8,128)(2,1)}, u32[]{:S(2)}, u32[]{:S(2)}) collective-permute-start(bf16[768,512]{1,0:T(8,128)(2,1)} %get-tuple-element.292), channel_id=1, source_target_pairs={{0,16},{4,20},{8,24},{12,28},{16,0},{20,4},{24,8},{28,12},{1,17},{... | collective-permute-start | bytes 2359304 | tf_op jit(solution)/shard_map/ppermute | solution.py:45
  1083.9 121.3 %collective-permute-start.20 = (bf16[768,512]{1,0:T(8,128)(2,1)}, bf16[768,512]{1,0:T(8,128)(2,1)}, u32[]{:S(2)}, u32[]{:S(2)}) collective-permute-start(bf16[768,512]{1,0:T(8,128)(2,1)} %get-tuple-element.291), channel_id=1, source_target_pairs={{0,24},{4,28},{8,0},{12,4},{16,8},{20,12},{24,16},{28,20},{1,25},{... | collective-permute-start | bytes 2359304 | tf_op jit(solution)/shard_map/ppermute | solution.py:45
  (134 other events, 582.7 us)

commit v3 on v2

--- a/solution.py
+++ b/solution.py
@@ -35,102 +35,12 @@
     return lax.ppermute(values, axis, [(0, 1), (1, 0)])
 
 
-def pair_swap(values):
-    count = lax.axis_size("dp")
-    return lax.ppermute(values, "dp", [(at, at ^ 1) for at in range(count)])
-
-
-def shifted(values, step):
-    count = lax.axis_size("dp")
-    return lax.ppermute(values, "dp", [(at, (at + step) % count) for at in range(count)])
-
-
 def ordered(mine, other, place, axis):
     return jnp.where(
         place == 0,
         jnp.concatenate([mine, other], axis),
         jnp.concatenate([other, mine], axis),
     )
-
-
-def dp_gather(block):
-    count = lax.axis_size("dp")
-    at = lax.axis_index("dp")
-    place = at % 2
-    line = jnp.stack([block] + [shifted(block, step) for step in range(2, count, 2)])
-    both = ordered(line[:, None], pair_swap(line)[:, None], place, 1)
-    pairs = count // 2
-    back = (at // 2 - jnp.arange(pairs)) % pairs
-    return jnp.take(both, back, axis=0).reshape((count,) + block.shape)
-
-
-def dp_scatter(blocks):
-    count = lax.axis_size("dp")
-    at = lax.axis_index("dp")
-    place = at % 2
-    split = blocks.reshape((count // 2, 2) + blocks.shape[1:])
-    mine = lax.dynamic_index_in_dim(split, place, 1, False)
-    other = lax.dynamic_index_in_dim(split, 1 - place, 1, False)
-    summed = (mine.astype(f32) + pair_swap(other).astype(f32)).astype(blocks.dtype)
-    total = lax.dynamic_index_in_dim(summed, at // 2, 0, False).astype(f32)
-    for step in range(1, count // 2):
-        part = lax.dynamic_index_in_dim(summed, (at // 2 + step) % (count // 2), 0, False)
-        total = total + shifted(part, 2 * step).astype(f32)
-    return total
-
-
-def gelu_value(values):
-    return jax.nn.gelu(values, approximate=False)
-
-
-def norm_forward(values, gain, shift):
-    centre = jnp.sum(values, 1, keepdims=True) / D
-    spread = jnp.sum(values * values, 1, keepdims=True) / D - centre * centre
-    inverse = lax.rsqrt(spread + norm_epsilon)
-    unit = (values - centre) * inverse
-    return ((unit * gain + shift).astype(bf16), unit, inverse)
-
-
-def norm_backward(grad, unit, inverse, gain):
-    scaled = grad * gain
-    first = jnp.sum(scaled, 1, keepdims=True)
-    second = jnp.sum(scaled * unit, 1, keepdims=True)
-    return inverse * (scaled - first / D - unit * (second / D))
-
-
-def attend_forward(stacked, bias):
-    factor = HEAD_DIM ** (-0.5)
-
-    def one_head(block):
-        scores = contract(block[0], block[1], (1,), (1,)) * factor + bias
-        peak = jnp.max(scores, 1, keepdims=True)
-        weights = jnp.exp(scores - peak)
-        total = jnp.sum(weights, 1, keepdims=True)
-        probs = (weights / total).astype(bf16)
-        return (
-            jnp.dot(probs, block[2], preferred_element_type=f32),
-            (peak + jnp.log(total))[:, 0],
-        )
-
-    return lax.map(one_head, stacked)
-
-
-def attend_backward(stacked, logsum, grads, bias):
-    factor = HEAD_DIM ** (-0.5)
-
-    def one_head(pack):
-        block, norm_log, back = pack
-        scores = contract(block[0], block[1], (1,), (1,)) * factor + bias
-        probs = jnp.exp(scores - norm_log[:, None])
-        back_probs = contract(back, block[2], (1,), (1,))
-        inner = jnp.sum(probs * back_probs, 1, keepdims=True)
-        back_scores = (probs * (back_probs - inner)).astype(bf16)
-        grad_query = jnp.dot(back_scores, block[1], preferred_element_type=f32) * factor
-        grad_key = contract(back_scores, block[0], (0,), (0,)) * factor
-        grad_value = contract(probs.astype(bf16), back, (0,), (0,))
-        return jnp.stack([grad_query, grad_key, grad_value])
-
-    return lax.map(one_head, (stacked, logsum, grads))
 
 
 def adam_step(master, first, second, grad, rate, decay):
@@ -142,9 +52,6 @@
         / (jnp.sqrt(second_new / (1.0 - beta_second**STEP)) + adam_epsilon)
     )
     return (first_new, second_new, master - rate * (ratio + decay * master))
-
-
-MARKS = [0, D, 2 * D, 3 * D, 4 * D, 5 * D, 6 * D, 7 * D, 8 * D, 8 * D + FF, 9 * D + FF, 10 * D + FF]
 
 
 MESH = pl.DeviceIdType.MESH
@@ -378,6 +285,7 @@
         active_out,
         slope_out,
         output_out,
+        head_mix_out,
         block_out,
         state,
         spot,
@@ -574,7 +482,7 @@
         for copy in core_copies:
             copy.wait()
         save("heads", 3, heads, heads_out.at[layer])
-        settle("lse")
+        settle("lse", "head_mix")
 
         def attend(owner):
             tile = rows // 2
@@ -619,6 +527,7 @@
         mixed[:, lanes] = head_mix[pl.ds(aligned(col * group, 16), group), :]
         back.wait()
         save("lse", 4, lse, lse_out.at[layer])
+        save("head_mix", 14, head_mix, head_mix_out.at[layer])
         save("mixed", 5, mixed, mixed_out.at[layer])
         ready(1)
         pump("project")
@@ -738,6 +647,7 @@
         shape(LAYERS, group, FF // 2, kind=bf16),
         shape(LAYERS, group, FF // 2, kind=bf16),
         shape(LAYERS, rows, D),
+        shape(LAYERS, 2 * group, width, kind=bf16),
         shape(rows, D, kind=bf16),
     ]
     dma = pltpu.SemaphoreType.DMA
@@ -779,19 +689,775 @@
         dma((LAYERS * 3,)),
         dma((LAYERS * 3,)),
         dma((KINDS,)),
-        dma((14,)),
+        dma((15,)),
     ]
     return pl.pallas_call(
         functools.partial(forward_kernel, mesh_count, tokens),
         out_shape=outs,
         in_specs=[WHOLE] * 3 + [ANY] * 4,
-        out_specs=[ANY] * 18 + [WHOLE],
+        out_specs=[ANY] * 19 + [WHOLE],
         scratch_shapes=scratch,
         compiler_params=pltpu.CompilerParams(
             collective_id=0, has_side_effects=True, vmem_limit_bytes=60 << 20
         ),
         name="forward",
     )(state, spot, bias, *shards)
+
+
+def fold(values):
+    return jnp.sum(values.reshape(-1, 8, values.shape[-1]), 0)
+
+
+def total(values):
+    return jnp.sum(values, 0, keepdims=True)
+
+
+def flip(picks, values):
+    high = values.astype(bf16)
+    rest = values - high.astype(f32)
+    middle = rest.astype(bf16)
+    low = (rest - middle.astype(f32)).astype(bf16)
+    return nt(picks, high) + nt(picks, middle) + nt(picks, low)
+
+
+class Scatter:
+    def __init__(self, place, sums, pair_rx, line_rx, outs, refs):
+        self.place, self.sums, self.pair_rx, self.line_rx = place, sums, pair_rx, line_rx
+        self.outs, self.result = outs, refs["result"]
+        self.x_send, self.x_recv = refs["x_send"], refs["x_recv"]
+        self.z_send, self.z_recv = refs["z_send"], refs["z_recv"]
+        self.x_free, self.z_free, self.out_sem = refs["x_free"], refs["z_free"], refs["out_sem"]
+        self.writing = {}
+
+    def size(self, kind):
+        return self.sums[kind].shape[0] // self.place.count
+
+    def block(self, kind, dp):
+        size = self.size(kind)
+        return pl.ds(aligned(dp * size, 16), size)
+
+    def x_copy(self, layer, kind, outer):
+        place = self.place
+        size = self.size(kind)
+        at = layer * KINDS + kind
+        return remote(
+            self.sums[kind].at[self.block(kind, 2 * outer + 1 - place.pair), :],
+            self.pair_rx[kind].at[pl.ds(outer * size, size), :],
+            self.x_send.at[at, outer],
+            self.x_recv.at[at, outer],
+            place.x_peer,
+        )
+
+    def z_copy(self, layer, kind, step):
+        place = self.place
+        size = self.size(kind)
+        at = layer * KINDS + kind
+        outer = lax.rem(place.outer + step, place.line)
+        return remote(
+            self.pair_rx[kind].at[pl.ds(aligned(outer * size, 16), size), :],
+            self.line_rx[kind].at[step - 1],
+            self.z_send.at[at, step - 1],
+            self.z_recv.at[at, step - 1],
+            place.z_peer(step),
+        )
+
+    def x_start(self, layer, kind):
+        if layer < LAYERS - 1:
+            pl.semaphore_wait(self.x_free.at[kind], 1)
+        for outer in range(self.place.line):
+            self.x_copy(layer, kind, outer).start()
+
+    def x_finish(self, layer, kind):
+        place = self.place
+        size = self.size(kind)
+        for outer in range(place.line):
+            self.x_copy(layer, kind, outer).wait()
+        rows = min(size, 64)
+
+        def step(at, carry):
+            outer = lax.div(at, size // rows)
+            inner = lax.rem(at, size // rows)
+            here = pl.ds(aligned(outer * size + inner * rows, 16), rows)
+            own = pl.ds(aligned((2 * outer + place.pair) * size + inner * rows, 16), rows)
+            pair_rx = self.pair_rx[kind]
+            value = pair_rx[here, :].astype(f32) + self.sums[kind][own, :].astype(f32)
+            pair_rx[here, :] = value.astype(bf16)
+            return carry
+
+        lax.fori_loop(0, place.line * (size // rows), step, 0)
+        if layer < LAYERS - 1:
+            pl.semaphore_wait(self.z_free.at[kind], place.line - 1)
+        for step_at in range(1, place.line):
+            self.z_copy(layer, kind, step_at).start()
+
+    def z_finish(self, layer, kind):
+        place = self.place
+        size = self.size(kind)
+        for step_at in range(1, place.line):
+            self.z_copy(layer, kind, step_at).wait()
+        if kind in self.writing:
+            self.writing.pop(kind).wait()
+        rows = min(size, 64)
+
+        def step(at, carry):
+            here = pl.ds(aligned(at * rows, 16), rows)
+            own = pl.ds(aligned(place.outer * size + at * rows, 16), rows)
+            value = self.pair_rx[kind][own, :].astype(f32)
+            for step_at in range(place.line - 1):
+                value = value + self.line_rx[kind][step_at, here, :].astype(f32)
+            self.result[kind][here, :] = value
+            return carry
+
+        lax.fori_loop(0, size // rows, step, 0)
+        copy = pltpu.make_async_copy(
+            self.result[kind], self.outs[kind].at[layer], self.out_sem.at[kind]
+        )
+        copy.start()
+        self.writing[kind] = copy
+        if layer == LAYERS - 1:
+            pl.semaphore_signal(
+                self.x_free.at[kind], inc=1, device_id=place.x_peer, device_id_type=MESH
+            )
+            for step_at in range(1, place.line):
+                pl.semaphore_signal(
+                    self.z_free.at[kind],
+                    inc=1,
+                    device_id=place.z_peer(step_at),
+                    device_id_type=MESH,
+                )
+
+    def finish(self):
+        for copy in self.writing.values():
+            copy.wait()
+
+
+def scatter_vectors(place, grads, packed, spare, spot, target, send, recv):
+    used = grads.shape[1] // 128 // place.line
+    packed[...] = jnp.zeros_like(packed)
+    for outer in range(place.line):
+        for layer in range(LAYERS):
+            for at in range(used):
+                start = (outer * used + at) * 128
+                packed[outer, layer, at : at + 1, :] = grads[layer : layer + 1, start : start + 128]
+    copies = []
+    for step in range(1, place.line):
+        outer = lax.rem(place.outer + step, place.line)
+        copy = remote(
+            packed.at[outer], spare.at[2 + step], send.at[2 + step], recv.at[2 + step], place.z_peer(step)
+        )
+        copy.start()
+        copies.append(copy)
+    for copy in copies:
+        copy.wait()
+    value = packed[place.outer]
+    for step in range(1, place.line):
+        value = value + spare[2 + step]
+    spot[...] = value
+    for at, peer in enumerate((place.x_peer, place.y_peer, place.c_peer)):
+        copy = remote(spot, spare.at[at], send.at[at], recv.at[at], peer)
+        copy.start()
+        copy.wait()
+        spot[...] = spot[...] + spare[at]
+    target[...] = spot[...]
+
+
+def backward_kernel(count, tokens, *refs):
+    (
+        grad_in,
+        vecs,
+        w_a,
+        w_b,
+        w_c,
+        w_d,
+        unit_one_in,
+        inv_one_in,
+        normed_in,
+        heads_in,
+        lse_in,
+        mixed_in,
+        branch_in,
+        unit_two_in,
+        inv_two_in,
+        normed_two_in,
+        active_in,
+        slope_in,
+        output_in,
+        head_mix_in,
+        grad_a,
+        grad_b,
+        grad_c,
+        grad_d,
+        grad_out,
+        vec_out,
+        wq,
+        wm,
+        wu,
+        wd,
+        active,
+        slope,
+        feed,
+        heads,
+        lse,
+        head_mix,
+        mixed,
+        aside,
+        unit,
+        inverse,
+        grad,
+        back_out,
+        back_branch,
+        part,
+        tx,
+        rx,
+        head_back,
+        head_tx,
+        head_grad,
+        key_sum,
+        value_sum,
+        half_tx,
+        sum_a,
+        sum_b,
+        sum_c,
+        sum_d,
+        pair_a,
+        pair_b,
+        pair_c,
+        pair_d,
+        line_a,
+        line_b,
+        line_c,
+        line_d,
+        result_a,
+        result_b,
+        result_c,
+        result_d,
+        vec_grads,
+        packed,
+        spare,
+        spot,
+        y_send,
+        y_recv,
+        c_send,
+        c_recv,
+        x_send,
+        x_recv,
+        z_send,
+        z_recv,
+        x_free,
+        z_free,
+        out_sem,
+        v_send,
+        v_recv,
+        load_sem,
+    ) = refs
+    rows = grad_in.shape[0]
+    group = 2 * rows
+    half = D // 2
+    width = half // 2
+    pairs = width // 128
+    place = Place(count)
+    row, col = place.row, place.col
+    sums = (sum_a, sum_b, sum_c, sum_d)
+    place.greet()
+    scatter = Scatter(
+        place,
+        sums,
+        (pair_a, pair_b, pair_c, pair_d),
+        (line_a, line_b, line_c, line_d),
+        (grad_a, grad_b, grad_c, grad_d),
+        {
+            "result": (result_a, result_b, result_c, result_d),
+            "x_send": x_send,
+            "x_recv": x_recv,
+            "z_send": z_send,
+            "z_recv": z_recv,
+            "x_free": x_free,
+            "z_free": z_free,
+            "out_sem": out_sem,
+        },
+    )
+    triple_back = active
+
+    sources = {
+        "wd": (w_d, wd),
+        "wu": (w_c, wu),
+        "wm": (w_b, wm),
+        "wq": (w_a, wq),
+        "slope": (slope_in, slope),
+        "active": (active_in, active),
+        "normed_two": (normed_two_in, feed),
+        "normed": (normed_in, feed),
+        "output": (output_in, aside),
+        "branch": (branch_in, aside),
+        "unit_two": (unit_two_in, unit),
+        "unit_one": (unit_one_in, unit),
+        "inv_two": (inv_two_in, inverse),
+        "inv_one": (inv_one_in, inverse),
+        "heads": (heads_in, heads),
+        "lse": (lse_in, lse),
+        "head_mix": (head_mix_in, head_mix),
+        "mixed": (mixed_in, mixed),
+    }
+    names = list(sources)
+    loading = {}
+
+    def load(layer, *wanted):
+        for name in wanted:
+            source, buffer = sources[name]
+            copy = pltpu.make_async_copy(
+                source.at[layer], buffer, load_sem.at[names.index(name)]
+            )
+            copy.start()
+            loading[name] = copy
+
+    def loaded(*wanted):
+        for name in wanted:
+            loading.pop(name).wait()
+
+    y_at = [0]
+
+    def y_copy(source, target):
+        at = y_at[0]
+        y_at[0] += 1
+        return remote(source, target, y_send.at[at], y_recv.at[at], place.y_peer)
+
+    c_at = [0]
+
+    def c_copy(source, target):
+        at = c_at[0]
+        c_at[0] += 1
+        return remote(source, target, c_send.at[at], c_recv.at[at], place.c_peer)
+
+    chunk = rows // SPLIT
+
+    def exchange_rows(buffer):
+        copies = []
+        for at in range(SPLIT):
+            copies.append(
+                y_copy(
+                    buffer.at[pl.ds(at * chunk, chunk), :],
+                    buffer.at[pl.ds(rows + at * chunk, chunk), :],
+                )
+            )
+            copies[-1].start()
+        return copies
+
+    load(1, "slope", "wd", "output", "wu", "normed_two", "active", "unit_two", "inv_two")
+    load(1, "wm", "mixed", "heads", "lse", "head_mix", "wq")
+    grad[...] = grad_in[...].astype(f32)
+    vec_grads[...] = jnp.zeros_like(vec_grads)
+    lane = lax.broadcasted_iota(jnp.int32, (1, 128), 1) < HEAD_DIM
+    pick_row = lax.broadcasted_iota(jnp.int32, (8, 128), 0)
+    pick_lane = lax.broadcasted_iota(jnp.int32, (8, 128), 1)
+    halves = (
+        ((pick_row == 0) & (pick_lane < HEAD_DIM)) | ((pick_row == 1) & (pick_lane >= HEAD_DIM))
+    ).astype(bf16)
+    firsts = (pick_lane == pick_row * HEAD_DIM).astype(bf16)
+    size = 32
+
+    def vector(layer, at):
+        return vecs[layer : layer + 1, at * D : (at + 1) * D]
+
+    def note(layer, at, value):
+        vec_grads[layer : layer + 1, at * D : (at + 1) * D] = value
+
+    def by_rows(count_rows, body, terms):
+        def step(at, carry):
+            adds = body(pl.ds(aligned(at * size, size), size))
+            return tuple(old + fold(new) for old, new in zip(carry, adds, strict=True))
+
+        zeros = tuple(jnp.zeros((8, D), f32) for _ in range(terms))
+        sums_ = lax.fori_loop(0, count_rows // size, step, zeros)
+        return [total(value) for value in sums_]
+
+    def half_tiles(kind):
+        return {0: 3, 1: 1, 2: FF // 2 // half, 3: FF // 2 // half}[kind]
+
+    def weight_grad(kind, owner, at):
+        owned = pl.ds(aligned(owner * half), half)
+        tile = pl.ds(aligned(at * half), half)
+        if kind == 0:
+            return tn(feed[:, owned], triple_back[:, tile])
+        if kind == 1:
+            return tn(mixed[...], back_branch[:, owned])
+        if kind == 2:
+            return tn(feed[:, owned], slope[:, tile])
+        return tn(active[:, tile], back_out[:, owned])
+
+    def spot_of(kind, at):
+        tile = pl.ds(aligned(at * half), half)
+        return (tile, slice(None)) if kind == 3 else (slice(None), tile)
+
+    half_copies = {}
+
+    def produce_other(layer, kind):
+        target = sums[kind]
+        buffer = half_tx[kind]
+
+        def step(at, carry):
+            buffer[spot_of(kind, at)] = weight_grad(kind, 1 - col, at).astype(bf16)
+            return carry
+
+        lax.fori_loop(0, half_tiles(kind), step, 0)
+        copy = c_copy(buffer, target)
+        copy.start()
+        half_copies[kind] = copy
+
+    def produce_own(layer, kind):
+        target = sums[kind]
+        half_copies.pop(kind).wait()
+
+        def step(at, carry):
+            here = spot_of(kind, at)
+            value = weight_grad(kind, col, at) + target[here].astype(f32)
+            target[here] = value.astype(bf16)
+            return carry
+
+        lax.fori_loop(0, half_tiles(kind), step, 0)
+        scatter.x_start(layer, kind)
+
+    for layer in reversed(range(LAYERS)):
+        last = layer == LAYERS - 1
+        loaded("output")
+
+        def out_rows(here):
+            value = grad[here, :]
+            back = (vector(layer, 13) * value).astype(bf16)
+            back_out[here, :] = back
+            return (value * aside[here, :], back.astype(f32))
+
+        scale_grad, bias_grad = by_rows(rows, out_rows, 2)
+        copies = exchange_rows(back_out)
+        note(layer, 13, scale_grad)
+        note(layer, 12, bias_grad)
+        load(layer, "branch")
+        if not last:
+            scatter.z_finish(1, 3)
+            scatter.z_finish(1, 2)
+        loaded("slope", "wd")
+
+        def inner_rows(start, count_rows):
+            def step(at, carry):
+                lanes = pl.ds(aligned(at * half), half)
+                value = nt(back_out[start : start + count_rows, :], wd[lanes, :])
+                back = (value * slope[start : start + count_rows, lanes].astype(f32)).astype(bf16)
+                slope[start : start + count_rows, lanes] = back
+                there = pl.ds(aligned(8 * D + row * (FF // 2) + at * half), half)
+                old = vec_grads[layer : layer + 1, there]
+                vec_grads[layer : layer + 1, there] = old + total(back.astype(f32))
+                return carry
+
+            lax.fori_loop(0, FF // 2 // half, step, 0)
+
+        def two_rows(start, count_rows, target, target_at):
+            def step(at, carry):
+                lanes = pl.ds(aligned(at * half), half)
+                value = nt(slope[start : start + count_rows, :], wu[lanes, :])
+                target[pl.ds(target_at, count_rows), lanes] = value.astype(target.dtype)
+                return carry
+
+            lax.fori_loop(0, 2, step, 0)
+
+        inner_rows(0, rows)
+        loaded("wu")
+        if not last:
+            scatter.x_finish(1, 1)
+        back_copies = []
+        for at in range(SPLIT):
+            copies[at].wait()
+            start = rows + at * chunk
+            inner_rows(start, chunk)
+            two_rows(start, chunk, tx, at * chunk)
+            view = pl.ds(at * chunk, chunk)
+            back_copies.append(y_copy(tx.at[view, :], rx.at[view, :]))
+            back_copies[-1].start()
+        two_rows(0, rows, part, 0)
+        if last:
+            load(0, "wd")
+        else:
+            scatter.x_finish(1, 0)
+        loaded("active", "normed_two")
+        produce_other(layer, 3)
+        produce_other(layer, 2)
+        produce_own(layer, 3)
+        produce_own(layer, 2)
+        load(layer, "normed")
+        for copy in back_copies:
+            copy.wait()
+        loaded("unit_two", "inv_two", "branch")
+
+        def middle_rows(here):
+            back = part[here, :] + rx[here, :].astype(f32)
+            norm = unit[here, :]
+            scaled = back * vector(layer, 6)
+            first = jnp.sum(scaled, 1, keepdims=True) * (1.0 / D)
+            second = jnp.sum(scaled * norm, 1, keepdims=True) * (1.0 / D)
+            scale = inverse[here, 0:1]
+            value = grad[here, :] + scale * (scaled - first - norm * second)
+            grad[here, :] = value
+            branch_back = (vector(layer, 5) * value).astype(bf16)
+            back_branch[here, :] = branch_back
+            return (back * norm, back, value * aside[here, :], branch_back.astype(f32))
+
+        terms = by_rows(rows, middle_rows, 4)
+        copies = exchange_rows(back_branch)
+        for at, value in zip((6, 7, 5, 4), terms, strict=True):
+            note(layer, at, value)
+        load(layer, "unit_one", "inv_one")
+        loaded("wm")
+
+        def mixed_rows(start, count_rows):
+            for owner in range(2):
+                lanes = slice(owner * width, owner * width + width)
+                value = nt(back_branch[start : start + count_rows, :], wm[lanes, :]).astype(bf16)
+
+                @pl.when(owner == col)
+                def _():
+                    head_back[pl.ds(aligned(col * group + start, 16), count_rows), :] = value
+
+                @pl.when(owner != col)
+                def _():
+                    head_tx[start : start + count_rows, :] = value
+
+        core_copies = []
+
+        def send_back(start):
+            core_copies.append(
+                c_copy(
+                    head_tx.at[pl.ds(start, rows), :],
+                    head_back.at[pl.ds(aligned(col * group + start, 16), rows), :],
+                )
+            )
+            core_copies[-1].start()
+
+        mixed_rows(0, rows)
+        send_back(0)
+        for copy in copies:
+            copy.wait()
+        mixed_rows(rows, rows)
+        send_back(rows)
+        loaded("heads", "lse", "head_mix", "mixed")
+        if last:
+            load(0, "wm")
+        else:
+            scatter.z_finish(1, 1)
+            scatter.z_finish(1, 0)
+        for copy in core_copies:
+            copy.wait()
+
+        piece = 2 * group // 4
+        head_copies = []
+        for pair in range(pairs):
+            lanes = slice(pair * 128, pair * 128 + 128)
+            key_lanes = slice(width + pair * 128, width + pair * 128 + 128)
+            value_lanes = slice(2 * width + pair * 128, 2 * width + pair * 128 + 128)
+            key_sum[...] = jnp.zeros_like(key_sum)
+            value_sum[...] = jnp.zeros_like(value_sum)
+
+            def step(at, carry, lanes=lanes, key_lanes=key_lanes, value_lanes=value_lanes):
+                here = pl.ds(aligned(at * 128), 128)
+                query = heads[here, lanes] * jnp.asarray(HEAD_DIM**-0.5, bf16)
+                back = head_back[here, lanes]
+                zero = jnp.zeros_like(query)
+                queries = jnp.concatenate(
+                    [jnp.where(lane, query, zero), jnp.where(lane, zero, query)], 0
+                )
+                backs = jnp.concatenate(
+                    [jnp.where(lane, back, zero), jnp.where(lane, zero, back)], 0
+                )
+                logs = flip(firsts, lse[here, lanes])
+                logs = jnp.concatenate([logs[0:1], logs[1:2]], 1)
+                inner = flip(halves, back.astype(f32) * head_mix[here, lanes].astype(f32))
+                inner = jnp.concatenate([inner[0:1], inner[1:2]], 1)
+                query_grad = jnp.zeros((256, 128), f32)
+                for block in range(4):
+                    keys = slice(block * piece, block * piece + piece)
+                    key = heads[keys, key_lanes]
+                    scores = nt(key, queries)
+                    probs = jnp.exp(jnp.minimum(scores - logs, 0.0))
+                    back_probs = nt(heads[keys, value_lanes], backs)
+                    back_scores = (probs * (back_probs - inner)).astype(bf16)
+                    value_sum[keys, :] += nn(probs.astype(bf16), backs)
+                    key_sum[keys, :] += nn(back_scores, queries)
+                    query_grad = query_grad + tn(back_scores, key)
+                query_grad = query_grad * HEAD_DIM**-0.5
+                head_grad[here, lanes] = jnp.where(
+                    lane, query_grad[:128], query_grad[128:]
+                ).astype(bf16)
+                return carry
+
+            lax.fori_loop(0, 2 * group // 128, step, 0)
+            for owner in range(2):
+                edge = owner * rows
+                valid = lax.broadcasted_iota(jnp.int32, (rows, 1), 0) < tokens - edge
+                for part_at in range(2):
+                    here = slice(owner * group + part_at * rows, owner * group + part_at * rows + rows)
+                    head_grad[here, key_lanes] = jnp.where(valid, key_sum[here, :], 0.0).astype(bf16)
+                    head_grad[here, value_lanes] = jnp.where(valid, value_sum[here, :], 0.0).astype(bf16)
+            if pair == pairs - 1:
+                if last:
+                    scatter.x_finish(1, 2)
+            else:
+                scatter.x_finish(layer, 3)
+            there = pl.ds(aligned((1 - col) * group, 16), group)
+            mine = pl.ds(aligned(col * group, 16), group)
+            for part_at, source in enumerate((lanes, key_lanes, value_lanes)):
+                target = pl.ds(aligned(part_at * half + col * width + pair * 128), 128)
+                copy = c_copy(head_grad.at[there, source], triple_back.at[:, target])
+                copy.start()
+                head_copies.append(copy)
+                triple_back[:, target] = head_grad[mine, source]
+                if part_at != 1:
+                    bias_at = pl.ds(
+                        aligned((3 * D if part_at else 2 * D) + row * half + col * width + pair * 128), 128
+                    )
+                    vec_grads[layer : layer + 1, bias_at] = total(head_grad[:, source].astype(f32))
+        if not last:
+            scatter.x_finish(0, 2)
+        for copy in head_copies:
+            copy.wait()
+        loaded("wq", "normed")
+        if not last:
+            produce_other(layer, 0)
+
+        def one_rows(start, count_rows, target, target_at):
+            def step(at, carry):
+                lanes = pl.ds(aligned(at * half), half)
+                value = nt(triple_back[start : start + count_rows, : 3 * half], wq[lanes, :])
+                target[pl.ds(target_at, count_rows), lanes] = value.astype(target.dtype)
+                return carry
+
+            lax.fori_loop(0, 2, step, 0)
+
+        back_copies = []
+        for at in range(SPLIT):
+            start = rows + at * chunk
+            one_rows(start, chunk, tx, at * chunk)
+            view = pl.ds(at * chunk, chunk)
+            back_copies.append(y_copy(tx.at[view, :], rx.at[view, :]))
+            back_copies[-1].start()
+        if last:
+            produce_other(layer, 1)
+            produce_other(layer, 0)
+            produce_own(layer, 1)
+            produce_own(layer, 0)
+        else:
+            produce_own(layer, 0)
+            produce_other(layer, 1)
+            produce_own(layer, 1)
+        one_rows(0, rows, part, 0)
+        if last:
+            load(0, "slope", "wu", "wq", "output", "normed_two", "active")
+            load(0, "mixed", "heads", "lse", "head_mix")
+        loaded("unit_one", "inv_one")
+        for copy in back_copies:
+            copy.wait()
+
+        def input_rows(here):
+            back = part[here, :] + rx[here, :].astype(f32)
+            norm = unit[here, :]
+            scaled = back * vector(layer, 0)
+            first = jnp.sum(scaled, 1, keepdims=True) * (1.0 / D)
+            second = jnp.sum(scaled * norm, 1, keepdims=True) * (1.0 / D)
+            scale = inverse[here, 0:1]
+            grad[here, :] = grad[here, :] + scale * (scaled - first - norm * second)
+            return (back * norm, back)
+
+        terms = by_rows(rows, input_rows, 2)
+        for at, value in zip((0, 1), terms, strict=True):
+            note(layer, at, value)
+        if last:
+            load(0, "unit_two", "inv_two")
+    grad_out[...] = grad[...]
+    scatter.z_finish(0, 3)
+    scatter.z_finish(0, 2)
+    scatter_vectors(place, vec_grads, packed, spare, spot, vec_out, v_send, v_recv)
+    scatter.x_finish(0, 0)
+    scatter.x_finish(0, 1)
+    scatter.z_finish(0, 0)
+    scatter.z_finish(0, 1)
+    scatter.finish()
+
+
+def backward_call(mesh_count, tokens, grad, vecs, weights, saved, spot_shape):
+    rows = grad.shape[0]
+    group = 2 * rows
+    half = D // 2
+    width = half // 2
+    line = mesh_count // 2
+    wide = FF // 2
+
+    def shape(*dims, kind=f32):
+        return jax.ShapeDtypeStruct(dims, kind)
+
+    halves = [(half, 3 * half), (half, half), (half, wide), (wide, half)]
+    shards = [(dims[0] // mesh_count, dims[1]) for dims in halves]
+    outs = [shape(LAYERS, *dims) for dims in shards]
+    outs += [shape(rows, D), shape(*spot_shape)]
+    dma = pltpu.SemaphoreType.DMA
+    scratch = [
+        pltpu.VMEM((D, 3 * half), bf16),
+        pltpu.VMEM((half, D), bf16),
+        pltpu.VMEM((D, wide), bf16),
+        pltpu.VMEM((wide, D), bf16),
+        pltpu.VMEM((group, wide), bf16),
+        pltpu.VMEM((group, wide), bf16),
+        pltpu.VMEM((group, D), bf16),
+        pltpu.VMEM((2 * group, 3 * width), bf16),
+        pltpu.VMEM((2 * group, width), f32),
+        pltpu.VMEM((2 * group, width), bf16),
+        pltpu.VMEM((group, half), bf16),
+        pltpu.VMEM((rows, D), f32),
+        pltpu.VMEM((rows, D), f32),
+        pltpu.VMEM((rows, 128), f32),
+        pltpu.VMEM((rows, D), f32),
+        pltpu.VMEM((group, D), bf16),
+        pltpu.VMEM((group, D), bf16),
+        pltpu.VMEM((rows, D), f32),
+        pltpu.VMEM((rows, D), bf16),
+        pltpu.VMEM((rows, D), bf16),
+        pltpu.VMEM((2 * group, width), bf16),
+        pltpu.VMEM((group, width), bf16),
+        pltpu.VMEM((2 * group, 3 * width), bf16),
+        pltpu.VMEM((2 * group, 128), f32),
+        pltpu.VMEM((2 * group, 128), f32),
+        [pltpu.VMEM(dims, bf16) for dims in halves],
+    ]
+    scratch += [pltpu.VMEM(dims, bf16) for dims in halves]
+    scratch += [pltpu.VMEM((dims[0] // 2, dims[1]), bf16) for dims in halves]
+    scratch += [pltpu.VMEM((line - 1,) + dims, bf16) for dims in shards]
+    scratch += [pltpu.VMEM(dims, f32) for dims in shards]
+    scratch += [
+        pltpu.VMEM((LAYERS, 10 * D + FF), f32),
+        pltpu.VMEM((line,) + spot_shape, f32),
+        pltpu.VMEM((line + 2,) + spot_shape, f32),
+        pltpu.VMEM(spot_shape, f32),
+        dma((LAYERS * 4 * SPLIT,)),
+        dma((LAYERS * 4 * SPLIT,)),
+        dma((LAYERS * 12,)),
+        dma((LAYERS * 12,)),
+        dma((GROUPS, line)),
+        dma((GROUPS, line)),
+        dma((GROUPS, line - 1)),
+        dma((GROUPS, line - 1)),
+        pltpu.SemaphoreType.REGULAR((KINDS,)),
+        pltpu.SemaphoreType.REGULAR((KINDS,)),
+        dma((KINDS,)),
+        dma((line + 2,)),
+        dma((line + 2,)),
+        dma((18,)),
+    ]
+    return pl.pallas_call(
+        functools.partial(backward_kernel, mesh_count, tokens),
+        out_shape=outs,
+        in_specs=[WHOLE] * 2 + [ANY] * 18,
+        out_specs=[ANY] * 4 + [WHOLE] * 2,
+        scratch_shapes=scratch,
+        compiler_params=pltpu.CompilerParams(
+            collective_id=1, has_side_effects=True, vmem_limit_bytes=63 << 20
+        ),
+        name="backward",
+    )(grad, vecs, *weights, *saved)
 
 
 def local(
@@ -820,8 +1486,6 @@
     rows = -(-tokens // (2 * TILE)) * TILE
     group = 2 * rows
     half = D // 2
-    heads = half // 2 // HEAD_DIM
-    width = heads * HEAD_DIM
 
     def to_tokens(values):
         padded = jnp.pad(values, ((0, 2 * rows - tokens), (0, 0))).reshape(2, rows, features)
@@ -834,33 +1498,6 @@
         mine = lax.dynamic_index_in_dim(split, col_at, 0, False)
         other = swap(lax.dynamic_index_in_dim(split, 1 - col_at, 0, False), "col")
         return ordered(mine, other, col_at, 0)[:tokens]
-
-    def row_rows(values):
-        return jnp.concatenate([values, swap(values, "row")], 0)
-
-    def row_sum(partial):
-        return partial[:rows] + swap(partial[rows:].astype(bf16), "row").astype(f32)
-
-    shard_shapes = [
-        values.shape[1:] for values in (triplet_master, project_master, expand_master, shrink_master)
-    ]
-    lane = half
-
-    def flat(parts):
-        return jnp.concatenate([part.reshape(-1, lane) for part in parts], 0)
-
-    def unflat(values, lead=()):
-        parts = []
-        at = 0
-        for shape in shard_shapes:
-            size = 1
-            for side in shape:
-                size *= side
-            size //= lane
-            parts.append(values[..., at : at + size, :].reshape(lead + shape))
-            at += size
-        return parts
-
 
     shards = [
         triplet_master.astype(bf16).reshape(LAYERS, -1, 3 * half),
@@ -873,135 +1510,23 @@
     spot = lax.dynamic_update_slice_in_dim(
         jnp.zeros((LAYERS, 8 * piece), f32), vectors_master, line_at * piece, 1
     ).reshape(LAYERS, -1, 128)
-    spot = jnp.pad(spot, ((0, 0), (0, -spot.shape[1] % 8), (0, 0)))
+    used = spot.shape[1]
+    spot = jnp.pad(spot, ((0, 0), (0, -used % 8), (0, 0)))
     place = jnp.arange(2 * group) % rows
     late = jnp.arange(2 * group) // group
-    valid = place + late * rows < tokens
-    bias = jnp.where(valid, 0.0, -1e30).astype(f32)[None]
-
-    def to_heads(values, parts):
-        split = values.reshape(group, parts, 2, width).transpose(2, 0, 1, 3)
-        mine = lax.dynamic_index_in_dim(split, col_at, 0, False)
-        other = swap(lax.dynamic_index_in_dim(split, 1 - col_at, 0, False), "col")
-        return (
-            ordered(mine, other, col_at, 0)
-            .reshape(2 * group, parts, heads, HEAD_DIM)
-            .transpose(2, 1, 0, 3)
-        )
-
-    def from_heads(values):
-        parts = values.shape[1]
-        split = values.transpose(2, 1, 0, 3).reshape(2, group, parts, width)
-        mine = lax.dynamic_index_in_dim(split, col_at, 0, False)
-        other = swap(lax.dynamic_index_in_dim(split, 1 - col_at, 0, False), "col")
-        return ordered(mine[:, :, None], other[:, :, None], col_at, 2).reshape(group, parts, half)
-
-    head_start = row_at * half + col_at * width
-
-    def pieces(vector):
-        return [vector[MARKS[at] : MARKS[at + 1]] for at in range(11)]
-
-    kept_all = forward_call(count, tokens, to_tokens(images), spot, bias, shards)
-    (w_a, w_b, w_c, w_d, vectors, *saved, block_rows) = kept_all
-    layer_pieces = [pieces(vectors[layer]) for layer in range(LAYERS)]
-    kept = []
-    weights = []
-    for layer in range(LAYERS):
-        (unit_one, inverse_one, normed_all, heads_all, lse, mixed, branch, unit_two, inverse_two,
-         normed_two_all, active, slope, output) = [value[layer] for value in saved]
-        weights.append((w_a[layer].reshape(D, 3, half), w_b[layer], w_c[layer], w_d[layer]))
-        stacked = heads_all.reshape(2 * group, 3, heads, HEAD_DIM).transpose(2, 1, 0, 3)
-        logsum = lse.reshape(2 * group, heads, HEAD_DIM)[:, :, 0].T
-        kept.append((unit_one, inverse_one[:, :1], normed_all, stacked, logsum, mixed, branch, unit_two,
-            inverse_two[:, :1], normed_two_all, slope, active, output))
+    bias = jnp.where(place + late * rows < tokens, 0.0, -1e30).astype(f32)[None]
+
+    (w_a, w_b, w_c, w_d, vectors, *saved, block_rows) = forward_call(
+        count, tokens, to_tokens(images), spot, bias, shards
+    )
     block_out = to_features(block_rows)
-    grad = to_tokens(cotangent).astype(f32)
-    reduced = [None] * LAYERS
-    vector_grads = [None] * LAYERS
-    for layer in reversed(range(LAYERS)):
-        (
-            unit_one,
-            inverse_one,
-            normed_all,
-            stacked,
-            logsum,
-            mixed,
-            branch,
-            unit_two,
-            inverse_two,
-            normed_two_all,
-            slope,
-            active,
-            output,
-        ) = kept[layer]
-        parts = layer_pieces[layer]
-        triplet_w, project_w, expand_w, shrink_w = weights[layer]
-        output_scale_grad = jnp.sum(grad * output, 0)
-        back_out = (parts[10] * grad).astype(bf16)
-        output_bias_grad = jnp.sum(back_out.astype(f32), 0)
-        back_out_all = row_rows(back_out)
-        shrink_grad = contract(active, back_out_all, (0,), (0,)).astype(bf16)
-        back_active = contract(back_out_all, shrink_w, (1,), (1,))
-        back_inner = (slope.astype(f32) * back_active).astype(bf16)
-        hidden_bias_grad = jnp.sum(back_inner.astype(f32), 0)
-        expand_grad = contract(normed_two_all, back_inner, (0,), (0,)).astype(bf16)
-        back_two = row_sum(contract(back_inner, expand_w, (1,), (1,)))
-        second_gain_grad = jnp.sum(back_two * unit_two, 0)
-        second_shift_grad = jnp.sum(back_two, 0)
-        grad_middle = grad + norm_backward(back_two, unit_two, inverse_two, parts[6])
-        branch_scale_grad = jnp.sum(grad_middle * branch, 0)
-        back_branch = (parts[5] * grad_middle).astype(bf16)
-        mixer_bias_grad = jnp.sum(back_branch.astype(f32), 0)
-        back_branch_all = row_rows(back_branch)
-        project_grad = contract(mixed, back_branch_all, (0,), (0,)).astype(bf16)
-        back_mixed = contract(back_branch_all, project_w, (1,), (1,)).astype(bf16)
-        back_heads = to_heads(back_mixed[:, None], 1)[:, 0]
-        back_stacked = attend_backward(stacked, logsum, back_heads, bias).astype(bf16)
-        triple_sums = jnp.sum(back_stacked.astype(f32), 2)
-        back_triple = from_heads(back_stacked)
-        triplet_grad = contract(normed_all, back_triple, (0,), (0,)).astype(bf16)
-        back_one = row_sum(contract(back_triple, triplet_w, (1, 2), (1, 2)))
-        norm_gain_grad = jnp.sum(back_one * unit_one, 0)
-        norm_shift_grad = jnp.sum(back_one, 0)
-        grad = grad_middle + norm_backward(back_one, unit_one, inverse_one, parts[0])
-
-        def spread(values, size, start):
-            return lax.dynamic_update_slice_in_dim(jnp.zeros((size,), f32), values, start, 0)
-
-        vector_grads[layer] = jnp.concatenate(
-            [
-                norm_gain_grad,
-                norm_shift_grad,
-                spread(triple_sums[:, 0].reshape(width), D, head_start),
-                spread(triple_sums[:, 2].reshape(width), D, head_start),
-                mixer_bias_grad,
-                branch_scale_grad,
-                second_gain_grad,
-                second_shift_grad,
-                spread(hidden_bias_grad, FF, row_at * (FF // 2)),
-                output_bias_grad,
-                output_scale_grad,
-            ]
-        )
-        wide = [
-            triplet_grad.reshape(2, count, -1, lane),
-            project_grad.reshape(count, -1, 2, lane).transpose(2, 0, 1, 3),
-            expand_grad.reshape(2, count, -1, lane),
-            shrink_grad.reshape(count, -1, 2, lane).transpose(2, 0, 1, 3),
-        ]
-        blocks = jnp.concatenate(wide, 2)
-        mine = lax.dynamic_index_in_dim(blocks, col_at, 0, False)
-        other = swap(lax.dynamic_index_in_dim(blocks, 1 - col_at, 0, False), "col")
-        reduced[layer] = unflat(
-            dp_scatter((mine.astype(f32) + other.astype(f32)).astype(bf16))
-        )
-    grad_out = to_features(grad)
-
-    spots = jnp.stack(vector_grads).reshape(LAYERS, count, 2, 2, -1)
-    for axis, at, dim in (("col", col_at, 3), ("row", row_at, 2)):
-        mine = lax.dynamic_index_in_dim(spots, at, dim, False)
-        spots = mine + swap(lax.dynamic_index_in_dim(spots, 1 - at, dim, False), axis)
-    vector_reduced = dp_scatter(spots.transpose(1, 0, 2))
+    *grads, grad_rows, vector_sums = backward_call(
+        count, tokens, to_tokens(cotangent), vectors, (w_a, w_b, w_c, w_d), saved, spot.shape
+    )
+    grad_out = to_features(grad_rows)
+    vector_reduced = lax.dynamic_slice_in_dim(
+        vector_sums[:, :used].reshape(LAYERS, -1), line_at * piece, piece, 1
+    )
 
     outs = []
     states = (
@@ -1011,8 +1536,9 @@
         (shrink_master, shrink_first, shrink_second),
     )
     for kind, (master, first, second) in enumerate(states):
-        total = jnp.stack([reduced[layer][kind] for layer in range(LAYERS)])
-        outs += adam_step(master, first, second, total, learn_rate, decay_rate)
+        outs += adam_step(
+            master, first, second, grads[kind].reshape(master.shape), learn_rate, decay_rate
+        )
     outs += adam_step(
         vectors_master, vectors_first, vectors_second, vector_reduced, vector_rate, 0.0
     )

time: 1230 us -> 580 us (0.47)
  the two profiles are of different devices: /device:TPU:9 before, /device:TPU:0 now
where the time goes in v3:
time: 580 us; the launch traced here: 571 us
  Pallas kernels  529 us (91%)
  local copies, waits for them, and re-layouts  21.4 us (4%)
  other arithmetic  18.8 us (3%)
    pallas_call x1, Pallas kernels, backward_call(): pl.pallas_call(functools.partial(backward_kernel, mesh_count, tokens), ou...  286 us
    pallas_call x1, Pallas kernels, forward_call(): pl.pallas_call(functools.partial(forward_kernel, mesh_count, tokens), out...  242 us
  transfers between devices with their start and end apart: 4, of which 0 were waited for; matrix products, arithmetic and copies ran while one was open for 6% of the time, Pallas kernels for 93%

profile of v3, /device:TPU:0, one launch (start us, length us, event | category | flops | bytes accessed | tf_op | source)
XLA Modules:
  0.0 571.0 jit_solution(7450310666041526750)
XLA Ops:
  0.7 0.0 copy-start.19
  0.7 1.2 pad.11
  1.9 0.9 dynamic-slice_bitcast_fusion.3
  2.8 0.5 collective-permute-start
  3.3 0.0 copy-done.19
  3.3 0.0 copy-start.24
  3.3 0.0 copy-start.14
  3.3 0.9 dynamic-slice_bitcast_fusion.1
  4.3 0.1 collective-permute-start.2
  4.3 0.0 copy-done.4
  4.4 0.6 compare_select_fusion.refs_2_
  5.0 0.6 broadcast_in_dim.12
  5.6 1.3 dynamic_update_slice.3
  7.0 1.5 reshape.135
  8.4 1.4 pad.12.refs_1_
  9.8 0.7 convert_element_type.18.refs_4_
  10.5 0.8 copy.59
  11.3 0.0 copy-done
  11.3 0.9 convert_element_type.19.refs_5_
  12.1 0.0 copy-done.2
  12.1 0.9 convert_element_type.20.refs_6_
  13.0 0.0 collective-permute-done
  13.0 2.2 maximum_select_fusion.refs_0_
  15.2 242.4 %forward.1 = (bf16[2,1024,1536]{2,1,0:T(8,128)(2,1)}, bf16[2,512,1024]{2,1,0:T(8,128)(2,1)}, bf16[2,1024,2048]{2,1,0:T(8,128)(2,1)}, bf16[2,2048,1024]{2,1,0:T(8...) custom-call(bf16[352,1024]{1,0:T(8,128)(2,1)} %maximum_select_fusion, ...), custom_call_target="tpu_custom_call" | custom-call | tf_op jit(solution)/shard_map/forward/pallas_call | solution.py:694
  257.6 2.8 reshape.137
  260.4 1.5 constant_dynamic-slice_fusion.3
  261.9 0.0 copy-start.6
  261.9 0.8 copy.73
  262.7 0.8 copy.72
  263.5 0.0 collective-permute-start.1
  263.5 0.0 collective-permute-done.2
  263.5 0.0 copy-done.6
  263.5 2.2 maximum_select_fusion.1.refs_0_
  265.7 286.4 %backward.1 = (f32[2,64,1536]{2,1,0:T(8,128)}, f32[2,64,512]{2,1,0:T(8,128)}, f32[2,64,2048]{2,1,0:T(8,128)}, f32[2,256,512]{2,1,0:T(8,128)}, f32[352,1024]{1,0:T(8,128)}, /*index=5*/f32[2,32,128]{2,1,0:T(8,128)}) custom-call(bf16[352,1024]{1,0:T(8,128)(2,1)} %maximum_select_fusion.1.refs_0_, f32[2,14336]{1,0:T(2,128)} %get-tuple-element.44.refs_1_, ...), custom_call_target="tpu_custom_call" | custom-call | tf_op jit(solution)/shard_map/backward/pallas_call | solution.py:1450
  552.1 2.8 reshape.139
  554.8 0.0 copy-start.15
  554.9 0.0 copy-start.20
  554.9 0.0 copy-start.21
  554.9 1.2 constant_dynamic-slice_fusion.1
  556.2 0.0 copy-start.1
  556.2 0.0 copy-start.8
  556.2 0.0 copy-start.9
  556.2 0.1 collective-permute-start.3
  556.4 0.0 copy-done.20
  556.4 1.0 multiply_subtract_fusion.3
  557.4 0.0 copy-done.13
  557.4 0.1 copy-done.1
  557.5 0.6 copy-done.8
  558.0 0.3 copy-done.9
  558.4 2.2 multiply_subtract_fusion.1
  560.6 0.0 copy-done.3
  560.6 0.7 copy-done.11
  561.3 0.3 copy-done.12
  561.7 2.3 multiply_subtract_fusion
  564.1 0.7 multiply_subtract_fusion.4
  564.8 0.0 copy-done.18
  564.8 0.3 copy-done.16
  565.1 0.2 copy-done.17
  565.3 1.8 multiply_subtract_fusion.2
  567.2 0.0 collective-permute-done.1
  567.2 0.0 copy-done.5
  567.2 2.2 fusion.5
  569.3 0.0 collective-permute-done.3
  569.3 1.2 fusion
  (33 shorter events, 0.3 us)
Async XLA Ops:
  0.7 2.6 copy-start.19
  2.8 1.5 copy-start.4
  2.8 10.2 %collective-permute-start = (bf16[352,512]{1,0:T(8,128)(2,1)}, bf16[352,512]{1,0:T(8,128)(2,1)}, u32[]{:S(2)}, u32[]{:S(2)}) collective-permute-start(bf16[352,512]{1,0:T(8,128)(2,1)} %get-tuple-element.108), channel_id=1, source_target_pairs={{0,1},{1,0},{2,3},{3,2},{4,5},{5,4},{6,7},{7,6},{8,9},{9,8},{10,11... | collective-permute-start | bytes 1081352 | tf_op jit(solution)/shard_map/ppermute | solution.py:35
  3.3 2.3 copy-start.24
  3.3 6.5 %copy-start.14 = (f32[2,64,512]{2,1,0:T(8,128)S(1)}, f32[2,64,512]{2,1,0:T(8,128)}, u32[]{:S(2)}) copy-start(f32[2,64,512]{2,1,0:T(8,128)} %param.22) | copy-start | bytes 786436
  4.3 7.0 %copy-start = (f32[2,64,2048]{2,1,0:T(8,128)S(1)}, f32[2,64,2048]{2,1,0:T(8,128)}, u32[]{:S(2)}) copy-start(f32[2,64,2048]{2,1,0:T(8,128)} %param.25) | copy-start | bytes 3145732
  4.3 259.2 %collective-permute-start.2 = (bf16[352,512]{1,0:T(8,128)(2,1)}, bf16[352,512]{1,0:T(8,128)(2,1)}, u32[]{:S(2)}, u32[]{:S(2)}) collective-permute-start(bf16[352,512]{1,0:T(8,128)(2,1)} %get-tuple-element.104), channel_id=1, source_target_pairs={{0,1},{1,0},{2,3},{3,2},{4,5},{5,4},{6,7},{7,6},{8,9},{9,8},{10,11... | collective-permute-start | bytes 1081352 | tf_op jit(solution)/shard_map/ppermute | solution.py:35
  7.0 5.2 copy-start.2
  11.3 1.7 copy-start.7
  261.9 1.6 copy-start.6
  263.5 303.7 %collective-permute-start.1 = (bf16[352,512]{1,0:T(8,128)(2,1)}, bf16[352,512]{1,0:T(8,128)(2,1)}, u32[]{:S(2)}, u32[]{:S(2)}) collective-permute-start(bf16[352,512]{1,0:T(8,128)(2,1)} %bitcast.35), channel_id=1, source_target_pairs={{0,1},{1,0},{2,3},{3,2},{4,5},{5,4},{6,7},{7,6},{8,9},{9,8},{10,11... | collective-permute-start | bytes 1081352 | tf_op jit(solution)/shard_map/ppermute | solution.py:35
  554.8 1.5 copy-start.15
  554.9 1.5 copy-start.20
  554.9 1.5 copy-start.21
  554.9 1.5 copy-start.22
  554.9 2.5 copy-start.13
  556.2 1.3 copy-start.1
  556.2 1.9 copy-start.8
  556.2 2.2 copy-start.9
  556.2 13.1 %collective-permute-start.3 = (f32[352,512]{1,0:T(8,128)S(1)}, f32[352,512]{1,0:T(8,128)S(1)}, u32[]{:S(2)}, u32[]{:S(2)}) collective-permute-start(f32[352,512]{1,0:T(8,128)S(1)} %bitcast.44), channel_id=1, source_target_pairs={{0,1},{1,0},{2,3},{3,2},{4,5},{5,4},{6,7},{7,6},{8,9},{9,8},{10,11... | collective-permute-start | bytes 2162696 | tf_op jit(solution)/shard_map/ppermute | solution.py:35
  558.4 2.2 copy-start.3
  558.4 2.2 copy-start.10
  558.4 3.0 copy-start.11
  558.4 3.3 copy-start.12
  561.7 2.3 copy-start.23
  561.7 2.4 copy-start.25
  561.7 2.4 copy-start.26
  561.7 3.1 copy-start.18
  563.9 1.1 copy-start.16
  563.9 1.4 copy-start.17
  565.3 1.8 copy-start.5

commit v4 on v3

--- a/solution.py
+++ b/solution.py
@@ -31,18 +31,6 @@
     )
 
 
-def swap(values, axis):
-    return lax.ppermute(values, axis, [(0, 1), (1, 0)])
-
-
-def ordered(mine, other, place, axis):
-    return jnp.where(
-        place == 0,
-        jnp.concatenate([mine, other], axis),
-        jnp.concatenate([other, mine], axis),
-    )
-
-
 def adam_step(master, first, second, grad, rate, decay):
     first_new = beta_first * first + (1.0 - beta_first) * grad
     second_new = beta_second * second + (1.0 - beta_second) * grad * grad
@@ -57,6 +45,9 @@
 MESH = pl.DeviceIdType.MESH
 KINDS = 4
 GROUPS = LAYERS * KINDS
+WINDOW = 2
+TRIGGER = 1.0
+LEAD = 25.0
 SPLIT = 2
 ANY = pl.BlockSpec(memory_space=pl.ANY)
 WHOLE = pl.BlockSpec(memory_space=pltpu.VMEM)
@@ -88,6 +79,12 @@
         self.y_peer = (self.dp, 1 - self.row, self.col)
         self.c_peer = (self.dp, self.row, 1 - self.col)
 
+    def nearest(self, at):
+        inside = (at + 1) // 2 if at % 2 else self.line - at // 2
+        return jnp.where(
+            self.outer == 0, self.line - at, jnp.where(self.outer == self.line - 1, at, inside)
+        )
+
     def ahead(self, step):
         return lax.rem(self.dp + 2 * step, self.count)
 
@@ -135,110 +132,195 @@
 
 
 class Gather:
-    def __init__(self, place, shards, wholes, send, recv, own):
-        self.place, self.shards, self.wholes = place, shards, wholes
-        self.send, self.recv, self.own = send, recv, own
+    def __init__(self, place, shards, wholes, far, refs):
+        self.place, self.shards, self.wholes, self.far = place, shards, wholes, far
+        self.send, self.recv, self.own = refs["send"], refs["recv"], refs["own"]
+        self.far_send, self.far_recv = refs["far_send"], refs["far_recv"]
+
+    def view(self, group, dp):
+        layer, kind = divmod(group, KINDS)
+        return weight_view(kind, self.wholes[kind], layer, self.place, dp, self.place.col)
+
+    def copy(self, group, at, source, target, peer):
+        return remote(source, target, self.send.at[group, at], self.recv.at[group, at], peer)
+
+    def shard(self, group):
+        layer, kind = divmod(group, KINDS)
+        return self.shards[kind].at[layer]
 
     def line_copy(self, group, step):
-        layer, kind = divmod(group, KINDS)
+        place = self.place
+        target = self.view(group, place.dp)
+        return self.copy(group, step - 1, self.shard(group), target, place.z_peer(step))
+
+    def pair_copy(self, group, step):
+        place = self.place
+        view = self.view(group, place.behind(step))
+        source = self.shard(group) if isinstance(step, int) else view
+        return self.copy(group, place.line - 1 + step, source, view, place.x_peer)
+
+    def core_copy(self, group, step, pair):
+        place = self.place
+        dp = lax.rem(place.x_dp + place.count - 2 * step, place.count) if pair else place.behind(step)
+        view = self.view(group, dp)
+        source = view if pair or not isinstance(step, int) else self.shard(group)
+        at = 2 * place.line - 1 + pair * place.line + step
+        return self.copy(group, at, source, view, place.c_peer)
+
+    def own_copy(self, group):
+        return pltpu.make_async_copy(
+            self.shard(group), self.view(group, self.place.dp), self.own.at[group]
+        )
+
+    def line_out(self, group):
+        for at in range(1, self.place.line):
+            self.line_copy(group, at).start()
+
+    def own_out(self, group):
+        self.pair_copy(group, 0).start()
+        self.core_copy(group, 0, 0).start()
+        self.own_copy(group).start()
+
+    def line_in(self, group, at):
+        step = self.place.nearest(at)
+        self.line_copy(group, step).wait_recv()
+        self.pair_copy(group, step).start()
+        self.core_copy(group, step, 0).start()
+
+    def pair_in(self, group, at):
+        step = self.place.nearest(at) if at else 0
+        self.pair_copy(group, step).wait_recv()
+        self.core_copy(group, step, 1).start()
+
+    def arrive(self, group):
+        self.own_copy(group).wait()
+        for pair in range(2):
+            for step in range(self.place.line):
+                self.core_copy(group, step, pair).wait_recv()
+
+    def far_copy(self, layer):
         place = self.place
         return remote(
-            self.shards[kind].at[layer],
-            weight_view(kind, self.wholes[kind], layer, place, place.dp, place.col),
-            self.send.at[group, step - 1],
-            self.recv.at[group, step - 1],
+            column_view(1, self.wholes[1], layer, place.col),
+            column_view(1, self.far, layer, place.col),
+            self.far_send.at[layer, 0],
+            self.far_recv.at[layer, 0],
+            place.y_peer,
+        )
+
+    def far_core_copy(self, layer):
+        view = column_view(1, self.far, layer, self.place.col)
+        return remote(
+            view, view, self.far_send.at[layer, 1], self.far_recv.at[layer, 1], self.place.c_peer
+        )
+
+    def far_start(self, layer):
+        self.own_copy(layer * KINDS + 1).wait()
+        self.far_copy(layer).start()
+
+    def far_in(self, layer):
+        self.far_copy(layer).wait_recv()
+        self.far_core_copy(layer).start()
+
+    def far_arrive(self, layer):
+        self.far_core_copy(layer).wait_recv()
+
+    def finish(self):
+        for group in range(GROUPS):
+            for step in range(self.place.line):
+                if step:
+                    self.line_copy(group, step).wait_send()
+                self.pair_copy(group, step).wait_send()
+                self.core_copy(group, step, 0).wait_send()
+                self.core_copy(group, step, 1).wait_send()
+        for layer in range(LAYERS):
+            self.far_copy(layer).wait_send()
+            self.far_core_copy(layer).wait_send()
+
+
+class Vectors:
+    def __init__(self, place, spot, raw, spare, send, recv):
+        self.place, self.spot, self.raw, self.spare = place, spot, raw, spare
+        self.send, self.recv = send, recv
+
+    def line_copy(self, step):
+        place = self.place
+        return remote(
+            self.spot,
+            self.raw.at[place.outer],
+            self.send.at[2 + step],
+            self.recv.at[2 + step],
             place.z_peer(step),
         )
 
-    def pair_copy(self, group, step):
-        layer, kind = divmod(group, KINDS)
-        place = self.place
-        view = weight_view(kind, self.wholes[kind], layer, place, place.behind(step), place.col)
-        at = place.line - 1 + step
-        return remote(
-            self.shards[kind].at[layer] if step == 0 else view,
-            view,
-            self.send.at[group, at],
-            self.recv.at[group, at],
-            place.x_peer,
-        )
-
-    def core_copy(self, group):
-        layer, kind = divmod(group, KINDS)
-        place = self.place
-        view = column_view(kind, self.wholes[kind], layer, place.col)
-        at = 2 * place.line - 1
-        return remote(
-            view, view, self.send.at[group, at], self.recv.at[group, at], place.c_peer
-        )
-
-    def own_copy(self, group):
-        layer, kind = divmod(group, KINDS)
-        place = self.place
-        return pltpu.make_async_copy(
-            self.shards[kind].at[layer],
-            weight_view(kind, self.wholes[kind], layer, place, place.dp, place.col),
-            self.own.at[group],
-        )
-
-    def start(self, group):
+    def start(self):
         for step in range(1, self.place.line):
-            self.line_copy(group, step).start()
-        self.pair_copy(group, 0).start()
-        self.own_copy(group).start()
-
-    def to_pair(self, group):
+            self.line_copy(step).start()
+        self.raw[self.place.outer] = self.spot[...]
+
+    def line_in(self):
         for step in range(1, self.place.line):
-            self.line_copy(group, step).wait_recv()
-            self.pair_copy(group, step).start()
-
-    def to_core(self, group):
-        self.own_copy(group).wait()
-        for step in range(self.place.line):
-            self.pair_copy(group, step).wait_recv()
-        self.core_copy(group).start()
-
-    def arrive(self, group):
-        self.core_copy(group).wait_recv()
-
-    def finish(self):
-        for group in range(GROUPS):
-            for step in range(1, self.place.line):
-                self.line_copy(group, step).wait_send()
-            for step in range(self.place.line):
-                self.pair_copy(group, step).wait_send()
-            self.core_copy(group).wait_send()
-
-
-def gather_vectors(place, spot, spare, raw, vecs, send, recv):
-    for at, peer in enumerate((place.c_peer, place.y_peer, place.x_peer)):
-        copy = remote(spot, spare.at[at], send.at[at], recv.at[at], peer)
+            self.line_copy(step).wait()
+
+    def add(self, at, peer):
+        copy = remote(self.raw, self.spare.at[at], self.send.at[at], self.recv.at[at], peer)
         copy.start()
         copy.wait()
-        spot[...] = spot[...] + spare[at]
-    copies = []
-    for step in range(1, place.line):
-        copy = remote(
-            spot, raw.at[place.outer], send.at[2 + step], recv.at[2 + step], place.z_peer(step)
-        )
-        copy.start()
-        copies.append(copy)
-    raw[place.outer] = spot[...]
-    for copy in copies:
-        copy.wait()
-    used = vecs.shape[1] // 128 // place.line
-    for outer in range(place.line):
-        for layer in range(LAYERS):
-            for at in range(used):
-                start = (outer * used + at) * 128
-                vecs[layer : layer + 1, start : start + 128] = raw[outer, layer, at : at + 1, :]
-
-
-def norm_rows(source, gain, shift, unit, inverse, target, rows):
-    size = 32
+        self.raw[...] = self.raw[...] + self.spare[at]
+
+    def spread(self, vecs):
+        size = self.spot.shape[1]
+        for outer in range(self.place.line):
+            vecs[:, outer * size : (outer + 1) * size] = self.raw[outer]
+
+
+def to_tokens(place, values, padded, arrived, target, send, recv):
+    rows = arrived.shape[0]
+    tokens, half = values.shape
+    padded[rows:, :] = jnp.zeros_like(padded[rows:, :])
+    padded[:tokens, :] = values[...]
+    copy = remote(
+        padded.at[pl.ds(aligned((1 - place.col) * rows, 16), rows), :],
+        arrived,
+        send,
+        recv,
+        place.c_peer,
+    )
+    copy.start()
+    own = padded[pl.ds(aligned(place.col * rows, 16), rows), :]
+    target[:, pl.ds(aligned(place.col * half), half)] = own.astype(target.dtype)
+    copy.wait()
+    other = pl.ds(aligned((1 - place.col) * half), half)
+    target[:, other] = arrived[...].astype(target.dtype)
+
+
+def to_features(place, values, arrived, target, send, recv):
+    rows = values.shape[0]
+    tokens, half = target.shape
+    copy = remote(
+        values.at[:, pl.ds(aligned((1 - place.col) * half), half)], arrived, send, recv, place.c_peer
+    )
+    copy.start()
+    own = values[:, pl.ds(aligned(place.col * half), half)]
+    copy.wait()
+    other = arrived[...]
+
+    @pl.when(place.col == 0)
+    def _():
+        target[:rows, :] = own
+        target[rows:, :] = other[: tokens - rows]
+
+    @pl.when(place.col == 1)
+    def _():
+        target[:rows, :] = other
+        target[rows:, :] = own[: tokens - rows]
+
+
+def norm_rows(source, gain, shift, unit, inverse, target, start, rows):
+    size = 16
 
     def step(at, carry):
-        place = pl.ds(aligned(at * size, size), size)
+        place = pl.ds(aligned(start + at * size, size), size)
         values = source[place, :].astype(f32)
         centre = jnp.sum(values, 1, keepdims=True) * (1.0 / D)
         spread = jnp.sum(values * values, 1, keepdims=True) * (1.0 / D) - centre * centre
@@ -258,9 +340,10 @@
     return values * normal, normal + values * density
 
 
-def forward_kernel(count, tokens, *refs):
+def forward_kernel(count, *refs):
     (
-        state_in,
+        images,
+        cotangent,
         spot_in,
         bias_in,
         shard_a,
@@ -271,6 +354,7 @@
         w_b,
         w_c,
         w_d,
+        w_far,
         vecs_out,
         unit_one_out,
         inv_one_out,
@@ -286,8 +370,12 @@
         slope_out,
         output_out,
         head_mix_out,
+        back_out_out,
+        cotangent_out,
         block_out,
         state,
+        padded,
+        arrived,
         spot,
         spare,
         raw,
@@ -296,6 +384,7 @@
         wm,
         wu,
         wd,
+        wf,
         unit,
         inverse,
         unit_two,
@@ -307,6 +396,8 @@
         head_mix,
         lse,
         mixed_all,
+        mixed_far,
+        back_out,
         branch,
         output,
         active,
@@ -317,6 +408,8 @@
         g_send,
         g_recv,
         g_own,
+        far_send,
+        far_recv,
         v_send,
         v_recv,
         y_send,
@@ -326,19 +419,85 @@
         stage_sem,
         save_sem,
     ) = refs
-    rows = state_in.shape[0]
+    tokens = images.shape[0]
+    rows = state.shape[0]
     group = 2 * rows
     half = D // 2
     width = half // 2
     place = Place(count)
     row, col = place.row, place.col
     wholes = (w_a, w_b, w_c, w_d)
-    gather = Gather(place, (shard_a, shard_b, shard_c, shard_d), wholes, g_send, g_recv, g_own)
+    gather = Gather(
+        place,
+        (shard_a, shard_b, shard_c, shard_d),
+        wholes,
+        w_far,
+        {
+            "send": g_send,
+            "recv": g_recv,
+            "own": g_own,
+            "far_send": far_send,
+            "far_recv": far_recv,
+        },
+    )
     place.greet()
-    gather.start(0)
-    gather.start(1)
+    spot[...] = spot_in[...]
+    vectors = Vectors(place, spot, raw, spare, v_send, v_recv)
+    vectors.start()
+    for at in range(WINDOW):
+        gather.line_out(at)
+
+    plan = []
+    due = [4.0]
+    for at in range(GROUPS):
+        dims = wholes[at % KINDS].shape
+        due.append(due[-1] + 1.1 * (dims[1] * dims[2] / 92e3))
+    for at in range(GROUPS):
+        begin, span = due[at], due[at + 1] - due[at]
+        for step in range(1, place.line):
+            line_due = begin + span * (0.3 + 0.7 * step / (place.line - 1))
+            plan.append((line_due, 1, gather.line_in, (at, step)))
+            if 0 < at < GROUPS - 1 and step == 1:
+                plan.append((line_due, 0.5, gather.own_out, (at + 1,)))
+            if at + WINDOW < GROUPS and step == max(1, round(TRIGGER * (place.line - 1))):
+                plan.append((line_due, 1.5, gather.line_out, (at + WINDOW,)))
+        for step in range(place.line):
+            pair_due = begin + span * (0.6 + 0.7 * step / (place.line - 1)) + 2.0
+            plan.append((pair_due, 2, gather.pair_in, (at, step)))
+    plan.sort(key=lambda item: item[:2])
+    last_of = [
+        max(
+            spot
+            for spot, item in enumerate(plan)
+            if item[2] == gather.pair_in and item[3] == (at, place.line - 1)
+        )
+        for at in range(GROUPS)
+    ]
+    plan_at = [0]
+
+    def advance(until):
+        for item in plan[plan_at[0] : until]:
+            item[2](*item[3])
+        plan_at[0] = max(until, plan_at[0])
+
+    def pump(time):
+        advance(sum(1 for item in plan if item[0] <= time + LEAD))
+
+    def ensure(at):
+        advance(last_of[at] + 1)
+
+    def pump_step(at, count_steps, begin, step_time):
+        for step in range(count_steps):
+            until = sum(1 for item in plan if item[0] <= begin + (step + 1) * step_time + LEAD)
+            if until > plan_at[0]:
+                pl.when(at == step)(functools.partial(advance, until))
 
     pending = {}
+
+    def settle(*names):
+        for name in names:
+            if name in pending:
+                pending.pop(name).wait()
 
     def save(name, at, source, target):
         settle(name)
@@ -346,19 +505,26 @@
         copy.start()
         pending[name] = copy
 
-    def settle(*names):
-        for name in names:
-            if name in pending:
-                pending.pop(name).wait()
-
     staged = {}
+    buffers = (wq, wm, wu, wd)
 
     def stage(kind, layer):
-        gather.arrive(layer * KINDS + kind)
-        buffer = (wq, wm, wu, wd)[kind]
-        copy = pltpu.make_async_copy(wholes[kind].at[layer], buffer, stage_sem.at[kind])
+        at = layer * KINDS + kind
+        if kind == 1:
+            for pair in range(2):
+                for step in range(place.line):
+                    gather.core_copy(at, step, pair).wait_recv()
+        else:
+            gather.arrive(at)
+        copy = pltpu.make_async_copy(wholes[kind].at[layer], buffers[kind], stage_sem.at[kind])
         copy.start()
         staged[kind] = copy
+
+    def stage_far(layer):
+        gather.far_arrive(layer)
+        copy = pltpu.make_async_copy(w_far.at[layer], wf, stage_sem.at[KINDS])
+        copy.start()
+        staged[KINDS] = copy
 
     def ready(kind):
         staged.pop(kind).wait()
@@ -368,45 +534,37 @@
     def y_copy(source, target):
         at = y_at[0]
         y_at[0] += 1
-        return remote(source, target, y_send.at[at], y_recv.at[at], place.y_peer)
+        copy = remote(source, target, y_send.at[at], y_recv.at[at], place.y_peer)
+        copy.start()
+        return copy
+
+    c_at = [0]
+
+    def c_copy(source, target):
+        at = c_at[0]
+        c_at[0] += 1
+        copy = remote(source, target, c_send.at[at], c_recv.at[at], place.c_peer)
+        copy.start()
+        return copy
 
     chunk = rows // SPLIT
 
-    def exchange_rows(buffer):
-        copies = []
-        for at in range(SPLIT):
-            copies.append(
-                y_copy(
-                    buffer.at[pl.ds(at * chunk, chunk), :],
-                    buffer.at[pl.ds(rows + at * chunk, chunk), :],
-                )
-            )
-            copies[-1].start()
-        return copies
-
-    spot[...] = spot_in[...]
-    state[...] = state_in[...].astype(f32)
-    gather_vectors(place, spot, spare, raw, vecs, v_send, v_recv)
+    def send_rows(buffer, at):
+        return y_copy(
+            buffer.at[pl.ds(at * chunk, chunk), :],
+            buffer.at[pl.ds(rows + at * chunk, chunk), :],
+        )
+
+    to_tokens(place, images, padded, arrived, state, c_send.at[0], c_recv.at[0])
+    c_at[0] = 2
+    vectors.line_in()
+    vectors.add(0, place.x_peer)
+    gather.own_out(0)
+    gather.own_out(1)
+    vectors.add(1, place.y_peer)
+    vectors.add(2, place.c_peer)
+    vectors.spread(vecs)
     save("vecs", 11, vecs, vecs_out)
-    gather.to_pair(0)
-    gather.start(2)
-
-    plan = {
-        (0, "norm"): ((gather.to_core, 0), (stage, 0, 0), (gather.to_pair, 1), (gather.start, 3)),
-        (0, "triple"): ((gather.to_core, 1),),
-        (0, "attend"): ((gather.to_pair, 2), (stage, 1, 0), (gather.start, 4)),
-        (0, "project"): ((gather.to_core, 2),),
-        (0, "branch"): ((gather.to_pair, 3), (gather.start, 5), (stage, 2, 0)),
-        (0, "expand"): ((gather.to_core, 3), (gather.start, 6)),
-        (0, "shrink"): ((gather.to_pair, 4),),
-        (0, "output"): ((gather.to_core, 4), (stage, 0, 1), (gather.to_pair, 5), (gather.start, 7)),
-        (1, "norm"): ((gather.to_core, 5),),
-        (1, "triple"): ((stage, 1, 1), (gather.to_pair, 6)),
-        (1, "attend"): ((gather.to_core, 6),),
-        (1, "project"): ((gather.to_pair, 7),),
-        (1, "branch"): ((stage, 2, 1),),
-        (1, "expand"): ((gather.to_core, 7),),
-    }
 
     lane = lax.broadcasted_iota(jnp.int32, (1, 128), 1) < HEAD_DIM
     valid = lax.broadcasted_iota(jnp.int32, (rows, 1), 0) < tokens - col * rows
@@ -414,81 +572,94 @@
     def vector(layer, at):
         return vecs[layer : layer + 1, at * D : (at + 1) * D]
 
+    def norm_one(layer, at):
+        norm_rows(
+            state, vector(layer, 0), vector(layer, 1), unit, inverse, normed, at * chunk, chunk
+        )
+        return send_rows(normed, at)
+
+    copies = [norm_one(0, at) for at in range(SPLIT)]
+    to_tokens(place, cotangent, padded, arrived, branch, c_send.at[1], c_recv.at[1])
+    cotangent_out[...] = branch[...].astype(bf16)
+    back_out[:rows, :] = (vector(LAYERS - 1, 13) * branch[...]).astype(bf16)
+    out_copies = [send_rows(back_out, at) for at in range(SPLIT)]
     for layer in range(LAYERS):
-
-        def pump(name, layer=layer):
-            for action, *args in plan.get((layer, name), ()):
-                action(*args)
-
-        settle("unit", "inverse", "normed")
-        norm_rows(state, vector(layer, 0), vector(layer, 1), unit, inverse, normed, rows)
-        copies = exchange_rows(normed)
+        first = layer == 0
+        heads, mixed = heads_all.at[layer], mixed_all.at[layer]
         save("unit", 0, unit, unit_one_out.at[layer])
         save("inverse", 1, inverse, inv_one_out.at[layer])
-        pump("norm")
+        if first:
+            ensure(0)
+            stage(0, 0)
         ready(0)
-        heads, mixed = heads_all.at[layer], mixed_all.at[layer]
-
-        def triple(start):
+
+        def triple(start, size):
             def step(at, carry):
                 part_at = lax.rem(at, 3)
                 mine = lax.div(at, 3)
                 owner = jnp.where(mine == 1, col, 1 - col)
                 column = aligned(part_at * half + owner * width)
-                value = nn(normed[start : start + rows, :], wq[:, pl.ds(column, width)])
+                value = nn(normed[start : start + size, :], wq[:, pl.ds(column, width)])
                 bias_at = aligned(
                     jnp.where(part_at == 2, 3 * D, 2 * D) + row * half + owner * width
                 )
                 bias = vecs[layer : layer + 1, pl.ds(bias_at, width)]
                 bias = bias * jnp.where(part_at == 1, 0.0, 1.0)
-                value = jnp.where(valid, value + bias, 0.0).astype(bf16)
+                inside = valid[start % rows : start % rows + size]
+                value = jnp.where(inside, value + bias, 0.0).astype(bf16)
                 lanes = pl.ds(aligned(part_at * width), width)
 
                 @pl.when(mine == 0)
                 def _():
-                    head_tx[start : start + rows, lanes] = value
+                    head_tx[start : start + size, lanes] = value
 
                 @pl.when(mine == 1)
                 def _():
-                    heads[pl.ds(aligned(col * group + start, 16), rows), lanes] = value
+                    heads[pl.ds(aligned(col * group + start, 16), size), lanes] = value
 
                 return carry
 
             lax.fori_loop(0, 6, step, 0)
-
-        core_copies = []
-
-        def send_heads(start):
-            at = layer * 3 + (start > 0)
-            core_copies.append(
-                remote(
-                    head_tx.at[pl.ds(start, rows), :],
-                    heads.at[pl.ds(aligned(col * group + start, 16), rows), :],
-                    c_send.at[at],
-                    c_recv.at[at],
-                    place.c_peer,
-                )
+            return c_copy(
+                head_tx.at[pl.ds(start, size), :],
+                heads.at[pl.ds(aligned(col * group + start, 16), size), :],
             )
-            core_copies[-1].start()
-
-        triple(0)
-        send_heads(0)
-        for copy in copies:
-            copy.wait()
+
+        core_copies = [triple(0, rows)]
+        if first:
+            ensure(1)
+            gather.far_start(0)
+            for copy in copies:
+                copy.wait()
+            core_copies.append(triple(rows, rows))
+            pump(33)
+        else:
+            ensure(5)
+            gather.far_start(1)
+            stage(1, 1)
+            pump(106)
+            copies[0].wait()
+            core_copies.append(triple(rows, chunk))
+            pump(111)
+            copies[1].wait()
+            core_copies.append(triple(rows + chunk, chunk))
+            pump(119)
         save("normed", 2, normed, normed_out.at[layer])
-        triple(rows)
-        send_heads(rows)
-        pump("triple")
         for copy in core_copies:
             copy.wait()
         save("heads", 3, heads, heads_out.at[layer])
         settle("lse", "head_mix")
 
-        def attend(owner):
+        attend_at = [35.0 if first else 121.0]
+
+        def attend(owner, side):
+            begin_time = attend_at[0]
+            attend_at[0] += 3.4
             tile = rows // 2
+            begin = owner * group + side * rows
 
             def step(at, carry):
-                place_rows = pl.ds(aligned(owner * group + at * tile, 16), tile)
+                place_rows = pl.ds(aligned(begin + at * tile, 16), tile)
                 for pair in range(width // 128):
                     lanes = slice(pair * 128, pair * 128 + 128)
                     query = heads[place_rows, lanes] * jnp.asarray(HEAD_DIM**-0.5, bf16)
@@ -508,65 +679,87 @@
                         lane, result[:tile], result[tile:]
                     ).astype(bf16)
                     lse[place_rows, lanes] = jnp.where(lane, logsum[:tile], logsum[tile:])
+                pump_step(at, rows // tile, begin_time, 1.7)
                 return carry
 
-            lax.fori_loop(0, group // tile, step, 0)
-
-        attend(1 - col)
-        lanes = pl.ds(aligned(col * width), width)
-        back = remote(
-            head_mix.at[pl.ds(aligned((1 - col) * group, 16), group), :],
-            mixed.at[:, lanes],
-            c_send.at[layer * 3 + 2],
-            c_recv.at[layer * 3 + 2],
-            place.c_peer,
-        )
-        back.start()
-        pump("attend")
-        attend(col)
-        mixed[:, lanes] = head_mix[pl.ds(aligned(col * group, 16), group), :]
-        back.wait()
+            lax.fori_loop(0, rows // tile, step, 0)
+            plan_at[0] = max(plan_at[0], sum(1 for item in plan if item[0] <= attend_at[0] + LEAD))
+
+        my_lanes = pl.ds(aligned(col * width), width)
+
+        def send_mixed(side):
+            return c_copy(
+                head_mix.at[pl.ds(aligned((1 - col) * group + side * rows, 16), rows), :],
+                mixed.at[pl.ds(side * rows, rows), my_lanes],
+            )
+
+        def keep_mixed(side):
+            mixed[side * rows : side * rows + rows, my_lanes] = head_mix[
+                pl.ds(aligned(col * group + side * rows, 16), rows), :
+            ]
+
+        attend(1 - col, 1)
+        copy = send_mixed(1)
+        attend(col, 1)
+        keep_mixed(1)
+        copy.wait()
+        settle("normed_two")
+        far_copy = y_copy(mixed.at[pl.ds(rows, rows), :], mixed_far)
+        if first:
+            stage(1, 0)
+        attend(1 - col, 0)
+        copy = send_mixed(0)
+        gather.far_in(layer)
+        attend(col, 0)
+        keep_mixed(0)
+        copy.wait()
         save("lse", 4, lse, lse_out.at[layer])
         save("head_mix", 14, head_mix, head_mix_out.at[layer])
         save("mixed", 5, mixed, mixed_out.at[layer])
+        stage_far(layer)
         ready(1)
-        pump("project")
-        settle("normed_two")
-
-        def project(start, size, target, target_at):
+        settle("branch", "unit_two", "inverse_two")
+
+        def project(start):
             def step(at, carry):
                 lanes = pl.ds(aligned(at * half), half)
-                value = nn(mixed[start : start + size, :], wm[:, lanes])
-                target[pl.ds(target_at, size), lanes] = value.astype(target.dtype)
+                value = nn(mixed[start : start + chunk, :], wm[:, lanes])
+                value = value + nn(mixed_far[start : start + chunk, :], wf[:, lanes])
+                bias_at = aligned(4 * D + at * half)
+                value = value + vecs[layer : layer + 1, pl.ds(bias_at, half)]
+                scale = vecs[layer : layer + 1, pl.ds(aligned(5 * D + at * half), half)]
+                branch[start : start + chunk, lanes] = value
+                state[start : start + chunk, lanes] += scale * value
                 return carry
 
             lax.fori_loop(0, 2, step, 0)
 
+        far_copy.wait()
+        ready(KINDS)
         copies = []
         for at in range(SPLIT):
-            project(rows + at * chunk, chunk, tx, at * chunk)
-            view = pl.ds(at * chunk, chunk)
-            copies.append(y_copy(tx.at[view, :], rx.at[view, :]))
-            copies[-1].start()
-        project(0, rows, part, 0)
-        pump("branch")
-        for copy in copies:
-            copy.wait()
-        settle("branch", "unit_two", "inverse_two")
-        branch[...] = part[...] + rx[...].astype(f32) + vector(layer, 4)
-        state[...] = state[...] + vector(layer, 5) * branch[...]
+            project(at * chunk)
+            norm_rows(
+                state,
+                vector(layer, 6),
+                vector(layer, 7),
+                unit_two,
+                inverse_two,
+                normed_two,
+                at * chunk,
+                chunk,
+            )
+            copies.append(send_rows(normed_two, at))
+            pump((50 if first else 137) + at * 1.5)
+        ensure(2 if first else 6)
+        stage(2, layer)
         save("branch", 6, branch, branch_out.at[layer])
-        norm_rows(
-            state, vector(layer, 6), vector(layer, 7), unit_two, inverse_two, normed_two, rows
-        )
-        copies = exchange_rows(normed_two)
         save("unit_two", 7, unit_two, unit_two_out.at[layer])
         save("inverse_two", 8, inverse_two, inv_two_out.at[layer])
-        pump("expand")
         ready(2)
-        settle("active", "slope")
-
-        def expand(start, size):
+        settle("active", "slope", "normed")
+
+        def expand(start, size, begin_time):
             def step(at, carry):
                 lanes = pl.ds(aligned(at * half), half)
                 bias_at = aligned(8 * D + row * (FF // 2) + at * half)
@@ -575,9 +768,12 @@
                 act, grad = gelu_both(value)
                 active[start : start + size, lanes] = act.astype(bf16)
                 slope[start : start + size, lanes] = grad.astype(bf16)
+                pump_step(at, FF // 2 // half, begin_time, 0.8)
                 return carry
 
             lax.fori_loop(0, FF // 2 // half, step, 0)
+            end = begin_time + FF // 2 // half * 0.8 + LEAD
+            plan_at[0] = max(plan_at[0], sum(1 for item in plan if item[0] <= end))
 
         def shrink(start, size, target, target_at):
             def step(at, carry):
@@ -588,38 +784,73 @@
 
             lax.fori_loop(0, 2, step, 0)
 
-        expand(0, rows)
-        stage(3, layer)
-        settle("normed")
-        ready(3)
+        def shrink_send(at):
+            shrink(rows + at * chunk, chunk, tx, at * chunk)
+            view = pl.ds(at * chunk, chunk)
+            return y_copy(tx.at[view, :], rx.at[view, :])
+
+        back_copies = []
+        if first:
+            expand(0, rows, 56.0)
+            copies[0].wait()
+            expand(rows, chunk, 63.0)
+            copies[1].wait()
+            expand(rows + chunk, chunk, 71.0)
+            ensure(3)
+            stage(3, 0)
+            ready(3)
+            back_copies.append(shrink_send(0))
+            back_copies.append(shrink_send(1))
+        else:
+            expand(0, rows, 139.0)
+            copies[0].wait()
+            expand(rows, chunk, 146.0)
+            ensure(7)
+            stage(3, 1)
+            ready(3)
+            back_copies.append(shrink_send(0))
+            copies[1].wait()
+            expand(rows + chunk, chunk, 160.0)
+            back_copies.append(shrink_send(1))
         shrink(0, rows, part, 0)
-        pump("shrink")
-        back_copies = []
-        for at in range(SPLIT):
-            copies[at].wait()
-            start = rows + at * chunk
-            expand(start, chunk)
-            shrink(start, chunk, tx, at * chunk)
-            view = pl.ds(at * chunk, chunk)
-            back_copies.append(y_copy(tx.at[view, :], rx.at[view, :]))
-            back_copies[-1].start()
         save("normed_two", 9, normed_two, normed_two_out.at[layer])
         save("active", 10, active, active_out.at[layer])
         save("slope", 12, slope, slope_out.at[layer])
-        pump("output")
-        for copy in back_copies:
-            copy.wait()
-        settle("output")
-        output[...] = part[...] + rx[...].astype(f32) + vector(layer, 12)
-        state[...] = state[...] + vector(layer, 13) * output[...]
+        if first:
+            pump(87)
+        else:
+            for copy in out_copies:
+                copy.wait()
+            save("back_out", 15, back_out, back_out_out)
+        settle("output", "unit", "inverse")
+        next_copies = []
+        for at in range(SPLIT):
+            back_copies[at].wait()
+            here = slice(at * chunk, at * chunk + chunk)
+            output[here, :] = part[here, :] + rx[here, :].astype(f32) + vector(layer, 12)
+            state[here, :] = state[here, :] + vector(layer, 13) * output[here, :]
+            if first:
+                next_copies.append(norm_one(1, at))
+                if at == 0:
+                    pump(94)
         save("output", 13, output, output_out.at[layer])
-    block_out[...] = state[...].astype(bf16)
+        if first:
+            ensure(4)
+            stage(0, 1)
+        copies = next_copies
+    tx[...] = state[...].astype(bf16)
+    to_features(place, tx, arrived, block_out, c_send.at[15], c_recv.at[15])
     gather.finish()
     settle(*list(pending))
 
 
-def forward_call(mesh_count, tokens, state, spot, bias, shards):
-    rows = state.shape[0]
+def padded_rows(tokens):
+    return -(-tokens // (2 * TILE)) * TILE
+
+
+def forward_call(mesh_count, images, cotangent, spot, bias, shards):
+    tokens = images.shape[0]
+    rows = padded_rows(tokens)
     group = 2 * rows
     half = D // 2
     width = half // 2
@@ -633,6 +864,7 @@
         shape(LAYERS, half, D, kind=bf16),
         shape(LAYERS, D, FF // 2, kind=bf16),
         shape(LAYERS, FF // 2, D, kind=bf16),
+        shape(LAYERS, half, D, kind=bf16),
         shape(LAYERS, 10 * D + FF),
         shape(LAYERS, rows, D),
         shape(LAYERS, rows, 128),
@@ -648,19 +880,24 @@
         shape(LAYERS, group, FF // 2, kind=bf16),
         shape(LAYERS, rows, D),
         shape(LAYERS, 2 * group, width, kind=bf16),
+        shape(group, D, kind=bf16),
         shape(rows, D, kind=bf16),
+        shape(tokens, half, kind=bf16),
     ]
     dma = pltpu.SemaphoreType.DMA
     scratch = [
         pltpu.VMEM((rows, D), f32),
+        pltpu.VMEM((group, half), bf16),
+        pltpu.VMEM((rows, half), bf16),
         pltpu.VMEM(spot.shape, f32),
-        pltpu.VMEM((3,) + spot.shape, f32),
+        pltpu.VMEM((3, line) + spot.shape, f32),
         pltpu.VMEM((line,) + spot.shape, f32),
         pltpu.VMEM((LAYERS, 10 * D + FF), f32),
         pltpu.VMEM((D, 3 * half), bf16),
         pltpu.VMEM((half, D), bf16),
         pltpu.VMEM((D, FF // 2), bf16),
         pltpu.VMEM((FF // 2, D), bf16),
+        pltpu.VMEM((half, D), bf16),
         pltpu.VMEM((rows, D), f32),
         pltpu.VMEM((rows, 128), f32),
         pltpu.VMEM((rows, D), f32),
@@ -672,6 +909,8 @@
         pltpu.VMEM((2 * group, width), bf16),
         pltpu.VMEM((2 * group, width), f32),
         pltpu.VMEM((LAYERS, group, half), bf16),
+        pltpu.VMEM((rows, half), bf16),
+        pltpu.VMEM((group, D), bf16),
         pltpu.VMEM((rows, D), f32),
         pltpu.VMEM((rows, D), f32),
         pltpu.VMEM((group, FF // 2), bf16),
@@ -679,29 +918,31 @@
         pltpu.VMEM((rows, D), bf16),
         pltpu.VMEM((rows, D), bf16),
         pltpu.VMEM((rows, D), f32),
-        dma((GROUPS, 2 * line)),
-        dma((GROUPS, 2 * line)),
+        dma((GROUPS, 4 * line - 1)),
+        dma((GROUPS, 4 * line - 1)),
         dma((GROUPS,)),
+        dma((LAYERS, 2)),
+        dma((LAYERS, 2)),
         dma((line + 2,)),
         dma((line + 2,)),
-        dma((LAYERS * 4 * SPLIT,)),
-        dma((LAYERS * 4 * SPLIT,)),
-        dma((LAYERS * 3,)),
-        dma((LAYERS * 3,)),
-        dma((KINDS,)),
-        dma((15,)),
+        dma((16,)),
+        dma((16,)),
+        dma((16,)),
+        dma((16,)),
+        dma((KINDS + 1,)),
+        dma((16,)),
     ]
     return pl.pallas_call(
-        functools.partial(forward_kernel, mesh_count, tokens),
+        functools.partial(forward_kernel, mesh_count),
         out_shape=outs,
-        in_specs=[WHOLE] * 3 + [ANY] * 4,
-        out_specs=[ANY] * 19 + [WHOLE],
+        in_specs=[WHOLE] * 8,
+        out_specs=[ANY] * 21 + [WHOLE] * 2,
         scratch_shapes=scratch,
         compiler_params=pltpu.CompilerParams(
             collective_id=0, has_side_effects=True, vmem_limit_bytes=60 << 20
         ),
         name="forward",
-    )(state, spot, bias, *shards)
+    )(images, cotangent, spot, bias, *shards)
 
 
 def fold(values):
@@ -748,17 +989,17 @@
             place.x_peer,
         )
 
-    def z_copy(self, layer, kind, step):
+    def z_copy(self, layer, kind, outer):
         place = self.place
         size = self.size(kind)
         at = layer * KINDS + kind
-        outer = lax.rem(place.outer + step, place.line)
+        step = lax.rem(outer - place.outer + place.line, place.line)
         return remote(
             self.pair_rx[kind].at[pl.ds(aligned(outer * size, 16), size), :],
             self.line_rx[kind].at[step - 1],
             self.z_send.at[at, step - 1],
             self.z_recv.at[at, step - 1],
-            place.z_peer(step),
+            (2 * outer + place.pair, place.row, place.col),
         )
 
     def x_start(self, layer, kind):
@@ -770,31 +1011,31 @@
     def x_finish(self, layer, kind):
         place = self.place
         size = self.size(kind)
+        rows = min(size, 64)
+        if layer < LAYERS - 1:
+            pl.semaphore_wait(self.z_free.at[kind], place.line - 1)
         for outer in range(place.line):
             self.x_copy(layer, kind, outer).wait()
-        rows = min(size, 64)
-
-        def step(at, carry):
-            outer = lax.div(at, size // rows)
-            inner = lax.rem(at, size // rows)
-            here = pl.ds(aligned(outer * size + inner * rows, 16), rows)
-            own = pl.ds(aligned((2 * outer + place.pair) * size + inner * rows, 16), rows)
-            pair_rx = self.pair_rx[kind]
-            value = pair_rx[here, :].astype(f32) + self.sums[kind][own, :].astype(f32)
-            pair_rx[here, :] = value.astype(bf16)
-            return carry
-
-        lax.fori_loop(0, place.line * (size // rows), step, 0)
-        if layer < LAYERS - 1:
-            pl.semaphore_wait(self.z_free.at[kind], place.line - 1)
-        for step_at in range(1, place.line):
-            self.z_copy(layer, kind, step_at).start()
+
+            def step(at, carry, outer=outer):
+                here = pl.ds(aligned(outer * size + at * rows, 16), rows)
+                own = pl.ds(aligned((2 * outer + place.pair) * size + at * rows, 16), rows)
+                pair_rx = self.pair_rx[kind]
+                value = pair_rx[here, :].astype(f32) + self.sums[kind][own, :].astype(f32)
+                pair_rx[here, :] = value.astype(bf16)
+                return carry
+
+            lax.fori_loop(0, size // rows, step, 0)
+
+            @pl.when(place.outer != outer)
+            def _(outer=outer):
+                self.z_copy(layer, kind, outer).start()
 
     def z_finish(self, layer, kind):
         place = self.place
         size = self.size(kind)
         for step_at in range(1, place.line):
-            self.z_copy(layer, kind, step_at).wait()
+            self.z_copy(layer, kind, lax.rem(place.outer + step_at, place.line)).wait()
         if kind in self.writing:
             self.writing.pop(kind).wait()
         rows = min(size, 64)
@@ -805,7 +1046,12 @@
             value = self.pair_rx[kind][own, :].astype(f32)
             for step_at in range(place.line - 1):
                 value = value + self.line_rx[kind][step_at, here, :].astype(f32)
-            self.result[kind][here, :] = value
+            if kind == 0:
+                third = value.shape[1] // 3
+                for part_at in range(3):
+                    self.result[kind][part_at, here, :] = value[:, part_at * third : (part_at + 1) * third]
+            else:
+                self.result[kind][here, :] = value
             return carry
 
         lax.fori_loop(0, size // rows, step, 0)
@@ -832,13 +1078,9 @@
 
 
 def scatter_vectors(place, grads, packed, spare, spot, target, send, recv):
-    used = grads.shape[1] // 128 // place.line
-    packed[...] = jnp.zeros_like(packed)
+    size = spot.shape[1]
     for outer in range(place.line):
-        for layer in range(LAYERS):
-            for at in range(used):
-                start = (outer * used + at) * 128
-                packed[outer, layer, at : at + 1, :] = grads[layer : layer + 1, start : start + 128]
+        packed[outer] = grads[:, outer * size : (outer + 1) * size]
     copies = []
     for step in range(1, place.line):
         outer = lax.rem(place.outer + step, place.line)
@@ -861,7 +1103,7 @@
     target[...] = spot[...]
 
 
-def backward_kernel(count, tokens, *refs):
+def backward_kernel(count, *refs):
     (
         grad_in,
         vecs,
@@ -883,6 +1125,7 @@
         slope_in,
         output_in,
         head_mix_in,
+        back_out_in,
         grad_a,
         grad_b,
         grad_c,
@@ -950,6 +1193,7 @@
         v_recv,
         load_sem,
     ) = refs
+    tokens = grad_out.shape[0]
     rows = grad_in.shape[0]
     group = 2 * rows
     half = D // 2
@@ -997,6 +1241,7 @@
         "lse": (lse_in, lse),
         "head_mix": (head_mix_in, head_mix),
         "mixed": (mixed_in, mixed),
+        "back_out": (back_out_in, back_out),
     }
     names = list(sources)
     loading = {}
@@ -1004,9 +1249,9 @@
     def load(layer, *wanted):
         for name in wanted:
             source, buffer = sources[name]
-            copy = pltpu.make_async_copy(
-                source.at[layer], buffer, load_sem.at[names.index(name)]
-            )
+            if name != "back_out":
+                source = source.at[layer]
+            copy = pltpu.make_async_copy(source, buffer, load_sem.at[names.index(name)])
             copy.start()
             loading[name] = copy
 
@@ -1019,7 +1264,9 @@
     def y_copy(source, target):
         at = y_at[0]
         y_at[0] += 1
-        return remote(source, target, y_send.at[at], y_recv.at[at], place.y_peer)
+        copy = remote(source, target, y_send.at[at], y_recv.at[at], place.y_peer)
+        copy.start()
+        return copy
 
     c_at = [0]
 
@@ -1030,19 +1277,17 @@
 
     chunk = rows // SPLIT
 
-    def exchange_rows(buffer):
-        copies = []
-        for at in range(SPLIT):
-            copies.append(
-                y_copy(
-                    buffer.at[pl.ds(at * chunk, chunk), :],
-                    buffer.at[pl.ds(rows + at * chunk, chunk), :],
-                )
-            )
-            copies[-1].start()
-        return copies
-
-    load(1, "slope", "wd", "output", "wu", "normed_two", "active", "unit_two", "inv_two")
+    def send_rows(buffer, at):
+        return y_copy(
+            buffer.at[pl.ds(at * chunk, chunk), :],
+            buffer.at[pl.ds(rows + at * chunk, chunk), :],
+        )
+
+    def send_part(at):
+        view = pl.ds(at * chunk, chunk)
+        return y_copy(tx.at[view, :], rx.at[view, :])
+
+    load(1, "back_out", "wd", "slope", "wu", "output", "active", "normed_two", "unit_two", "inv_two")
     load(1, "wm", "mixed", "heads", "lse", "head_mix", "wq")
     grad[...] = grad_in[...].astype(f32)
     vec_grads[...] = jnp.zeros_like(vec_grads)
@@ -1053,17 +1298,17 @@
         ((pick_row == 0) & (pick_lane < HEAD_DIM)) | ((pick_row == 1) & (pick_lane >= HEAD_DIM))
     ).astype(bf16)
     firsts = (pick_lane == pick_row * HEAD_DIM).astype(bf16)
-    size = 32
+    size = 16
 
     def vector(layer, at):
         return vecs[layer : layer + 1, at * D : (at + 1) * D]
 
     def note(layer, at, value):
-        vec_grads[layer : layer + 1, at * D : (at + 1) * D] = value
-
-    def by_rows(count_rows, body, terms):
+        vec_grads[layer : layer + 1, at * D : (at + 1) * D] += value
+
+    def by_rows(start, count_rows, body, terms):
         def step(at, carry):
-            adds = body(pl.ds(aligned(at * size, size), size))
+            adds = body(pl.ds(aligned(start + at * size, size), size))
             return tuple(old + fold(new) for old, new in zip(carry, adds, strict=True))
 
         zeros = tuple(jnp.zeros((8, D), f32) for _ in range(terms))
@@ -1116,22 +1361,23 @@
         lax.fori_loop(0, half_tiles(kind), step, 0)
         scatter.x_start(layer, kind)
 
+    def out_rows(layer, start, count_rows):
+        def body(here):
+            value = grad[here, :]
+            back = (vector(layer, 13) * value).astype(bf16)
+            if layer < LAYERS - 1:
+                back_out[here, :] = back
+            return (value * aside[here, :], back.astype(f32))
+
+        for at, value in zip((13, 12), by_rows(start, count_rows, body, 2), strict=True):
+            note(layer, at, value)
+
     for layer in reversed(range(LAYERS)):
         last = layer == LAYERS - 1
-        loaded("output")
-
-        def out_rows(here):
-            value = grad[here, :]
-            back = (vector(layer, 13) * value).astype(bf16)
-            back_out[here, :] = back
-            return (value * aside[here, :], back.astype(f32))
-
-        scale_grad, bias_grad = by_rows(rows, out_rows, 2)
-        copies = exchange_rows(back_out)
-        note(layer, 13, scale_grad)
-        note(layer, 12, bias_grad)
-        load(layer, "branch")
-        if not last:
+        if last:
+            loaded("back_out")
+        else:
+            load(0, "branch")
             scatter.z_finish(1, 3)
             scatter.z_finish(1, 2)
         loaded("slope", "wd")
@@ -1158,19 +1404,24 @@
 
             lax.fori_loop(0, 2, step, 0)
 
-        inner_rows(0, rows)
-        loaded("wu")
-        if not last:
-            scatter.x_finish(1, 1)
-        back_copies = []
-        for at in range(SPLIT):
-            copies[at].wait()
+        def back_chunk(at):
             start = rows + at * chunk
             inner_rows(start, chunk)
             two_rows(start, chunk, tx, at * chunk)
-            view = pl.ds(at * chunk, chunk)
-            back_copies.append(y_copy(tx.at[view, :], rx.at[view, :]))
-            back_copies[-1].start()
+            return send_part(at)
+
+        if last:
+            loaded("wu")
+            back_copies = [back_chunk(at) for at in range(SPLIT)]
+            inner_rows(0, rows)
+        else:
+            inner_rows(0, rows)
+            loaded("wu")
+            scatter.x_finish(1, 1)
+            back_copies = []
+            for at in range(SPLIT):
+                out_copies[at].wait()
+                back_copies.append(back_chunk(at))
         two_rows(0, rows, part, 0)
         if last:
             load(0, "wd")
@@ -1182,8 +1433,10 @@
         produce_own(layer, 3)
         produce_own(layer, 2)
         load(layer, "normed")
-        for copy in back_copies:
-            copy.wait()
+        if last:
+            loaded("output")
+            out_rows(layer, 0, rows)
+            load(1, "branch")
         loaded("unit_two", "inv_two", "branch")
 
         def middle_rows(here):
@@ -1199,10 +1452,13 @@
             back_branch[here, :] = branch_back
             return (back * norm, back, value * aside[here, :], branch_back.astype(f32))
 
-        terms = by_rows(rows, middle_rows, 4)
-        copies = exchange_rows(back_branch)
-        for at, value in zip((6, 7, 5, 4), terms, strict=True):
-            note(layer, at, value)
+        copies = []
+        for at in range(SPLIT):
+            back_copies[at].wait()
+            terms = by_rows(at * chunk, chunk, middle_rows, 4)
+            copies.append(send_rows(back_branch, at))
+            for spot_at, value in zip((6, 7, 5, 4), terms, strict=True):
+                note(layer, spot_at, value)
         load(layer, "unit_one", "inv_one")
         loaded("wm")
 
@@ -1221,21 +1477,21 @@
 
         core_copies = []
 
-        def send_back(start):
+        def send_back(start, count_rows):
             core_copies.append(
                 c_copy(
-                    head_tx.at[pl.ds(start, rows), :],
-                    head_back.at[pl.ds(aligned(col * group + start, 16), rows), :],
+                    head_tx.at[pl.ds(start, count_rows), :],
+                    head_back.at[pl.ds(aligned(col * group + start, 16), count_rows), :],
                 )
             )
             core_copies[-1].start()
 
         mixed_rows(0, rows)
-        send_back(0)
-        for copy in copies:
-            copy.wait()
-        mixed_rows(rows, rows)
-        send_back(rows)
+        send_back(0, rows)
+        for at in range(SPLIT):
+            copies[at].wait()
+            mixed_rows(rows + at * chunk, chunk)
+            send_back(rows + at * chunk, chunk)
         loaded("heads", "lse", "head_mix", "mixed")
         if last:
             load(0, "wm")
@@ -1331,11 +1587,8 @@
 
         back_copies = []
         for at in range(SPLIT):
-            start = rows + at * chunk
-            one_rows(start, chunk, tx, at * chunk)
-            view = pl.ds(at * chunk, chunk)
-            back_copies.append(y_copy(tx.at[view, :], rx.at[view, :]))
-            back_copies[-1].start()
+            one_rows(rows + at * chunk, chunk, tx, at * chunk)
+            back_copies.append(send_part(at))
         if last:
             produce_other(layer, 1)
             produce_other(layer, 0)
@@ -1350,8 +1603,6 @@
             load(0, "slope", "wu", "wq", "output", "normed_two", "active")
             load(0, "mixed", "heads", "lse", "head_mix")
         loaded("unit_one", "inv_one")
-        for copy in back_copies:
-            copy.wait()
 
         def input_rows(here):
             back = part[here, :] + rx[here, :].astype(f32)
@@ -1363,24 +1614,32 @@
             grad[here, :] = grad[here, :] + scale * (scaled - first - norm * second)
             return (back * norm, back)
 
-        terms = by_rows(rows, input_rows, 2)
-        for at, value in zip((0, 1), terms, strict=True):
-            note(layer, at, value)
+        if last:
+            loaded("output")
+        out_copies = []
+        for at in range(SPLIT):
+            back_copies[at].wait()
+            terms = by_rows(at * chunk, chunk, input_rows, 2)
+            if last:
+                out_rows(0, at * chunk, chunk)
+                out_copies.append(send_rows(back_out, at))
+            for spot_at, value in zip((0, 1), terms, strict=True):
+                note(layer, spot_at, value)
         if last:
             load(0, "unit_two", "inv_two")
-    grad_out[...] = grad[...]
     scatter.z_finish(0, 3)
     scatter.z_finish(0, 2)
-    scatter_vectors(place, vec_grads, packed, spare, spot, vec_out, v_send, v_recv)
+    to_features(place, grad, aside.at[:, pl.ds(0, half)], grad_out, c_send.at[26], c_recv.at[26])
     scatter.x_finish(0, 0)
     scatter.x_finish(0, 1)
+    scatter_vectors(place, vec_grads, packed, spare, spot, vec_out, v_send, v_recv)
     scatter.z_finish(0, 0)
     scatter.z_finish(0, 1)
     scatter.finish()
 
 
 def backward_call(mesh_count, tokens, grad, vecs, weights, saved, spot_shape):
-    rows = grad.shape[0]
+    rows = padded_rows(tokens)
     group = 2 * rows
     half = D // 2
     width = half // 2
@@ -1392,8 +1651,9 @@
 
     halves = [(half, 3 * half), (half, half), (half, wide), (wide, half)]
     shards = [(dims[0] // mesh_count, dims[1]) for dims in halves]
-    outs = [shape(LAYERS, *dims) for dims in shards]
-    outs += [shape(rows, D), shape(*spot_shape)]
+    results = [(3, shards[0][0], half)] + shards[1:]
+    outs = [shape(LAYERS, *dims) for dims in results]
+    outs += [shape(tokens, half), shape(*spot_shape)]
     dma = pltpu.SemaphoreType.DMA
     scratch = [
         pltpu.VMEM((D, 3 * half), bf16),
@@ -1426,7 +1686,7 @@
     scratch += [pltpu.VMEM(dims, bf16) for dims in halves]
     scratch += [pltpu.VMEM((dims[0] // 2, dims[1]), bf16) for dims in halves]
     scratch += [pltpu.VMEM((line - 1,) + dims, bf16) for dims in shards]
-    scratch += [pltpu.VMEM(dims, f32) for dims in shards]
+    scratch += [pltpu.VMEM(dims, f32) for dims in results]
     scratch += [
         pltpu.VMEM((LAYERS, 10 * D + FF), f32),
         pltpu.VMEM((line,) + spot_shape, f32),
@@ -1434,8 +1694,8 @@
         pltpu.VMEM(spot_shape, f32),
         dma((LAYERS * 4 * SPLIT,)),
         dma((LAYERS * 4 * SPLIT,)),
-        dma((LAYERS * 12,)),
-        dma((LAYERS * 12,)),
+        dma((LAYERS * 13 + 1,)),
+        dma((LAYERS * 13 + 1,)),
         dma((GROUPS, line)),
         dma((GROUPS, line)),
         dma((GROUPS, line - 1)),
@@ -1445,12 +1705,12 @@
         dma((KINDS,)),
         dma((line + 2,)),
         dma((line + 2,)),
-        dma((18,)),
+        dma((19,)),
     ]
     return pl.pallas_call(
-        functools.partial(backward_kernel, mesh_count, tokens),
+        functools.partial(backward_kernel, mesh_count),
         out_shape=outs,
-        in_specs=[WHOLE] * 2 + [ANY] * 18,
+        in_specs=[WHOLE] * 2 + [ANY] * 19,
         out_specs=[ANY] * 4 + [WHOLE] * 2,
         scratch_shapes=scratch,
         compiler_params=pltpu.CompilerParams(
@@ -1487,18 +1747,6 @@
     group = 2 * rows
     half = D // 2
 
-    def to_tokens(values):
-        padded = jnp.pad(values, ((0, 2 * rows - tokens), (0, 0))).reshape(2, rows, features)
-        mine = lax.dynamic_index_in_dim(padded, col_at, 0, False)
-        other = swap(lax.dynamic_index_in_dim(padded, 1 - col_at, 0, False), "col")
-        return ordered(mine, other, col_at, 1)
-
-    def to_features(values):
-        split = values.reshape(rows, 2, features).transpose(1, 0, 2)
-        mine = lax.dynamic_index_in_dim(split, col_at, 0, False)
-        other = swap(lax.dynamic_index_in_dim(split, 1 - col_at, 0, False), "col")
-        return ordered(mine, other, col_at, 0)[:tokens]
-
     shards = [
         triplet_master.astype(bf16).reshape(LAYERS, -1, 3 * half),
         project_master.astype(bf16),
@@ -1507,26 +1755,20 @@
     ]
     piece = vectors_master.shape[1]
     line_at = (lax.axis_index("dp") % 2 * 2 + row_at) * 2 + col_at
-    spot = lax.dynamic_update_slice_in_dim(
-        jnp.zeros((LAYERS, 8 * piece), f32), vectors_master, line_at * piece, 1
-    ).reshape(LAYERS, -1, 128)
-    used = spot.shape[1]
-    spot = jnp.pad(spot, ((0, 0), (0, -used % 8), (0, 0)))
+    spot = jnp.where(
+        jnp.arange(8 * piece) // piece == line_at, jnp.tile(vectors_master, (1, 8)), 0.0
+    )
     place = jnp.arange(2 * group) % rows
     late = jnp.arange(2 * group) // group
     bias = jnp.where(place + late * rows < tokens, 0.0, -1e30).astype(f32)[None]
 
-    (w_a, w_b, w_c, w_d, vectors, *saved, block_rows) = forward_call(
-        count, tokens, to_tokens(images), spot, bias, shards
+    (w_a, w_b, w_c, w_d, _, vectors, *saved, grad_rows, block_out) = forward_call(
+        count, images, cotangent, spot, bias, shards
     )
-    block_out = to_features(block_rows)
-    *grads, grad_rows, vector_sums = backward_call(
-        count, tokens, to_tokens(cotangent), vectors, (w_a, w_b, w_c, w_d), saved, spot.shape
+    *grads, grad_out, vector_sums = backward_call(
+        count, tokens, grad_rows, vectors, (w_a, w_b, w_c, w_d), saved, spot.shape
     )
-    grad_out = to_features(grad_rows)
-    vector_reduced = lax.dynamic_slice_in_dim(
-        vector_sums[:, :used].reshape(LAYERS, -1), line_at * piece, piece, 1
-    )
+    vector_reduced = lax.dynamic_slice_in_dim(vector_sums, line_at * piece, piece, 1)
 
     outs = []
     states = (
@@ -1535,10 +1777,9 @@
         (expand_master, expand_first, expand_second),
         (shrink_master, shrink_first, shrink_second),
     )
+    grads[0] = grads[0].transpose(0, 2, 1, 3)
     for kind, (master, first, second) in enumerate(states):
-        outs += adam_step(
-            master, first, second, grads[kind].reshape(master.shape), learn_rate, decay_rate
-        )
+        outs += adam_step(master, first, second, grads[kind], learn_rate, decay_rate)
     outs += adam_step(
         vectors_master, vectors_first, vectors_second, vector_reduced, vector_rate, 0.0
     )

time: 580 us -> 535 us (0.922)
  Pallas kernels: 529 us -> 502 us
  local copies, waits for them, and re-layouts: 21.4 us -> 4.61 us
    pallas_call x2, Pallas kernels: 529 us -> 502 us  [the longest x1 272 us: backward_call(): pl.pallas_call(functools.partial(backward_kernel, mesh_count), out_shape=...]
    select_n x4 -> x1, other arithmetic: 7.73 us -> 0.63 us  [local(): jnp.where(jnp.arange(8 * piece) // piece == line_at, jnp.tile(vectors_mas...]
    reshape x3 -> x0, local copies, waits for them, and re-layouts: 7.09 us -> none  [the longest x2 5.62 us: to_features(): split = values.reshape(rows, 2, features).transpose(1, 0, 2)]
  transfers between devices with their start and end apart: 4 -> 0, of which waited for: 0 -> 0; matrix products, arithmetic and copies ran while one was open for 6% -> 0% of each run, Pallas kernels for 93% -> 0%
where the time goes in v4:
time: 535 us; the launch traced here: 525 us
  Pallas kernels  502 us (94%)
  other arithmetic  17.5 us (3%)
    pallas_call x1, Pallas kernels, backward_call(): pl.pallas_call(functools.partial(backward_kernel, mesh_count), out_shape=...  272 us
    pallas_call x1, Pallas kernels, forward_call(): pl.pallas_call(functools.partial(forward_kernel, mesh_count), out_shape=o...  229 us
    sub x5, other arithmetic, adam_step(): return (first_new, second_new, master - rate * (ratio + decay * master))  11.7 us

profile of v4, /device:TPU:0, one launch (start us, length us, event | category | flops | bytes accessed | tf_op | source)
XLA Modules:
  0.0 524.9 jit_solution(10247785241919655001)
XLA Ops:
  0.7 0.0 copy-start.2
  0.7 0.0 copy-start
  0.7 0.6 compare_select_fusion.refs_3_
  1.3 0.7 tile.4
  2.0 0.1 tile.10
  2.1 0.6 broadcast_select_fusion.refs_2_
  2.8 1.6 convert_element_type.13.refs_5_
  4.4 1.2 convert_bitcast_fusion
  5.6 0.8 copy.36
  6.3 0.0 copy-done
  6.3 0.9 convert_element_type.14.refs_6_
  7.2 0.0 copy-done.2
  7.2 0.9 convert_element_type.15.refs_7_
  8.1 229.1 %forward.1 = (bf16[2,1024,1536]{2,1,0:T(8,128)(2,1)}, bf16[2,512,1024]{2,1,0:T(8,128)(2,1)}, bf16[2,1024,2048]{2,1,0:T(8,128)(2,1)}, bf16[2,2048,1024]{2,1,0:T(8...) custom-call(bf16[685,512]{1,0:T(8,128)(2,1)} %refs_0_.1, ...), custom_call_target="tpu_custom_call" | custom-call | tf_op jit(solution)/shard_map/forward/pallas_call | solution.py:935
  237.1 0.0 copy-start.13
  237.1 0.0 copy-start.14
  237.2 0.0 copy-start.15
  237.2 0.0 copy-start.4
  237.2 272.5 %backward.1 = (f32[2,3,64,512]{3,2,1,0:T(8,128)}, f32[2,64,512]{2,1,0:T(8,128)}, f32[2,64,2048]{2,1,0:T(8,128)}, f32[2,256,512]{2,1,0:T(8,128)}, f32[685,512]{1,0:T(8,128)}, /*index=5*/f32[2,3584]{1,0:T(2,128)}) custom-call(bf16[352,1024]{1,0:T(8,128)(2,1)} %get-tuple-element.46.refs_0_, f32[2,14336]{1,0:T(2,128)} %get-tuple-element.47.refs_1_, ...), custom_call_target="tpu_custom_call" | custom-call | tf_op jit(solution)/shard_map/backward/pallas_call | solution.py:1710
  509.6 0.0 copy-done.13
  509.7 0.0 copy-done.14
  509.7 0.0 copy-done.15
  509.7 1.4 multiply_subtract_fusion.4
  511.1 2.2 multiply_subtract_fusion.3
  513.3 0.0 copy-start.1
  513.3 0.0 copy-start.6
  513.3 0.0 copy-start.7
  513.3 0.0 copy-start.11
  513.3 0.0 copy-done.4
  513.3 3.6 multiply_subtract_fusion.2
  516.9 0.0 copy-done.1
  516.9 0.0 copy-done.6
  516.9 0.0 copy-done.7
  516.9 0.0 copy-done.11
  517.0 0.0 copy-start.3
  517.0 0.0 copy-start.8
  517.0 0.0 copy-start.9
  517.0 0.0 copy-start.10
  517.0 2.2 multiply_subtract_fusion.1
  519.2 0.0 copy-done.3
  519.2 0.0 copy-done.8
  519.2 0.7 copy-done.9
  520.0 0.3 copy-done.10
  520.3 0.0 copy-start.12
  520.3 0.0 copy-start.5
  520.3 2.3 multiply_subtract_fusion
  522.5 0.0 copy-done.12
  522.5 0.9 copy.39
  523.4 0.0 copy-done.5
  523.4 1.1 copy.40
  (1 shorter events, 0.0 us)
Async XLA Ops:
  0.7 6.6 %copy-start.2 = (f32[2,256,512]{2,1,0:T(8,128)S(1)}, f32[2,256,512]{2,1,0:T(8,128)}, u32[]{:S(2)}) copy-start(f32[2,256,512]{2,1,0:T(8,128)} %param.28) | copy-start | bytes 3145732
  0.7 5.7 %copy-start = (f32[2,64,2048]{2,1,0:T(8,128)S(1)}, f32[2,64,2048]{2,1,0:T(8,128)}, u32[]{:S(2)}) copy-start(f32[2,64,2048]{2,1,0:T(8,128)} %param.25) | copy-start | bytes 3145732
  237.1 272.5 %copy-start.13 = (f32[2,448]{1,0:T(2,128)S(1)}, f32[2,448]{1,0:T(2,128)}, u32[]{:S(2)}) copy-start(f32[2,448]{1,0:T(2,128)} %param.31) | copy-start | bytes 10756
  237.1 272.5 %copy-start.14 = (f32[2,448]{1,0:T(2,128)S(1)}, f32[2,448]{1,0:T(2,128)}, u32[]{:S(2)}) copy-start(f32[2,448]{1,0:T(2,128)} %param.33) | copy-start | bytes 10756
  237.2 272.5 %copy-start.15 = (f32[2,448]{1,0:T(2,128)S(1)}, f32[2,448]{1,0:T(2,128)}, u32[]{:S(2)}) copy-start(f32[2,448]{1,0:T(2,128)} %param.32) | copy-start | bytes 10756
  237.2 276.1 %copy-start.4 = (f32[2,64,3,512]{3,1,2,0:T(8,128)S(1)}, f32[2,64,3,512]{3,1,2,0:T(8,128)}, u32[]{:S(2)}) copy-start(f32[2,64,3,512]{3,1,2,0:T(8,128)} %param.19) | copy-start | bytes 2359300
  513.3 3.7 copy-start.1
  513.3 3.7 copy-start.6
  513.3 3.7 copy-start.7
  513.3 3.7 copy-start.11
  517.0 2.3 copy-start.3
  517.0 2.3 copy-start.8
  517.0 3.0 copy-start.9
  517.0 3.3 copy-start.10
  520.3 2.3 copy-start.12
  520.3 3.1 copy-start.5

commit v5 on v4

--- a/solution.py
+++ b/solution.py
@@ -45,9 +45,10 @@
 MESH = pl.DeviceIdType.MESH
 KINDS = 4
 GROUPS = LAYERS * KINDS
-WINDOW = 2
+WINDOW = 3
 TRIGGER = 1.0
 LEAD = 25.0
+EARLY = 4
 SPLIT = 2
 ANY = pl.BlockSpec(memory_space=pl.ANY)
 WHOLE = pl.BlockSpec(memory_space=pltpu.VMEM)
@@ -345,11 +346,10 @@
         images,
         cotangent,
         spot_in,
-        bias_in,
-        shard_a,
-        shard_b,
-        shard_c,
-        shard_d,
+        master_a,
+        master_b,
+        master_c,
+        master_d,
         w_a,
         w_b,
         w_c,
@@ -372,7 +372,11 @@
         head_mix_out,
         back_out_out,
         cotangent_out,
-        block_out,
+        middle_out,
+        shard_a,
+        shard_b,
+        shard_c,
+        shard_d,
         state,
         padded,
         arrived,
@@ -444,7 +448,24 @@
     spot[...] = spot_in[...]
     vectors = Vectors(place, spot, raw, spare, v_send, v_recv)
     vectors.start()
+    cast_done = set()
+
+    def cast(at):
+        if at in cast_done or at >= GROUPS:
+            return
+        cast_done.add(at)
+        layer, kind = divmod(at, KINDS)
+        if kind == 0:
+            for part_at in range(3):
+                shard_a[layer, :, part_at * half : (part_at + 1) * half] = master_a[
+                    layer, part_at
+                ].astype(bf16)
+        else:
+            source = (master_a, master_b, master_c, master_d)[kind]
+            (shard_a, shard_b, shard_c, shard_d)[kind][layer] = source[layer].astype(bf16)
+
     for at in range(WINDOW):
+        cast(at)
         gather.line_out(at)
 
     plan = []
@@ -457,8 +478,8 @@
         for step in range(1, place.line):
             line_due = begin + span * (0.3 + 0.7 * step / (place.line - 1))
             plan.append((line_due, 1, gather.line_in, (at, step)))
-            if 0 < at < GROUPS - 1 and step == 1:
-                plan.append((line_due, 0.5, gather.own_out, (at + 1,)))
+            if at >= EARLY and step == 1:
+                plan.append((begin - 5.0, 0.5, gather.own_out, (at,)))
             if at + WINDOW < GROUPS and step == max(1, round(TRIGGER * (place.line - 1))):
                 plan.append((line_due, 1.5, gather.line_out, (at + WINDOW,)))
         for step in range(place.line):
@@ -559,14 +580,23 @@
     c_at[0] = 2
     vectors.line_in()
     vectors.add(0, place.x_peer)
-    gather.own_out(0)
-    gather.own_out(1)
+    for at in range(GROUPS):
+        cast(at)
+    for at in range(EARLY):
+        gather.own_out(at)
     vectors.add(1, place.y_peer)
     vectors.add(2, place.c_peer)
     vectors.spread(vecs)
     save("vecs", 11, vecs, vecs_out)
 
     lane = lax.broadcasted_iota(jnp.int32, (1, 128), 1) < HEAD_DIM
+    key_at = lax.broadcasted_iota(jnp.int32, (1, 2 * group), 1)
+    late = key_at >= group
+    spare_row = tokens - rows
+    padding = late & (
+        (key_at >= group + spare_row) & (key_at < group + rows) | (key_at >= group + rows + spare_row)
+    )
+    mask = jnp.where(padding, -1e30, 0.0)
     valid = lax.broadcasted_iota(jnp.int32, (rows, 1), 0) < tokens - col * rows
 
     def vector(layer, at):
@@ -669,7 +699,7 @@
                     )
                     key = heads[:, width + pair * 128 : width + pair * 128 + 128]
                     value = heads[:, 2 * width + pair * 128 : 2 * width + pair * 128 + 128]
-                    scores = nt(both, key) + bias_in[...]
+                    scores = nt(both, key) + mask
                     peak = jnp.max(scores, 1, keepdims=True)
                     weights = jnp.exp(scores - peak)
                     total = jnp.sum(weights, 1, keepdims=True)
@@ -803,16 +833,11 @@
             back_copies.append(shrink_send(1))
         else:
             expand(0, rows, 139.0)
-            copies[0].wait()
-            expand(rows, chunk, 146.0)
-            ensure(7)
-            stage(3, 1)
-            ready(3)
-            back_copies.append(shrink_send(0))
-            copies[1].wait()
-            expand(rows + chunk, chunk, 160.0)
-            back_copies.append(shrink_send(1))
-        shrink(0, rows, part, 0)
+            for at in range(SPLIT):
+                copies[at].wait()
+                expand(rows + at * chunk, chunk, 146.0 + 8.0 * at)
+        if first:
+            shrink(0, rows, part, 0)
         save("normed_two", 9, normed_two, normed_two_out.at[layer])
         save("active", 10, active, active_out.at[layer])
         save("slope", 12, slope, slope_out.at[layer])
@@ -822,24 +847,24 @@
             for copy in out_copies:
                 copy.wait()
             save("back_out", 15, back_out, back_out_out)
-        settle("output", "unit", "inverse")
+            save("state", 16, state, middle_out)
+            break
+        settle("unit", "inverse")
         next_copies = []
         for at in range(SPLIT):
             back_copies[at].wait()
             here = slice(at * chunk, at * chunk + chunk)
             output[here, :] = part[here, :] + rx[here, :].astype(f32) + vector(layer, 12)
             state[here, :] = state[here, :] + vector(layer, 13) * output[here, :]
-            if first:
-                next_copies.append(norm_one(1, at))
-                if at == 0:
-                    pump(94)
-        save("output", 13, output, output_out.at[layer])
-        if first:
-            ensure(4)
-            stage(0, 1)
+            next_copies.append(norm_one(1, at))
+            if at == 0:
+                pump(94)
+        save("output", 13, output, output_out)
+        ensure(4)
+        stage(0, 1)
         copies = next_copies
-    tx[...] = state[...].astype(bf16)
-    to_features(place, tx, arrived, block_out, c_send.at[15], c_recv.at[15])
+    ensure(GROUPS - 1)
+    gather.arrive(GROUPS - 1)
     gather.finish()
     settle(*list(pending))
 
@@ -848,7 +873,7 @@
     return -(-tokens // (2 * TILE)) * TILE
 
 
-def forward_call(mesh_count, images, cotangent, spot, bias, shards):
+def forward_call(mesh_count, images, cotangent, spot, masters):
     tokens = images.shape[0]
     rows = padded_rows(tokens)
     group = 2 * rows
@@ -878,14 +903,18 @@
         shape(LAYERS, group, D, kind=bf16),
         shape(LAYERS, group, FF // 2, kind=bf16),
         shape(LAYERS, group, FF // 2, kind=bf16),
-        shape(LAYERS, rows, D),
+        shape(rows, D),
         shape(LAYERS, 2 * group, width, kind=bf16),
         shape(group, D, kind=bf16),
         shape(rows, D, kind=bf16),
-        shape(tokens, half, kind=bf16),
+        shape(rows, D),
     ]
     dma = pltpu.SemaphoreType.DMA
     scratch = [
+        pltpu.VMEM((LAYERS, D // (2 * mesh_count), 3 * half), bf16),
+        pltpu.VMEM((LAYERS, half // mesh_count, half), bf16),
+        pltpu.VMEM((LAYERS, D // (2 * mesh_count), FF // 2), bf16),
+        pltpu.VMEM((LAYERS, FF // 2 // mesh_count, half), bf16),
         pltpu.VMEM((rows, D), f32),
         pltpu.VMEM((group, half), bf16),
         pltpu.VMEM((rows, half), bf16),
@@ -930,19 +959,19 @@
         dma((16,)),
         dma((16,)),
         dma((KINDS + 1,)),
-        dma((16,)),
+        dma((17,)),
     ]
     return pl.pallas_call(
         functools.partial(forward_kernel, mesh_count),
         out_shape=outs,
-        in_specs=[WHOLE] * 8,
-        out_specs=[ANY] * 21 + [WHOLE] * 2,
+        in_specs=[WHOLE] * 7,
+        out_specs=[ANY] * 21 + [WHOLE] + [ANY],
         scratch_shapes=scratch,
         compiler_params=pltpu.CompilerParams(
             collective_id=0, has_side_effects=True, vmem_limit_bytes=60 << 20
         ),
         name="forward",
-    )(images, cotangent, spot, bias, *shards)
+    )(images, cotangent, spot, *masters)
 
 
 def fold(values):
@@ -1126,12 +1155,14 @@
         output_in,
         head_mix_in,
         back_out_in,
+        middle_in,
         grad_a,
         grad_b,
         grad_c,
         grad_d,
         grad_out,
         vec_out,
+        block_out,
         wq,
         wm,
         wu,
@@ -1152,6 +1183,8 @@
         part,
         tx,
         rx,
+        rx_out,
+        arrived,
         head_back,
         head_tx,
         head_grad,
@@ -1242,6 +1275,7 @@
         "head_mix": (head_mix_in, head_mix),
         "mixed": (mixed_in, mixed),
         "back_out": (back_out_in, back_out),
+        "middle": (middle_in, part),
     }
     names = list(sources)
     loading = {}
@@ -1249,7 +1283,7 @@
     def load(layer, *wanted):
         for name in wanted:
             source, buffer = sources[name]
-            if name != "back_out":
+            if name not in ("back_out", "output", "middle"):
                 source = source.at[layer]
             copy = pltpu.make_async_copy(source, buffer, load_sem.at[names.index(name)])
             copy.start()
@@ -1287,7 +1321,7 @@
         view = pl.ds(at * chunk, chunk)
         return y_copy(tx.at[view, :], rx.at[view, :])
 
-    load(1, "back_out", "wd", "slope", "wu", "output", "active", "normed_two", "unit_two", "inv_two")
+    load(1, "back_out", "wd", "slope", "wu", "branch", "active", "normed_two", "unit_two", "inv_two")
     load(1, "wm", "mixed", "heads", "lse", "head_mix", "wq")
     grad[...] = grad_in[...].astype(f32)
     vec_grads[...] = jnp.zeros_like(vec_grads)
@@ -1337,7 +1371,12 @@
 
     def produce_other(layer, kind):
         target = sums[kind]
-        buffer = half_tx[kind]
+        buffer = {
+            0: half_tx[0].at[:, pl.ds(0, 3 * half)],
+            1: half_tx[0].at[:, pl.ds(3 * half, half)],
+            2: half_tx[0],
+            3: half_tx[1],
+        }[kind]
 
         def step(at, carry):
             buffer[spot_of(kind, at)] = weight_grad(kind, 1 - col, at).astype(bf16)
@@ -1365,12 +1404,32 @@
         def body(here):
             value = grad[here, :]
             back = (vector(layer, 13) * value).astype(bf16)
-            if layer < LAYERS - 1:
-                back_out[here, :] = back
+            back_out[here, :] = back
             return (value * aside[here, :], back.astype(f32))
 
         for at, value in zip((13, 12), by_rows(start, count_rows, body, 2), strict=True):
             note(layer, at, value)
+
+    def last_rows(layer, start, count_rows):
+        def body(here):
+            value = aside[here, :] + rx_out[here, :].astype(f32) + vector(layer, 12)
+            result = part[here, :] + vector(layer, 13) * value
+            back_out[here, :] = result.astype(bf16)
+            gradient = grad_in[here, :].astype(f32)
+            back = (vector(layer, 13) * gradient).astype(bf16)
+            return (gradient * value, back.astype(f32))
+
+        for at, value in zip((13, 12), by_rows(start, count_rows, body, 2), strict=True):
+            note(layer, at, value)
+
+    def shrink(start, count_rows, target, target_at):
+        def step(at, carry):
+            lanes = pl.ds(aligned(at * half), half)
+            value = nn(active[start : start + count_rows, :], wd[:, lanes])
+            target[pl.ds(target_at, count_rows), lanes] = value.astype(target.dtype)
+            return carry
+
+        lax.fori_loop(0, 2, step, 0)
 
     for layer in reversed(range(LAYERS)):
         last = layer == LAYERS - 1
@@ -1423,9 +1482,7 @@
                 out_copies[at].wait()
                 back_copies.append(back_chunk(at))
         two_rows(0, rows, part, 0)
-        if last:
-            load(0, "wd")
-        else:
+        if not last:
             scatter.x_finish(1, 0)
         loaded("active", "normed_two")
         produce_other(layer, 3)
@@ -1433,10 +1490,6 @@
         produce_own(layer, 3)
         produce_own(layer, 2)
         load(layer, "normed")
-        if last:
-            loaded("output")
-            out_rows(layer, 0, rows)
-            load(1, "branch")
         loaded("unit_two", "inv_two", "branch")
 
         def middle_rows(here):
@@ -1488,10 +1541,20 @@
 
         mixed_rows(0, rows)
         send_back(0, rows)
+        if last:
+            shrink(rows, rows, tx, 0)
+            shrink(0, rows, aside, 0)
+            load(0, "wd")
+            load(1, "middle")
         for at in range(SPLIT):
             copies[at].wait()
             mixed_rows(rows + at * chunk, chunk)
             send_back(rows + at * chunk, chunk)
+        if last:
+            last_copies = [
+                y_copy(tx.at[view, :], rx_out.at[view, :])
+                for view in (pl.ds(at * chunk, chunk) for at in range(SPLIT))
+            ]
         loaded("heads", "lse", "head_mix", "mixed")
         if last:
             load(0, "wm")
@@ -1501,7 +1564,7 @@
         for copy in core_copies:
             copy.wait()
 
-        piece = 2 * group // 4
+        piece = 2 * group // 2
         head_copies = []
         for pair in range(pairs):
             lanes = slice(pair * 128, pair * 128 + 128)
@@ -1526,7 +1589,7 @@
                 inner = flip(halves, back.astype(f32) * head_mix[here, lanes].astype(f32))
                 inner = jnp.concatenate([inner[0:1], inner[1:2]], 1)
                 query_grad = jnp.zeros((256, 128), f32)
-                for block in range(4):
+                for block in range(2):
                     keys = slice(block * piece, block * piece + piece)
                     key = heads[keys, key_lanes]
                     scores = nt(key, queries)
@@ -1573,6 +1636,9 @@
         for copy in head_copies:
             copy.wait()
         loaded("wq", "normed")
+        if last:
+            for copy in last_copies:
+                copy.wait()
         if not last:
             produce_other(layer, 0)
 
@@ -1594,6 +1660,11 @@
             produce_other(layer, 0)
             produce_own(layer, 1)
             produce_own(layer, 0)
+            loaded("middle")
+            last_rows(layer, 0, rows)
+            to_features(
+                place, back_out.at[pl.ds(0, rows), :], arrived, block_out, c_send.at[27], c_recv.at[27]
+            )
         else:
             produce_own(layer, 0)
             produce_other(layer, 1)
@@ -1653,7 +1724,7 @@
     shards = [(dims[0] // mesh_count, dims[1]) for dims in halves]
     results = [(3, shards[0][0], half)] + shards[1:]
     outs = [shape(LAYERS, *dims) for dims in results]
-    outs += [shape(tokens, half), shape(*spot_shape)]
+    outs += [shape(tokens, half), shape(*spot_shape), shape(tokens, half, kind=bf16)]
     dma = pltpu.SemaphoreType.DMA
     scratch = [
         pltpu.VMEM((D, 3 * half), bf16),
@@ -1676,12 +1747,14 @@
         pltpu.VMEM((rows, D), f32),
         pltpu.VMEM((rows, D), bf16),
         pltpu.VMEM((rows, D), bf16),
+        pltpu.VMEM((rows, D), bf16),
+        pltpu.VMEM((rows, half), bf16),
         pltpu.VMEM((2 * group, width), bf16),
         pltpu.VMEM((group, width), bf16),
         pltpu.VMEM((2 * group, 3 * width), bf16),
         pltpu.VMEM((2 * group, 128), f32),
         pltpu.VMEM((2 * group, 128), f32),
-        [pltpu.VMEM(dims, bf16) for dims in halves],
+        [pltpu.VMEM(dims, bf16) for dims in halves[2:]],
     ]
     scratch += [pltpu.VMEM(dims, bf16) for dims in halves]
     scratch += [pltpu.VMEM((dims[0] // 2, dims[1]), bf16) for dims in halves]
@@ -1694,8 +1767,8 @@
         pltpu.VMEM(spot_shape, f32),
         dma((LAYERS * 4 * SPLIT,)),
         dma((LAYERS * 4 * SPLIT,)),
-        dma((LAYERS * 13 + 1,)),
-        dma((LAYERS * 13 + 1,)),
+        dma((LAYERS * 13 + 2,)),
+        dma((LAYERS * 13 + 2,)),
         dma((GROUPS, line)),
         dma((GROUPS, line)),
         dma((GROUPS, line - 1)),
@@ -1705,13 +1778,13 @@
         dma((KINDS,)),
         dma((line + 2,)),
         dma((line + 2,)),
-        dma((19,)),
+        dma((20,)),
     ]
     return pl.pallas_call(
         functools.partial(backward_kernel, mesh_count),
         out_shape=outs,
-        in_specs=[WHOLE] * 2 + [ANY] * 19,
-        out_specs=[ANY] * 4 + [WHOLE] * 2,
+        in_specs=[WHOLE] * 2 + [ANY] * 20,
+        out_specs=[ANY] * 4 + [WHOLE] * 3,
         scratch_shapes=scratch,
         compiler_params=pltpu.CompilerParams(
             collective_id=1, has_side_effects=True, vmem_limit_bytes=63 << 20
@@ -1742,31 +1815,23 @@
     count = lax.axis_size("dp")
     row_at = lax.axis_index("row")
     col_at = lax.axis_index("col")
-    tokens, features = images.shape
-    rows = -(-tokens // (2 * TILE)) * TILE
-    group = 2 * rows
-    half = D // 2
-
-    shards = [
-        triplet_master.astype(bf16).reshape(LAYERS, -1, 3 * half),
-        project_master.astype(bf16),
-        expand_master.astype(bf16),
-        shrink_master.astype(bf16),
-    ]
+    masters = (triplet_master.transpose(0, 2, 1, 3), project_master, expand_master, shrink_master)
     piece = vectors_master.shape[1]
     line_at = (lax.axis_index("dp") % 2 * 2 + row_at) * 2 + col_at
     spot = jnp.where(
         jnp.arange(8 * piece) // piece == line_at, jnp.tile(vectors_master, (1, 8)), 0.0
     )
-    place = jnp.arange(2 * group) % rows
-    late = jnp.arange(2 * group) // group
-    bias = jnp.where(place + late * rows < tokens, 0.0, -1e30).astype(f32)[None]
-
-    (w_a, w_b, w_c, w_d, _, vectors, *saved, grad_rows, block_out) = forward_call(
-        count, images, cotangent, spot, bias, shards
+    (w_a, w_b, w_c, w_d, _, vectors, *saved, grad_rows, middle) = forward_call(
+        count, images, cotangent, spot, masters
     )
-    *grads, grad_out, vector_sums = backward_call(
-        count, tokens, grad_rows, vectors, (w_a, w_b, w_c, w_d), saved, spot.shape
+    *grads, grad_out, vector_sums, block_out = backward_call(
+        count,
+        images.shape[0],
+        grad_rows,
+        vectors,
+        (w_a, w_b, w_c, w_d),
+        (*saved, middle),
+        spot.shape,
     )
     vector_reduced = lax.dynamic_slice_in_dim(vector_sums, line_at * piece, piece, 1)
 

time: 535 us -> 502 us (0.938)
  Pallas kernels: 502 us -> 475 us
    pallas_call x1, Pallas kernels: 229 us -> 206 us  [forward_call(): pl.pallas_call(functools.partial(forward_kernel, mesh_count), out_shape=o...]
where the time goes in v5:
time: 502 us; the launch traced here: 492 us
  Pallas kernels  475 us (95%)
  other arithmetic  12.4 us (2%)
    pallas_call x1, Pallas kernels, backward_call(): pl.pallas_call(functools.partial(backward_kernel, mesh_count), out_shape=...  269 us
    pallas_call x1, Pallas kernels, forward_call(): pl.pallas_call(functools.partial(forward_kernel, mesh_count), out_shape=o...  206 us
    sub x5, other arithmetic, adam_step(): return (first_new, second_new, master - rate * (ratio + decay * master))  11.7 us

profile of v5, /device:TPU:0, one launch (start us, length us, event | category | flops | bytes accessed | tf_op | source)
XLA Modules:
  0.0 492.5 jit_solution(9748332838759502811)
XLA Ops:
  0.7 0.7 tile.4
  1.4 0.1 tile.10
  1.5 0.6 broadcast_select_fusion.refs_2_
  2.1 205.8 %forward.1 = (bf16[2,1024,1536]{2,1,0:T(8,128)(2,1)}, bf16[2,512,1024]{2,1,0:T(8,128)(2,1)}, bf16[2,1024,2048]{2,1,0:T(8,128)(2,1)}, bf16[2,2048,1024]{2,1,0:T(8...) custom-call(bf16[685,512]{1,0:T(8,128)(2,1)} %refs_0_.1, ...), custom_call_target="tpu_custom_call" | custom-call | tf_op jit(solution)/shard_map/forward/pallas_call | solution.py:964
  207.9 0.0 copy-start.11
  207.9 0.0 copy-start.12
  207.9 0.0 copy-start.13
  207.9 0.0 copy-start.2
  207.9 269.3 %backward.1 = (f32[2,3,64,512]{3,2,1,0:T(8,128)}, f32[2,64,512]{2,1,0:T(8,128)}, f32[2,64,2048]{2,1,0:T(8,128)}, f32[2,256,512]{2,1,0:T(8,128)}, f32[685,512]{1,...) custom-call(bf16[352,1024]{1,0:T(8,128)(2,1)} %get-tuple-element.46.refs_0_, ...), custom_call_target="tpu_custom_call" | custom-call | tf_op jit(solution)/shard_map/backward/pallas_call | solution.py:1783
  477.2 0.0 copy-done.11
  477.2 0.0 copy-done.12
  477.2 0.0 copy-done.13
  477.3 1.4 multiply_subtract_fusion.4
  478.6 2.2 multiply_subtract_fusion.3
  480.8 0.0 copy-start
  480.8 0.0 copy-start.4
  480.8 0.0 copy-start.5
  480.8 0.0 copy-start.9
  480.9 0.0 copy-done.2
  480.9 3.6 multiply_subtract_fusion.2
  484.5 0.0 copy-done
  484.5 0.0 copy-done.4
  484.5 0.0 copy-done.5
  484.5 0.0 copy-done.9
  484.5 0.0 copy-start.1
  484.5 0.0 copy-start.6
  484.6 0.0 copy-start.7
  484.6 0.0 copy-start.8
  484.6 2.2 multiply_subtract_fusion.1
  486.8 0.0 copy-done.1
  486.8 0.0 copy-done.6
  486.8 0.7 copy-done.7
  487.5 0.3 copy-done.8
  487.8 0.0 copy-start.10
  487.8 0.0 copy-start.3
  487.9 2.3 multiply_subtract_fusion
  490.1 0.0 copy-done.10
  490.1 0.9 copy.36
  491.0 0.0 copy-done.3
  491.0 1.1 copy.37
  (1 shorter events, 0.0 us)
Async XLA Ops:
  207.9 269.3 %copy-start.11 = (f32[2,448]{1,0:T(2,128)S(1)}, f32[2,448]{1,0:T(2,128)}, u32[]{:S(2)}) copy-start(f32[2,448]{1,0:T(2,128)} %param.31) | copy-start | bytes 10756
  207.9 269.3 %copy-start.12 = (f32[2,448]{1,0:T(2,128)S(1)}, f32[2,448]{1,0:T(2,128)}, u32[]{:S(2)}) copy-start(f32[2,448]{1,0:T(2,128)} %param.33) | copy-start | bytes 10756
  207.9 269.3 %copy-start.13 = (f32[2,448]{1,0:T(2,128)S(1)}, f32[2,448]{1,0:T(2,128)}, u32[]{:S(2)}) copy-start(f32[2,448]{1,0:T(2,128)} %param.32) | copy-start | bytes 10756
  207.9 272.9 %copy-start.2 = (f32[2,64,3,512]{3,1,2,0:T(8,128)S(1)}, f32[2,64,3,512]{3,1,2,0:T(8,128)}, u32[]{:S(2)}) copy-start(f32[2,64,3,512]{3,1,2,0:T(8,128)} %param.19) | copy-start | bytes 2359300
  480.8 3.7 copy-start
  480.8 3.7 copy-start.4
  480.8 3.7 copy-start.5
  480.8 3.7 copy-start.9
  484.5 2.3 copy-start.1
  484.5 2.3 copy-start.6
  484.6 3.0 copy-start.7
  484.6 3.3 copy-start.8
  487.8 2.3 copy-start.10
  487.8 3.1 copy-start.3

commit v6 on v5

--- a/solution.py
+++ b/solution.py
@@ -1140,6 +1140,7 @@
         w_b,
         w_c,
         w_d,
+        w_far,
         unit_one_in,
         inv_one_in,
         normed_in,
@@ -1167,6 +1168,9 @@
         wm,
         wu,
         wd,
+        wf,
+        far_tx,
+        far_rx,
         active,
         slope,
         feed,
@@ -1259,6 +1263,7 @@
         "wd": (w_d, wd),
         "wu": (w_c, wu),
         "wm": (w_b, wm),
+        "wf": (w_far, wf),
         "wq": (w_a, wq),
         "slope": (slope_in, slope),
         "active": (active_in, active),
@@ -1322,7 +1327,7 @@
         return y_copy(tx.at[view, :], rx.at[view, :])
 
     load(1, "back_out", "wd", "slope", "wu", "branch", "active", "normed_two", "unit_two", "inv_two")
-    load(1, "wm", "mixed", "heads", "lse", "head_mix", "wq")
+    load(1, "wf", "wm", "mixed", "heads", "lse", "head_mix", "wq")
     grad[...] = grad_in[...].astype(f32)
     vec_grads[...] = jnp.zeros_like(vec_grads)
     lane = lax.broadcasted_iota(jnp.int32, (1, 128), 1) < HEAD_DIM
@@ -1488,9 +1493,15 @@
         produce_other(layer, 3)
         produce_other(layer, 2)
         produce_own(layer, 3)
-        produce_own(layer, 2)
-        load(layer, "normed")
-        loaded("unit_two", "inv_two", "branch")
+        loaded("unit_two", "inv_two", "branch", "wf")
+
+        def far_rows(at):
+            here = slice(at * chunk, at * chunk + chunk)
+            far_tx[here, :] = nt(back_branch[here, :], wf[...]).astype(bf16)
+            return y_copy(
+                far_tx.at[pl.ds(at * chunk, chunk), :], far_rx.at[pl.ds(at * chunk, chunk), :]
+            )
+
 
         def middle_rows(here):
             back = part[here, :] + rx[here, :].astype(f32)
@@ -1509,24 +1520,23 @@
         for at in range(SPLIT):
             back_copies[at].wait()
             terms = by_rows(at * chunk, chunk, middle_rows, 4)
-            copies.append(send_rows(back_branch, at))
+            copies.append(far_rows(at))
             for spot_at, value in zip((6, 7, 5, 4), terms, strict=True):
                 note(layer, spot_at, value)
+        branch_copies = [send_rows(back_branch, at) for at in range(SPLIT)]
         load(layer, "unit_one", "inv_one")
+        if last:
+            load(0, "wf")
         loaded("wm")
 
-        def mixed_rows(start, count_rows):
-            for owner in range(2):
-                lanes = slice(owner * width, owner * width + width)
-                value = nt(back_branch[start : start + count_rows, :], wm[lanes, :]).astype(bf16)
-
-                @pl.when(owner == col)
-                def _():
-                    head_back[pl.ds(aligned(col * group + start, 16), count_rows), :] = value
-
-                @pl.when(owner != col)
-                def _():
-                    head_tx[start : start + count_rows, :] = value
+        def keep_back(owner, start, count_rows, value):
+            @pl.when(owner == col)
+            def _():
+                head_back[pl.ds(aligned(col * group + start, 16), count_rows), :] = value
+
+            @pl.when(owner != col)
+            def _():
+                head_tx[start : start + count_rows, :] = value
 
         core_copies = []
 
@@ -1539,8 +1549,12 @@
             )
             core_copies[-1].start()
 
-        mixed_rows(0, rows)
+        for owner in range(2):
+            lanes = slice(owner * width, owner * width + width)
+            keep_back(owner, 0, rows, nt(back_branch[:rows, :], wm[lanes, :]).astype(bf16))
         send_back(0, rows)
+        produce_own(layer, 2)
+        load(layer, "normed")
         if last:
             shrink(rows, rows, tx, 0)
             shrink(0, rows, aside, 0)
@@ -1548,7 +1562,10 @@
             load(1, "middle")
         for at in range(SPLIT):
             copies[at].wait()
-            mixed_rows(rows + at * chunk, chunk)
+            here = slice(at * chunk, at * chunk + chunk)
+            for owner in range(2):
+                lanes = slice(owner * width, owner * width + width)
+                keep_back(owner, rows + at * chunk, chunk, far_rx[here, lanes])
             send_back(rows + at * chunk, chunk)
         if last:
             last_copies = [
@@ -1618,6 +1635,10 @@
                     scatter.x_finish(1, 2)
             else:
                 scatter.x_finish(layer, 3)
+                for copy in branch_copies:
+                    copy.wait()
+                produce_other(layer, 1)
+                produce_own(layer, 1)
             there = pl.ds(aligned((1 - col) * group, 16), group)
             mine = pl.ds(aligned(col * group, 16), group)
             for part_at, source in enumerate((lanes, key_lanes, value_lanes)):
@@ -1656,9 +1677,7 @@
             one_rows(rows + at * chunk, chunk, tx, at * chunk)
             back_copies.append(send_part(at))
         if last:
-            produce_other(layer, 1)
             produce_other(layer, 0)
-            produce_own(layer, 1)
             produce_own(layer, 0)
             loaded("middle")
             last_rows(layer, 0, rows)
@@ -1667,8 +1686,6 @@
             )
         else:
             produce_own(layer, 0)
-            produce_other(layer, 1)
-            produce_own(layer, 1)
         one_rows(0, rows, part, 0)
         if last:
             load(0, "slope", "wu", "wq", "output", "normed_two", "active")
@@ -1701,11 +1718,11 @@
     scatter.z_finish(0, 3)
     scatter.z_finish(0, 2)
     to_features(place, grad, aside.at[:, pl.ds(0, half)], grad_out, c_send.at[26], c_recv.at[26])
+    scatter.x_finish(0, 1)
     scatter.x_finish(0, 0)
-    scatter.x_finish(0, 1)
     scatter_vectors(place, vec_grads, packed, spare, spot, vec_out, v_send, v_recv)
+    scatter.z_finish(0, 1)
     scatter.z_finish(0, 0)
-    scatter.z_finish(0, 1)
     scatter.finish()
 
 
@@ -1731,6 +1748,9 @@
         pltpu.VMEM((half, D), bf16),
         pltpu.VMEM((D, wide), bf16),
         pltpu.VMEM((wide, D), bf16),
+        pltpu.VMEM((half, D), bf16),
+        pltpu.VMEM((rows, half), bf16),
+        pltpu.VMEM((rows, half), bf16),
         pltpu.VMEM((group, wide), bf16),
         pltpu.VMEM((group, wide), bf16),
         pltpu.VMEM((group, D), bf16),
@@ -1765,8 +1785,8 @@
         pltpu.VMEM((line,) + spot_shape, f32),
         pltpu.VMEM((line + 2,) + spot_shape, f32),
         pltpu.VMEM(spot_shape, f32),
-        dma((LAYERS * 4 * SPLIT,)),
-        dma((LAYERS * 4 * SPLIT,)),
+        dma((24,)),
+        dma((24,)),
         dma((LAYERS * 13 + 2,)),
         dma((LAYERS * 13 + 2,)),
         dma((GROUPS, line)),
@@ -1778,12 +1798,12 @@
         dma((KINDS,)),
         dma((line + 2,)),
         dma((line + 2,)),
-        dma((20,)),
+        dma((21,)),
     ]
     return pl.pallas_call(
         functools.partial(backward_kernel, mesh_count),
         out_shape=outs,
-        in_specs=[WHOLE] * 2 + [ANY] * 20,
+        in_specs=[WHOLE] * 2 + [ANY] * 21,
         out_specs=[ANY] * 4 + [WHOLE] * 3,
         scratch_shapes=scratch,
         compiler_params=pltpu.CompilerParams(
@@ -1821,7 +1841,7 @@
     spot = jnp.where(
         jnp.arange(8 * piece) // piece == line_at, jnp.tile(vectors_master, (1, 8)), 0.0
     )
-    (w_a, w_b, w_c, w_d, _, vectors, *saved, grad_rows, middle) = forward_call(
+    (w_a, w_b, w_c, w_d, w_far, vectors, *saved, grad_rows, middle) = forward_call(
         count, images, cotangent, spot, masters
     )
     *grads, grad_out, vector_sums, block_out = backward_call(
@@ -1829,7 +1849,7 @@
         images.shape[0],
         grad_rows,
         vectors,
-        (w_a, w_b, w_c, w_d),
+        (w_a, w_b, w_c, w_d, w_far),
         (*saved, middle),
         spot.shape,
     )

time: 502 us -> 485 us (0.966)
  Pallas kernels: 475 us -> 458 us
    pallas_call x1, Pallas kernels: 269 us -> 252 us  [backward_call(): pl.pallas_call(functools.partial(backward_kernel, mesh_count), out_shape=...]
where the time goes in v6:
time: 485 us; the launch traced here: 475 us
  Pallas kernels  458 us (94%)
  other arithmetic  12.4 us (3%)
    pallas_call x1, Pallas kernels, backward_call(): pl.pallas_call(functools.partial(backward_kernel, mesh_count), out_shape=...  252 us
    pallas_call x1, Pallas kernels, forward_call(): pl.pallas_call(functools.partial(forward_kernel, mesh_count), out_shape=o...  206 us
    sub x5, other arithmetic, adam_step(): return (first_new, second_new, master - rate * (ratio + decay * master))  11.7 us

profile of v6, /device:TPU:0, one launch (start us, length us, event | category | flops | bytes accessed | tf_op | source)
XLA Modules:
  0.0 475.3 jit_solution(7460804085911457034)
XLA Ops:
  0.7 0.7 tile.4
  1.4 0.1 tile.10
  1.5 0.6 broadcast_select_fusion.refs_2_
  2.1 205.7 %forward.1 = (bf16[2,1024,1536]{2,1,0:T(8,128)(2,1)}, bf16[2,512,1024]{2,1,0:T(8,128)(2,1)}, bf16[2,1024,2048]{2,1,0:T(8,128)(2,1)}, bf16[2,2048,1024]{2,1,0:T(8...) custom-call(bf16[685,512]{1,0:T(8,128)(2,1)} %refs_0_.1, ...), custom_call_target="tpu_custom_call" | custom-call | tf_op jit(solution)/shard_map/forward/pallas_call | solution.py:964
  207.8 0.0 copy-start.11
  207.8 0.0 copy-start.12
  207.9 0.0 copy-start.13
  207.9 0.0 copy-start.2
  207.9 252.1 %backward.1 = (f32[2,3,64,512]{3,2,1,0:T(8,128)}, f32[2,64,512]{2,1,0:T(8,128)}, f32[2,64,2048]{2,1,0:T(8,128)}, f32[2,256,512]{2,1,0:T(8,128)}, f32[685,512]{1,...) custom-call(bf16[352,1024]{1,0:T(8,128)(2,1)} %get-tuple-element.47.refs_0_, ...), custom_call_target="tpu_custom_call" | custom-call | tf_op jit(solution)/shard_map/backward/pallas_call | solution.py:1803
  460.0 0.0 copy-done.11
  460.0 0.0 copy-done.12
  460.0 0.0 copy-done.13
  460.0 1.4 multiply_subtract_fusion.4
  461.4 2.2 multiply_subtract_fusion.3
  463.6 0.0 copy-start
  463.6 0.0 copy-start.4
  463.6 0.0 copy-start.5
  463.6 0.0 copy-start.9
  463.6 0.0 copy-done.2
  463.6 3.6 multiply_subtract_fusion.2
  467.3 0.0 copy-done
  467.3 0.0 copy-done.4
  467.3 0.0 copy-done.5
  467.3 0.0 copy-done.9
  467.3 0.0 copy-start.1
  467.3 0.0 copy-start.6
  467.3 0.0 copy-start.7
  467.3 0.0 copy-start.8
  467.4 2.2 multiply_subtract_fusion.1
  469.6 0.0 copy-done.1
  469.6 0.0 copy-done.6
  469.6 0.7 copy-done.7
  470.3 0.3 copy-done.8
  470.6 0.0 copy-start.10
  470.6 0.0 copy-start.3
  470.6 2.3 multiply_subtract_fusion
  472.9 0.0 copy-done.10
  472.9 0.9 copy.36
  473.7 0.0 copy-done.3
  473.7 1.1 copy.37
  (1 shorter events, 0.0 us)
Async XLA Ops:
  207.8 252.2 %copy-start.11 = (f32[2,448]{1,0:T(2,128)S(1)}, f32[2,448]{1,0:T(2,128)}, u32[]{:S(2)}) copy-start(f32[2,448]{1,0:T(2,128)} %param.31) | copy-start | bytes 10756
  207.8 252.2 %copy-start.12 = (f32[2,448]{1,0:T(2,128)S(1)}, f32[2,448]{1,0:T(2,128)}, u32[]{:S(2)}) copy-start(f32[2,448]{1,0:T(2,128)} %param.33) | copy-start | bytes 10756
  207.9 252.2 %copy-start.13 = (f32[2,448]{1,0:T(2,128)S(1)}, f32[2,448]{1,0:T(2,128)}, u32[]{:S(2)}) copy-start(f32[2,448]{1,0:T(2,128)} %param.32) | copy-start | bytes 10756
  207.9 255.8 %copy-start.2 = (f32[2,64,3,512]{3,1,2,0:T(8,128)S(1)}, f32[2,64,3,512]{3,1,2,0:T(8,128)}, u32[]{:S(2)}) copy-start(f32[2,64,3,512]{3,1,2,0:T(8,128)} %param.19) | copy-start | bytes 2359300
  463.6 3.7 copy-start
  463.6 3.7 copy-start.4
  463.6 3.7 copy-start.5
  463.6 3.7 copy-start.9
  467.3 2.3 copy-start.1
  467.3 2.3 copy-start.6
  467.3 3.0 copy-start.7
  467.3 3.3 copy-start.8
  470.6 2.3 copy-start.10
  470.6 3.1 copy-start.3

commit v7 on v6

--- a/solution.py
+++ b/solution.py
@@ -1106,30 +1106,47 @@
             copy.wait()
 
 
-def scatter_vectors(place, grads, packed, spare, spot, target, send, recv):
-    size = spot.shape[1]
-    for outer in range(place.line):
-        packed[outer] = grads[:, outer * size : (outer + 1) * size]
-    copies = []
-    for step in range(1, place.line):
-        outer = lax.rem(place.outer + step, place.line)
-        copy = remote(
-            packed.at[outer], spare.at[2 + step], send.at[2 + step], recv.at[2 + step], place.z_peer(step)
+class VectorSums:
+    def __init__(self, place, grads, packed, spare, spot, send, recv):
+        self.place, self.grads, self.packed = place, grads, packed
+        self.spare, self.spot, self.send, self.recv = spare, spot, send, recv
+        self.peers = (place.x_peer, place.y_peer, place.c_peer)
+
+    def line_copy(self, step):
+        place = self.place
+        return remote(
+            self.packed.at[lax.rem(place.outer + step, place.line)],
+            self.spare.at[2 + step],
+            self.send.at[2 + step],
+            self.recv.at[2 + step],
+            place.z_peer(step),
         )
-        copy.start()
-        copies.append(copy)
-    for copy in copies:
-        copy.wait()
-    value = packed[place.outer]
-    for step in range(1, place.line):
-        value = value + spare[2 + step]
-    spot[...] = value
-    for at, peer in enumerate((place.x_peer, place.y_peer, place.c_peer)):
-        copy = remote(spot, spare.at[at], send.at[at], recv.at[at], peer)
-        copy.start()
-        copy.wait()
-        spot[...] = spot[...] + spare[at]
-    target[...] = spot[...]
+
+    def line_start(self):
+        size = self.spot.shape[1]
+        for outer in range(self.place.line):
+            self.packed[outer] = self.grads[:, outer * size : (outer + 1) * size]
+        for step in range(1, self.place.line):
+            self.line_copy(step).start()
+
+    def line_finish(self):
+        value = self.packed[self.place.outer]
+        for step in range(1, self.place.line):
+            self.line_copy(step).wait()
+            value = value + self.spare[2 + step]
+        self.spot[...] = value
+
+    def copy(self, at):
+        return remote(
+            self.spot, self.spare.at[at], self.send.at[at], self.recv.at[at], self.peers[at]
+        )
+
+    def start(self, at):
+        self.copy(at).start()
+
+    def finish(self, at):
+        self.copy(at).wait()
+        self.spot[...] = self.spot[...] + self.spare[at]
 
 
 def backward_kernel(count, *refs):
@@ -1481,7 +1498,6 @@
         else:
             inner_rows(0, rows)
             loaded("wu")
-            scatter.x_finish(1, 1)
             back_copies = []
             for at in range(SPLIT):
                 out_copies[at].wait()
@@ -1623,6 +1639,8 @@
                 return carry
 
             lax.fori_loop(0, 2 * group // 128, step, 0)
+            if pair == pairs - 1:
+                scatter.x_finish(layer, 2)
             for owner in range(2):
                 edge = owner * rows
                 valid = lax.broadcasted_iota(jnp.int32, (rows, 1), 0) < tokens - edge
@@ -1630,10 +1648,7 @@
                     here = slice(owner * group + part_at * rows, owner * group + part_at * rows + rows)
                     head_grad[here, key_lanes] = jnp.where(valid, key_sum[here, :], 0.0).astype(bf16)
                     head_grad[here, value_lanes] = jnp.where(valid, value_sum[here, :], 0.0).astype(bf16)
-            if pair == pairs - 1:
-                if last:
-                    scatter.x_finish(1, 2)
-            else:
+            if pair < pairs - 1:
                 scatter.x_finish(layer, 3)
                 for copy in branch_copies:
                     copy.wait()
@@ -1652,8 +1667,7 @@
                         aligned((3 * D if part_at else 2 * D) + row * half + col * width + pair * 128), 128
                     )
                     vec_grads[layer : layer + 1, bias_at] = total(head_grad[:, source].astype(f32))
-        if not last:
-            scatter.x_finish(0, 2)
+        scatter.x_finish(layer, 1)
         for copy in head_copies:
             copy.wait()
         loaded("wq", "normed")
@@ -1686,6 +1700,7 @@
             )
         else:
             produce_own(layer, 0)
+            scatter.z_finish(0, 3)
         one_rows(0, rows, part, 0)
         if last:
             load(0, "slope", "wu", "wq", "output", "normed_two", "active")
@@ -1715,12 +1730,16 @@
                 note(layer, spot_at, value)
         if last:
             load(0, "unit_two", "inv_two")
-    scatter.z_finish(0, 3)
+    vector_sums = VectorSums(place, vec_grads, packed, spare, spot, v_send, v_recv)
     scatter.z_finish(0, 2)
+    vector_sums.line_start()
     to_features(place, grad, aside.at[:, pl.ds(0, half)], grad_out, c_send.at[26], c_recv.at[26])
-    scatter.x_finish(0, 1)
+    vector_sums.line_finish()
     scatter.x_finish(0, 0)
-    scatter_vectors(place, vec_grads, packed, spare, spot, vec_out, v_send, v_recv)
+    for at in range(3):
+        vector_sums.start(at)
+        vector_sums.finish(at)
+    vec_out[...] = spot[...]
     scatter.z_finish(0, 1)
     scatter.z_finish(0, 0)
     scatter.finish()

time: 485 us -> 478 us (0.986)
  the two profiles are of different devices: /device:TPU:0 before, /device:TPU:8 now
where the time goes in v7:
time: 478 us; the launch traced here: 469 us
  Pallas kernels  451 us (94%)
  other arithmetic  12.4 us (3%)
    pallas_call x1, Pallas kernels, backward_call(): pl.pallas_call(functools.partial(backward_kernel, mesh_count), out_shape=...  238 us
    pallas_call x1, Pallas kernels, forward_call(): pl.pallas_call(functools.partial(forward_kernel, mesh_count), out_shape=o...  213 us
    sub x5, other arithmetic, adam_step(): return (first_new, second_new, master - rate * (ratio + decay * master))  11.7 us

profile of v7, /device:TPU:8, one launch (start us, length us, event | category | flops | bytes accessed | tf_op | source)
XLA Modules:
  0.0 468.7 jit_solution(9831159520279701939)
XLA Ops:
  0.7 0.7 tile.4
  1.4 0.1 tile.10
  1.5 0.6 broadcast_select_fusion.refs_2_
  2.1 213.4 %forward.1 = (bf16[2,1024,1536]{2,1,0:T(8,128)(2,1)}, bf16[2,512,1024]{2,1,0:T(8,128)(2,1)}, bf16[2,1024,2048]{2,1,0:T(8,128)(2,1)}, bf16[2,2048,1024]{2,1,0:T(8...) custom-call(bf16[685,512]{1,0:T(8,128)(2,1)} %refs_0_.1, ...), custom_call_target="tpu_custom_call" | custom-call | tf_op jit(solution)/shard_map/forward/pallas_call | solution.py:964
  215.5 0.0 copy-start.11
  215.5 0.0 copy-start.12
  215.5 0.0 copy-start.13
  215.6 0.0 copy-start.2
  215.6 237.9 %backward.1 = (f32[2,3,64,512]{3,2,1,0:T(8,128)}, f32[2,64,512]{2,1,0:T(8,128)}, f32[2,64,2048]{2,1,0:T(8,128)}, f32[2,256,512]{2,1,0:T(8,128)}, f32[685,512]{1,...) custom-call(bf16[352,1024]{1,0:T(8,128)(2,1)} %get-tuple-element.47.refs_0_, ...), custom_call_target="tpu_custom_call" | custom-call | tf_op jit(solution)/shard_map/backward/pallas_call | solution.py:1822
  453.4 0.0 copy-done.11
  453.4 0.0 copy-done.12
  453.5 0.0 copy-done.13
  453.5 1.4 multiply_subtract_fusion.4
  454.9 2.2 multiply_subtract_fusion.3
  457.0 0.0 copy-start
  457.0 0.0 copy-start.4
  457.1 0.0 copy-start.5
  457.1 0.0 copy-start.9
  457.1 0.0 copy-done.2
  457.1 3.6 multiply_subtract_fusion.2
  460.7 0.0 copy-done
  460.7 0.0 copy-done.4
  460.7 0.0 copy-done.5
  460.7 0.0 copy-done.9
  460.7 0.0 copy-start.1
  460.8 0.0 copy-start.6
  460.8 0.0 copy-start.7
  460.8 0.0 copy-start.8
  460.8 2.2 multiply_subtract_fusion.1
  463.0 0.0 copy-done.1
  463.0 0.0 copy-done.6
  463.0 0.7 copy-done.7
  463.7 0.3 copy-done.8
  464.1 0.0 copy-start.10
  464.1 0.0 copy-start.3
  464.1 2.3 multiply_subtract_fusion
  466.3 0.0 copy-done.10
  466.3 0.9 copy.36
  467.2 0.0 copy-done.3
  467.2 1.1 copy.37
  (1 shorter events, 0.0 us)
Async XLA Ops:
  215.5 237.9 %copy-start.11 = (f32[2,448]{1,0:T(2,128)S(1)}, f32[2,448]{1,0:T(2,128)}, u32[]{:S(2)}) copy-start(f32[2,448]{1,0:T(2,128)} %param.31) | copy-start | bytes 10756
  215.5 237.9 %copy-start.12 = (f32[2,448]{1,0:T(2,128)S(1)}, f32[2,448]{1,0:T(2,128)}, u32[]{:S(2)}) copy-start(f32[2,448]{1,0:T(2,128)} %param.33) | copy-start | bytes 10756
  215.5 237.9 %copy-start.13 = (f32[2,448]{1,0:T(2,128)S(1)}, f32[2,448]{1,0:T(2,128)}, u32[]{:S(2)}) copy-start(f32[2,448]{1,0:T(2,128)} %param.32) | copy-start | bytes 10756
  215.6 241.5 %copy-start.2 = (f32[2,64,3,512]{3,1,2,0:T(8,128)S(1)}, f32[2,64,3,512]{3,1,2,0:T(8,128)}, u32[]{:S(2)}) copy-start(f32[2,64,3,512]{3,1,2,0:T(8,128)} %param.19) | copy-start | bytes 2359300
  457.0 3.7 copy-start
  457.0 3.7 copy-start.4
  457.1 3.7 copy-start.5
  457.1 3.7 copy-start.9
  460.7 2.3 copy-start.1
  460.8 2.3 copy-start.6
  460.8 3.0 copy-start.7
  460.8 3.3 copy-start.8
  464.1 2.3 copy-start.10
  464.1 3.1 copy-start.3
